TPU v7x, 32 devices: a whole 2x2x4 slice. The times are simulated.
32 devices in a mesh: group: 4 (over z), tensor: 8 (over y, x, core).
Axes of the slice: x: 2, y: 2, z: 4, core: 2. Of those that a mesh axis runs over, the one named last changes fastest.
Arguments:
- residual_in: bfloat16 [1024, 2048], P(('group', 'tensor')), parts along dimension 0, may hold values from -22 to 22
- attn_gain: float32 [2048], replicated, may hold values from 0.5 to 1.5
- w_query: bfloat16 [2048, 4096], P(None, 'tensor'), may hold values from -0.125 to 0.125
- w_keyval: bfloat16 [1024, 2048], P('tensor'), may hold values from -0.125 to 0.125
- query_gain: float32 [128], replicated, may hold values from 0.1 to 1.9
- key_gain: float32 [128], replicated, may hold values from 0.1 to 1.9
- w_out: bfloat16 [4096, 2048], P('tensor'), may hold values from -0.09375 to 0.09375
- ffn_gain: float32 [2048], replicated, may hold values from 0.5 to 1.5
- w_gate: bfloat16 [8, 768, 2048], P('tensor'), may hold values from -0.125 to 0.125
- w_up: bfloat16 [8, 768, 2048], P('tensor'), may hold values from -0.125 to 0.125
- w_down: bfloat16 [8, 768, 2048], P('tensor'), may hold values from -0.21875 to 0.21875
- key_cache: bfloat16 [32, 1024, 512], P(('group', 'tensor')), parts along dimension 0, may hold values from -110 to 110
- value_cache: bfloat16 [32, 1024, 512], P(('group', 'tensor')), parts along dimension 0, may hold values from -18 to 18
- prefix_lens: int32 [32], P(('group', 'tensor')), parts along dimension 0, may hold values from 1 to 992
- accepted: int32 [32], P(('group', 'tensor')), parts along dimension 0, may hold values from 1 to 8
- accept_path: int32 [32, 8], P(('group', 'tensor')), parts along dimension 0, may hold values from 0 to 14, as said below
- parents: int32 [32, 32], P(('group', 'tensor')), parts along dimension 0, may hold values from -1 to 30, as said below
- slot_kinds: int32 [32], P(('group', 'tensor')), parts along dimension 0, may hold values from 0 to 1
- expert_ids: int32 [1024, 8], P('group'), parts along dimension 0, may hold values from 0 to 127, as said below
- gate_probs: float32 [1024, 8], P('group'), parts along dimension 0, may hold values from 0.1 to 1
Outputs:
- mixed: bfloat16 [1024, 2048], P(('group', 'tensor')), parts along dimension 0
There are 4 independent parts, one for each index of `group`. A program takes and returns all parts, laid end to end along the dimension named above; an argument that names none is the same for every part. Nothing has to cross between parts.
Inputs may be any that keep to these rules, and one draw needn't show every extreme that they name: `expert_ids`: the tokens of each slot name each of the 128 experts exactly 32 * 8 // 128 times; a token never names one expert twice. `accept_path`: each row starts at 0 and rises by 1 or 2 from one entry to the next. `parents`: node 0 of every slot has parent -1; every other node's parent is an earlier node of the same slot.
All inputs are finite; a program needn't handle non-finite values.
Results may differ from a plain program's by a relative error of at most 0.02.
Values may be sent and summed in bfloat16 or wider, within the bound.
No kernel may reach another device: no remote copies, remote signals or barrier semaphores. Data moves between devices by JAX's collectives and lax.ppermute only.
A program may use at most 128 MiB of HBM per device.

v0:
```python
import functools
import math

import jax
import jax.numpy as jnp
import numpy as np
from jax import lax
from jax.experimental import pallas as pl
from jax.experimental.pallas import tpu as pltpu
from jax.sharding import PartitionSpec as P

EXPERTS = 128
SINK = 4
WIN = 512

EPSILON = 1e-06
NEG_FILL = -1e30
ROPE_BASE = 1000000.0
LOG2E = math.log2(math.e)
F32 = jnp.float32
BF16 = jnp.bfloat16
MIB = 1 << 20


def iota(shape, dim):
    return lax.broadcasted_iota(jnp.int32, shape, dim)


def dot(left, right):
    return jnp.dot(left, right, preferred_element_type=F32)


def dot_last(left, right):
    return lax.dot_general(left, right, (((1,), (1,)), ((), ())), preferred_element_type=F32)


def dot_first(left, right):
    return lax.dot_general(left, right, (((0,), (0,)), ((), ())), preferred_element_type=F32)


def norm_rows(values):
    return values * lax.rsqrt(jnp.mean(values * values, axis=-1, keepdims=True) + EPSILON)


def in_vmem(shape, dtype):
    return pltpu.VMEM(shape, dtype)


def call(kernel, name, outs, args, scratch=(), limit=16, flops=0, moved=0, same=None):
    arrays = []
    specs = []
    for array, space in args:
        if space is pltpu.HBM or space is pltpu.VMEM:
            array = pltpu.with_memory_space_constraint(array, space)
        arrays.append(array)
        specs.append(pl.BlockSpec(memory_space=space))
    return pl.pallas_call(
        kernel,
        out_shape=outs,
        in_specs=specs,
        out_specs=[pl.BlockSpec(memory_space=pltpu.VMEM) for _ in outs],
        scratch_shapes=list(scratch),
        input_output_aliases=same or {},
        compiler_params=pltpu.CompilerParams(vmem_limit_bytes=limit * MIB),
        cost_estimate=pl.CostEstimate(flops=flops, bytes_accessed=moved, transcendentals=0),
        name=name,
    )(*arrays)


def hop(value, step):
    devices = lax.axis_size("tensor")
    return lax.ppermute(value, "tensor", [(i, i ^ step) for i in range(devices)])


def exchange(blocks):
    return [blocks[0]] + [hop(blocks[j], 2 * j) for j in range(1, len(blocks))]


def window_rows(path_len):
    return -(-(WIN + 2 * (path_len - 1) + 16) // 16) * 16


def prep_kernel(path_len, per, n_weights, *refs):
    key_cache, value_cache, prefix_ref, accepted_ref, kind_ref = refs[:5]
    small_in = refs[5:12]
    sources = refs[12 : 12 + n_weights]
    refs = refs[12 + n_weights :]
    keys_ref, values_ref, mask_ref, rot_ref, pick_ref, combine_ref, weight_ref = refs[:7]
    targets = refs[7 : 7 + n_weights]
    refs = refs[7 + n_weights :]
    path_ref, parents_ref, ids_ref, gates_ref, freq_ref, q_gain_ref, k_gain_ref = refs[:7]
    hit_ref, rank_ref, own_ref, small_sems, cache_sems, weight_sems = refs[7:]

    me = lax.axis_index("tensor")
    new = mask_ref.shape[0]
    kv_heads, span, head = keys_ref.shape
    cache_len = key_cache.shape[1]
    wide = window_rows(path_len)
    sink_at, win_at = new, new + 16
    end = win_at + wide

    small = [
        pltpu.make_async_copy(source, target, small_sems.at[which])
        for which, (source, target) in enumerate(zip(small_in, refs[:7]))
    ]
    for copy in small:
        copy.start()
    prefix = prefix_ref[0]
    accepted = accepted_ref[0]
    total = prefix + accepted
    low = jnp.maximum(total - WIN, 0)
    start = pl.multiple_of(jnp.minimum((low // 16) * 16, cache_len - wide), 16)
    copies = []
    for which, (cache, buf) in enumerate(((key_cache, keys_ref), (value_cache, values_ref))):
        for kv in range(kv_heads):
            cols = pl.ds(kv * head, head)
            copies.append(
                pltpu.make_async_copy(
                    cache.at[0, pl.ds(start, wide), cols],
                    buf.at[kv, pl.ds(win_at, wide)],
                    cache_sems.at[which, kv, 0],
                )
            )
            copies.append(
                pltpu.make_async_copy(
                    cache.at[0, pl.ds(0, 16), cols],
                    buf.at[kv, pl.ds(sink_at, 16)],
                    cache_sems.at[which, kv, 1],
                )
            )
    for which, (source, target) in enumerate(zip(sources, targets)):
        copies.append(pltpu.make_async_copy(source, target, weight_sems.at[which]))
    for copy in copies:
        copy.start()

    for buf in (keys_ref, values_ref):
        buf[:, 0:new, :] = jnp.zeros((kv_heads, new, head), BF16)
        buf[:, end:span, :] = jnp.zeros((kv_heads, span - end, head), BF16)

    for copy in small:
        copy.wait()
    column = iota((1, span), 1)
    row = jnp.where(column < win_at, column - sink_at, start + column - win_at)
    taken = jnp.zeros((1, span), jnp.bool_)
    for step in range(path_len):
        at = prefix + path_ref[0, step]
        taken = taken | ((row == at) & (step < accepted))
    old = (row < prefix) & ((row < SINK) | (row >= total - WIN))
    in_window = (column >= win_at) & (column < end) & (old | taken)
    in_sink = (column >= sink_at) & (column < win_at) & (row < SINK) & (row < prefix) & (start > 0)
    seen = jnp.where(in_window | in_sink, 0.0, NEG_FILL)
    mask_ref[...] = jnp.broadcast_to(seen, mask_ref.shape)

    down, across = iota((new, new), 0), iota((new, new), 1)
    eye = (down == across).astype(F32)
    back = eye + (down == parents_ref[...]).astype(F32)
    for _ in range((new - 1).bit_length()):
        half = back.astype(BF16)
        back = jnp.minimum(dot(half, half), 1.0)
    reach = dot_first(back.astype(BF16), eye.astype(BF16))
    tree = (kind_ref[0] == 1).astype(F32)
    causal = (across <= down).astype(F32)
    allowed = tree * reach + (1.0 - tree) * causal
    mask_ref[:, 0:new] = jnp.where(allowed > 0.5, 0.0, NEG_FILL)
    depth = tree * (jnp.sum(reach, axis=1, keepdims=True) - 1.0)
    depth = depth + (1.0 - tree) * iota((new, 1), 0).astype(F32)
    angle = (total.astype(F32) + depth) * freq_ref[...]
    lane = iota(angle.shape, 1)
    cosine, sine = jnp.cos(angle), jnp.sin(angle)
    sine = jnp.where(lane < head // 2, -sine, sine)
    for which, gain_ref in enumerate((q_gain_ref, k_gain_ref)):
        gain = jnp.broadcast_to(gain_ref[...], angle.shape)
        rot_ref[2 * which] = cosine * gain
        rot_ref[2 * which + 1] = sine * pltpu.roll(gain, head // 2, 1)

    all_tokens = ids_ref.shape[1]
    devices = hit_ref.shape[0]
    chips = devices // 2
    tokens = chips * new
    slot = iota((all_tokens, tokens), 1) // new
    source = (me ^ (2 * slot)) * new + iota((all_tokens, tokens), 1) % new
    order = (iota((all_tokens, tokens), 0) == source).astype(F32)
    ids = dot(ids_ref[...].astype(F32).astype(BF16), order.astype(BF16))
    gates = lax.dot_general(
        gates_ref[...],
        order,
        (((1,), (0,)), ((), ())),
        precision=lax.Precision.HIGHEST,
        preferred_element_type=F32,
    )
    for rel in range(devices):
        named = (ids == (me ^ rel).astype(F32)).astype(F32)
        hit_ref[rel : rel + 1, :] = jnp.max(named, axis=0, keepdims=True)
    before, later = iota((tokens, tokens), 0), iota((tokens, tokens), 1)
    earlier = (before < later) & (before // new == later // new)
    rank_ref[...] = dot(hit_ref[...].astype(BF16), earlier.astype(F32).astype(BF16))
    rows = chips * per
    slot_of = iota((rows, tokens), 1) // new
    row_slot = iota((rows, tokens), 0) // per
    row_rank = (iota((rows, tokens), 0) % per).astype(F32)
    in_first = iota((1, tokens), 1) < new
    for rel in range(devices):
        hit = hit_ref[rel : rel + 1, :] > 0.5
        rank = rank_ref[rel : rel + 1, :]
        chosen = (slot_of == (row_slot ^ (rel // 2))) & hit & (rank == row_rank)
        pick_ref[rel * rows : (rel + 1) * rows, :] = chosen.astype(F32)
        if rel < 2:
            named = ids == (me ^ rel).astype(F32)
            weight = jnp.sum(jnp.where(named, gates, 0.0), axis=0, keepdims=True)
            weight = jnp.sum(jnp.where(chosen, weight, 0.0), axis=1, keepdims=True)
            weight_ref[rel * rows : (rel + 1) * rows, :] = jnp.broadcast_to(
                weight, (rows, weight_ref.shape[1])
            )
        for place in range(per):
            at = rel * per + place
            own_ref[at : at + 1, :] = (in_first & hit & (rank == float(place))).astype(F32)
    first = (iota((tokens, new), 0) == iota((tokens, new), 1)).astype(F32)
    combine_ref[...] = lax.dot_general(
        first.astype(BF16),
        own_ref[...].astype(BF16),
        (((0,), (1,)), ((), ())),
        preferred_element_type=F32,
    )
    for copy in copies:
        copy.wait()


def project_kernel(chips, *refs):
    blocks = refs[:chips]
    gain_ref, wq_ref, wkv_ref, wq_sib, wkv_sib, _ = refs[chips : chips + 6]
    outs = refs[chips + 6 : 2 * chips + 6]
    normed = refs[-1]
    rows = blocks[0].shape[0]
    gain = gain_ref[...]
    for j in range(chips):
        values = norm_rows(blocks[j][...].astype(F32)) * gain
        normed[j * rows : (j + 1) * rows, :] = values.astype(BF16)
    values = normed[...]

    def put(result, at):
        result = result.astype(BF16)
        for j in range(chips):
            outs[j][:, at : at + result.shape[1]] = result[j * rows : (j + 1) * rows]

    wide, narrow = wq_ref.shape[1], wkv_ref.shape[0]
    put(dot(values, wq_ref[...]), 0)
    put(dot(values, wq_sib[...]), wide)
    put(dot_last(values, wkv_ref[...]), 2 * wide)
    put(dot_last(values, wkv_sib[...]), 2 * wide + narrow)


def attend_kernel(chips, q_width, kv_ready, *refs):
    got = refs[:chips]
    at = chips + 1 if kv_ready else chips
    keys_ref, values_ref, mask_ref, rot_ref = refs[at : at + 4]
    outs = refs[at + 6 : at + 6 + chips]
    fresh_ref = refs[chips] if kv_ready else refs[-1]
    me = lax.axis_index("tensor")
    chip = me // 2
    new = got[0].shape[0]
    kv_heads, span, head = keys_ref.shape
    per_chip = 2 * q_width // head
    group = chips * per_chip // kv_heads

    if not kv_ready:
        for rel in range(2 * chips):
            left = 2 * q_width + (rel % 2) * head
            fresh_ref[rel] = got[rel // 2][:, left : left + head]

    def rope(values, which):
        values = norm_rows(values.astype(F32))
        turned = pltpu.roll(values, head // 2, 1)
        return (values * rot_ref[2 * which] + turned * rot_ref[2 * which + 1]).astype(BF16)

    scale = head ** (-0.5) * LOG2E
    for j in range(chips):
        kv = (chip ^ j) * per_chip // group
        key_at, value_at = kv, kv + kv_heads
        if not kv_ready:
            key_at, value_at = me ^ key_at, me ^ value_at
        keys = jnp.concatenate([rope(fresh_ref[key_at], 1), keys_ref[kv, new:span]], axis=0)
        values = jnp.concatenate([fresh_ref[value_at], values_ref[kv, new:span]], axis=0)
        query = jnp.concatenate(
            [rope(got[j][:, h * head : (h + 1) * head], 0) for h in range(per_chip)], axis=0
        )
        score = dot_last(query, keys) * scale
        score = score.reshape(per_chip, new, span) + mask_ref[...][None]
        expo = jnp.exp2(score - jnp.max(score, axis=-1, keepdims=True))
        denom = jnp.sum(expo, axis=-1, keepdims=True).reshape(per_chip * new, 1)
        expo = expo.astype(BF16).reshape(per_chip * new, span)
        result = (dot(expo, values) / denom).astype(BF16)
        for h in range(per_chip):
            outs[j][:, h * head : (h + 1) * head] = result[h * new : (h + 1) * new]


def spread_kernel(chips, *refs):
    got = refs[:chips]
    pick_ref, w_ref, w_sib = refs[chips : chips + 3]
    outs = refs[chips + 6 : 2 * chips + 6]
    rows_ref = refs[-1]
    new = got[0].shape[0]
    depth, width = w_ref.shape
    each = rows_ref.shape[1]
    heads = jnp.concatenate([got[j][...] for j in range(chips)], axis=0)
    picked = dot(pick_ref[...].astype(BF16), heads).astype(BF16)
    extra = each - new
    for j in range(chips):
        rows_ref[j, 0:new, :] = got[j][...]
        rows_ref[j, new:each, :] = picked[j * extra : (j + 1) * extra]
    left = rows_ref[...].reshape(chips * each, 2 * depth)
    tile = min(512, width)
    for at in range(0, width, tile):
        part = dot(left[:, :depth], w_ref[:, at : at + tile])
        part = (part + dot(left[:, depth:], w_sib[:, at : at + tile])).astype(BF16)
        for j in range(chips):
            outs[j][:, at : at + tile] = part[j * each : (j + 1) * each]


def fetch_kernel(_, up_in, down_in, up_out, down_out, sems):
    copies = [
        pltpu.make_async_copy(up_in, up_out, sems.at[0]),
        pltpu.make_async_copy(down_in, down_out, sems.at[1]),
    ]
    for copy in copies:
        copy.start()
    for copy in copies:
        copy.wait()


def select_kernel(chips, *refs):
    blocks = refs[:chips]
    pick_ref, _ = refs[chips : chips + 2]
    sources = refs[chips + 2 : chips + 3]
    picked_ref = refs[chips + 3]
    targets = refs[chips + 4 : chips + 5]
    sems = refs[-1]
    copies = [
        pltpu.make_async_copy(source, target, sems.at[which])
        for which, (source, target) in enumerate(zip(sources, targets))
    ]
    for copy in copies:
        copy.start()
    values = jnp.concatenate([block[...] for block in blocks], axis=0)
    pick = pick_ref[0 : picked_ref.shape[0], :].astype(BF16)
    picked_ref[...] = dot(pick, values)
    for copy in copies:
        copy.wait()


def hidden_kernel(chips, *refs):
    got = refs[:chips]
    own_ref, out_ref = refs[chips:]
    new = own_ref.shape[0]
    total = own_ref[...].astype(F32)
    for j in range(chips):
        total = total + got[j][0:new, :].astype(F32)
    out_ref[...] = total


def expert_kernel(chips, per, *refs):
    got = refs[:chips]
    picked_ref, weight_ref, gain_ref = refs[chips : chips + 3]
    weights = refs[chips + 3 : chips + 9]
    outs = refs[chips + 9 :]
    rows = chips * per
    hidden = picked_ref[...]
    new = got[0].shape[0] - 2 * rows
    for j in range(chips):
        hidden = hidden + got[j][new:, :].astype(F32)
    normed = norm_rows(hidden) * gain_ref[...]
    for core in range(2):
        gate_ref, up_ref, down_ref = weights[3 * core : 3 * core + 3]
        right = normed[core * rows : (core + 1) * rows].astype(BF16)
        gate = dot_last(gate_ref[0], right)
        up = dot_last(up_ref[0], right)
        inner = (gate / (1.0 + jnp.exp(-gate)) * up).astype(BF16)
        result = dot_first(inner, down_ref[0])
        result = (result * weight_ref[core * rows : (core + 1) * rows, 0:1]).astype(BF16)
        for j in range(chips):
            outs[j][core * per : (core + 1) * per, :] = result[j * per : (j + 1) * per]


def combine_kernel(chips, *refs):
    hidden_ref, combine_ref = refs[:2]
    got = refs[2 : 2 + chips]
    out_ref = refs[2 + chips]
    rows = jnp.concatenate([block[...].astype(F32) for block in got], axis=0)
    moe = dot(combine_ref[...].astype(BF16), rows.astype(BF16))
    out_ref[...] = (hidden_ref[...] + moe).astype(BF16)


def body(
    residual_in,
    attn_gain,
    w_query,
    w_keyval,
    query_gain,
    key_gain,
    w_out,
    ffn_gain,
    w_gate,
    w_up,
    w_down,
    key_cache,
    value_cache,
    prefix_lens,
    accepted,
    accept_path,
    parents,
    slot_kinds,
    expert_ids,
    gate_probs,
):
    devices = lax.axis_size("tensor")
    chips = devices // 2
    new, width = residual_in.shape
    head = query_gain.shape[0]
    kv_heads = key_cache.shape[2] // head
    q_width = w_query.shape[1]
    new_width = w_keyval.shape[0]
    all_tokens, top = expert_ids.shape
    tokens = chips * new
    per = new * top // EXPERTS
    path_len = accept_path.shape[1]
    rows = 2 * chips * per
    assert key_cache.shape[0] == 1 and w_gate.shape[0] == 1
    assert devices & (devices - 1) == 0
    vmem, smem, hbm, anywhere = pltpu.VMEM, pltpu.SMEM, pltpu.HBM, pl.ANY

    blocks = exchange([residual_in] * chips)
    wq_sib = hop(w_query, 1)
    wkv_sib = hop(w_keyval, 1)

    freq = ROPE_BASE ** (-2.0 * np.arange(head // 2) / head)
    freq = jnp.asarray(np.concatenate([freq, freq])[None, :], F32)
    span = -(-(new + 16 + window_rows(path_len)) // 128) * 128
    weights = [attn_gain[None, :], ffn_gain[None, :], w_query, w_keyval, w_out]
    prepared = call(
        functools.partial(prep_kernel, path_len, per, len(weights)),
        "prep",
        [
            in_vmem((kv_heads, span, head), BF16),
            in_vmem((kv_heads, span, head), BF16),
            in_vmem((new, span), F32),
            in_vmem((4, new, head), F32),
            in_vmem((chips * rows, tokens), F32),
            in_vmem((new, devices * per), F32),
            in_vmem((rows, 128), F32),
        ]
        + [in_vmem(weight.shape, weight.dtype) for weight in weights],
        [
            (key_cache, hbm),
            (value_cache, hbm),
            (prefix_lens, smem),
            (accepted, smem),
            (slot_kinds, smem),
            (accept_path, hbm),
            (parents, hbm),
            (expert_ids.T, hbm),
            (gate_probs.T, hbm),
            (freq, hbm),
            (query_gain[None, :], hbm),
            (key_gain[None, :], hbm),
        ]
        + [(weight, hbm) for weight in weights],
        [
            pltpu.SMEM((1, path_len), jnp.int32),
            pltpu.VMEM((1, new), jnp.int32),
            pltpu.VMEM((top, all_tokens), jnp.int32),
            pltpu.VMEM((top, all_tokens), F32),
            pltpu.VMEM((1, head), F32),
            pltpu.VMEM((1, head), F32),
            pltpu.VMEM((1, head), F32),
            pltpu.VMEM((devices, tokens), F32),
            pltpu.VMEM((devices, tokens), F32),
            pltpu.VMEM((devices * per, tokens), F32),
            pltpu.SemaphoreType.DMA((7,)),
            pltpu.SemaphoreType.DMA((2, kv_heads, 2)),
            pltpu.SemaphoreType.DMA((len(weights),)),
        ],
        limit=16,
        moved=4 * span * kv_heads * head * 2,
    )
    keys, values, mask, rot, pick, combine, weight, gain, ffn, wq, wkv, wo = prepared

    *projected, wo = call(
        functools.partial(project_kernel, chips),
        "project",
        [in_vmem((new, 2 * (q_width + new_width)), BF16)] * chips
        + [in_vmem(wo.shape, wo.dtype)],
        [(block, vmem) for block in blocks]
        + [
            (gain, vmem),
            (wq, vmem),
            (wkv, vmem),
            (wq_sib, vmem),
            (wkv_sib, vmem),
            (wo, vmem),
        ],
        [pltpu.VMEM((tokens, width), BF16)],
        limit=16,
        same={chips + 5: chips},
        flops=4 * tokens * width * (q_width + new_width),
        moved=4 * width * (q_width + new_width),
    )
    wo_sib = hop(wo, 1)

    got = exchange(projected)
    picked, wg = call(
        functools.partial(select_kernel, chips),
        "select",
        [in_vmem((rows, width), F32)] + [in_vmem(w.shape, w.dtype) for w in (w_gate,)],
        [(block, vmem) for block in blocks]
        + [(pick, vmem), (projected[0], anywhere), (w_gate, hbm)],
        [pltpu.SemaphoreType.DMA((2,))],
        limit=8,
        flops=2 * rows * width * tokens,
        moved=8 * width * w_gate.shape[1],
    )
    kv_ready = []
    if new_width != head:
        pieces = [
            got[rel // 2][:, 2 * q_width + (rel % 2) * new_width :][:, :new_width]
            for rel in range(devices)
        ]
        pieces = jnp.stack(pieces)[lax.axis_index("tensor") ^ jnp.arange(devices)]
        pieces = pieces.transpose(1, 0, 2).reshape(new, 2 * kv_heads, head)
        kv_ready = [(pieces.transpose(1, 0, 2), vmem)]
    at = chips + len(kv_ready) + 5
    *attended, wg = call(
        functools.partial(attend_kernel, chips, q_width, bool(kv_ready)),
        "attend",
        [in_vmem((new, 2 * q_width), BF16)] * chips
        + [in_vmem(w.shape, w.dtype) for w in (wg,)],
        [(block, vmem) for block in got]
        + kv_ready
        + [(keys, vmem), (values, vmem), (mask, vmem), (rot, vmem)]
        + [(wo_sib, anywhere), (wg, vmem)],
        [] if kv_ready else [pltpu.VMEM((devices, new, head), BF16)],
        limit=16,
        same={at: chips},
        flops=8 * new * chips * q_width * span,
        moved=4 * span * kv_heads * head,
    )
    wg_sib = hop(wg, 1)
    heads = exchange(attended)
    wu, wd = call(
        fetch_kernel,
        "fetch",
        [in_vmem(w.shape, w.dtype) for w in (w_up, w_down)],
        [(attended[0], anywhere), (w_up, hbm), (w_down, hbm)],
        [pltpu.SemaphoreType.DMA((2,))],
        limit=8,
        moved=8 * width * w_gate.shape[1],
    )

    *partial, wu, wd = call(
        functools.partial(spread_kernel, chips),
        "spread",
        [in_vmem((new + rows, width), BF16)] * chips
        + [in_vmem(w.shape, w.dtype) for w in (wu, wd)],
        [(block, vmem) for block in heads]
        + [(pick, vmem), (wo, vmem), (wo_sib, vmem), (wg_sib, anywhere), (wu, vmem), (wd, vmem)],
        [pltpu.VMEM((chips, new + rows, 2 * q_width), BF16)],
        same={chips + 4: chips, chips + 5: chips + 1},
        limit=16,
        flops=4 * chips * (new + rows) * width * q_width,
        moved=4 * q_width * width,
    )
    wu_sib, wd_sib = hop(wu, 1), hop(wd, 1)
    partials = exchange(partial)
    results = call(
        functools.partial(expert_kernel, chips, per),
        "expert",
        [in_vmem((2 * per, width), BF16)] * chips,
        [(block, vmem) for block in partials]
        + [(picked, vmem), (weight, vmem), (ffn, vmem)]
        + [(w, vmem) for w in (wg, wu, wd, wg_sib, wu_sib, wd_sib)],
        limit=16,
        flops=12 * rows * width * w_gate.shape[1],
        moved=12 * width * w_gate.shape[1],
    )
    returned = exchange(results)
    hidden = call(
        functools.partial(hidden_kernel, chips),
        "hidden",
        [in_vmem((new, width), F32)],
        [(block, vmem) for block in partials] + [(residual_in, vmem)],
        limit=8,
        moved=2 * chips * new * width,
    )[0]
    return call(
        functools.partial(combine_kernel, chips),
        "combine",
        [jax.ShapeDtypeStruct((new, width), BF16)],
        [(hidden, vmem), (combine, vmem)] + [(block, vmem) for block in returned],
        limit=8,
        moved=6 * new * width,
    )[0]


def solution(mesh):
    in_specs = (
        P(("group", "tensor"), None),
        P(),
        P(None, "tensor"),
        P("tensor", None),
        P(),
        P(),
        P("tensor", None),
        P(),
        P("tensor", None, None),
        P("tensor", None, None),
        P("tensor", None, None),
        P(("group", "tensor"), None, None),
        P(("group", "tensor"), None, None),
        P(("group", "tensor")),
        P(("group", "tensor")),
        P(("group", "tensor"), None),
        P(("group", "tensor"), None),
        P(("group", "tensor")),
        P("group", None),
        P("group", None),
    )
    out_specs = P(("group", "tensor"), None)
    return jax.shard_map(body, mesh=mesh, in_specs=in_specs, out_specs=out_specs, check_vma=False)
```

profile of v0, /device:TPU:0, one launch (start us, length us, event | category | flops | bytes accessed | tf_op | source)
XLA Modules:
  0.0 55.4 jit_solution(10096043813565206795)
XLA Ops:
  0.0 0.5 collective-permute-start.3
  0.5 3.9 %collective-permute-start.2 = (bf16[32,2048]{1,0:T(8,128)(2,1)}, bf16[32,2048]{1,0:T(8,128)(2,1)S(1)}, u32[]{:S(2)}, u32[]{:S(2)}) collective-permute-start(bf16[32,2048]{1,0:T(8,128)(2,1)} %refs_4_.2), channel_id=1, source_target_pairs={{0,6},{1,7},{2,4},{3,5},{4,2},{5,3},{6,0},{7,1},{8,14},{9,15},{10,... | collective-permute-start | bytes 393224 | tf_op jit(solution)/shard_map/ppermute | solution.py:72
  4.4 0.5 collective-permute-start.1
  6.9 3.4 %prep.1 = (bf16[4,640,128]{2,1,0:T(8,128)(2,1)S(1)}, bf16[4,640,128]{2,1,0:T(8,128)(2,1)S(1)}, f32[32,640]{1,0:T(8,128)S(1)}, f32[4,32,128]{2,1,0:T(8,128)S(1)},...) custom-call(bf16[1,1024,512]{2,1,0:T(8,128)(2,1)} %refs_0_.3, ...), custom_call_target="tpu_custom_call" | custom-call | bytes 2621440 | tf_op jit(solution)/shard_map/prep/pallas_call | solution.py:57
  10.3 0.8 %collective-permute-done.1.refs_2_ = bf16[32,2048]{1,0:T(8,128)(2,1)S(1)} collective-permute-done((bf16[32,2048]{1,0:T(8,128)(2,1)}, bf16[32,2048]{1,0:T(8,128)(2,1)S(1)}, u32[]{:S(2)}, u32[]{:S(2)}) %collective-permute-start.1) | collective-permute-done | bytes 131104 | tf_op jit(solution)/shard_map/ppermute | solution.py:72
  11.4 1.1 %project.1 = (bf16[32,1280]{1,0:T(8,128)(2,1)S(1)}, bf16[32,1280]{1,0:T(8,128)(2,1)S(1)}, bf16[32,1280]{1,0:T(8,128)(2,1)S(1)}, bf16[32,1280]{1,0:T(8,128)(2,1)S(1)}, bf16[512,2048]{1,0:T(8,128)(2,1)S(1)}) custom-call(bf16[32,2048]{1,0:T(8,128)(2,1)S(1)} %copy-done, ...), custom_call_target="tpu_custom_call", output_to_operand_aliasing={{4}: (9, {})} | custom-call | flops 671088640 | bytes 5242880 | tf_op jit(solution)/shard_map/project/pallas_call | solution.py:57
  12.6 1.6 %collective-permute-start.5 = (bf16[32,1280]{1,0:T(8,128)(2,1)S(1)}, bf16[32,1280]{1,0:T(8,128)(2,1)S(1)}, u32[]{:S(2)}, u32[]{:S(2)}) collective-permute-start(bf16[32,1280]{1,0:T(8,128)(2,1)S(1)} %get-tuple-element.46), channel_id=1, source_target_pairs={{0,2},{1,3},{2,0},{3,1},{4,6},{5,7},{6,4},{7,5},{8,10},{9,11},{10,... | collective-permute-start | bytes 245768 | tf_op jit(solution)/shard_map/ppermute | solution.py:72
  14.2 0.9 %collective-permute-start.6 = (bf16[32,1280]{1,0:T(8,128)(2,1)S(1)}, bf16[32,1280]{1,0:T(8,128)(2,1)S(1)}, u32[]{:S(2)}, u32[]{:S(2)}) collective-permute-start(bf16[32,1280]{1,0:T(8,128)(2,1)S(1)} %get-tuple-element.47), channel_id=1, source_target_pairs={{0,4},{1,5},{2,6},{3,7},{4,0},{5,1},{6,2},{7,3},{8,12},{9,13},{10,... | collective-permute-start | bytes 245768 | tf_op jit(solution)/shard_map/ppermute | solution.py:72
  15.1 1.0 %collective-permute-start.7 = (bf16[32,1280]{1,0:T(8,128)(2,1)S(1)}, bf16[32,1280]{1,0:T(8,128)(2,1)S(1)}, u32[]{:S(2)}, u32[]{:S(2)}) collective-permute-start(bf16[32,1280]{1,0:T(8,128)(2,1)S(1)} %get-tuple-element.48), channel_id=1, source_target_pairs={{0,6},{1,7},{2,4},{3,5},{4,2},{5,3},{6,0},{7,1},{8,14},{9,15},{10,... | collective-permute-start | bytes 245768 | tf_op jit(solution)/shard_map/ppermute | solution.py:72
  16.1 1.9 %select.1 = (f32[16,2048]{1,0:T(8,128)S(1)}, bf16[1,768,2048]{2,1,0:T(8,128)(2,1)S(1)}) custom-call(bf16[32,2048]{1,0:T(8,128)(2,1)S(1)} %copy-done, bf16[32,2048]{1,0:T(8,128)(2,1)S(1)} %collective-permute-done.refs_1_, bf16[32,2048]{1,0:T(8,128)(2,1)S(1)} %collective-permute-done.1.refs_2_, bf16[32,2048]{1,0:T(8,128)(2,1)S(1)} %collective-permute-done.2.refs_3_, ...), custom_call_target="tpu_custom_call" | custom-call | flops 8388608 | bytes 12582912 | tf_op jit(solution)/shard_map/select/pallas_call | solution.py:57
  18.1 1.5 %collective-permute-done.6.refs_2_ = bf16[32,1280]{1,0:T(8,128)(2,1)S(1)} collective-permute-done((bf16[32,1280]{1,0:T(8,128)(2,1)S(1)}, bf16[32,1280]{1,0:T(8,128)(2,1)S(1)}, u32[]{:S(2)}, u32[]{:S(2)}) %collective-permute-start.6) | collective-permute-done | bytes 81952 | tf_op jit(solution)/shard_map/ppermute | solution.py:72
  19.6 0.9 %collective-permute-done.7.refs_3_ = bf16[32,1280]{1,0:T(8,128)(2,1)S(1)} collective-permute-done((bf16[32,1280]{1,0:T(8,128)(2,1)S(1)}, bf16[32,1280]{1,0:T(8,128)(2,1)S(1)}, u32[]{:S(2)}, u32[]{:S(2)}) %collective-permute-start.7) | collective-permute-done | bytes 81952 | tf_op jit(solution)/shard_map/ppermute | solution.py:72
  20.5 2.1 %attend.1 = (bf16[32,1024]{1,0:T(8,128)(2,1)S(1)}, bf16[32,1024]{1,0:T(8,128)(2,1)S(1)}, bf16[32,1024]{1,0:T(8,128)(2,1)S(1)}, bf16[32,1024]{1,0:T(8,128)(2,1)S(1)}, bf16[1,768,2048]{2,1,0:T(8,128)(2,1)S(1)}) custom-call(bf16[32,1280]{1,0:T(8,128)(2,1)S(1)} %get-tuple-element.45.refs_5_.refs_0_, ...), custom_call_target="tpu_custom_call", output_to_operand_aliasing={{4}: (9, {})} | custom-call | flops 335544320 | bytes 1310720 | tf_op jit(solution)/shard_map/attend/pallas_call | solution.py:57
  22.7 1.1 %collective-permute-start.9 = (bf16[32,1024]{1,0:T(8,128)(2,1)S(1)}, bf16[32,1024]{1,0:T(8,128)(2,1)S(1)}, u32[]{:S(2)}, u32[]{:S(2)}) collective-permute-start(bf16[32,1024]{1,0:T(8,128)(2,1)S(1)} %get-tuple-element.57), channel_id=1, source_target_pairs={{0,2},{1,3},{2,0},{3,1},{4,6},{5,7},{6,4},{7,5},{8,10},{9,11},{10,... | collective-permute-start | bytes 196616 | tf_op jit(solution)/shard_map/ppermute | solution.py:72
  23.7 0.9 %collective-permute-start.10 = (bf16[32,1024]{1,0:T(8,128)(2,1)S(1)}, bf16[32,1024]{1,0:T(8,128)(2,1)S(1)}, u32[]{:S(2)}, u32[]{:S(2)}) collective-permute-start(bf16[32,1024]{1,0:T(8,128)(2,1)S(1)} %get-tuple-element.58), channel_id=1, source_target_pairs={{0,4},{1,5},{2,6},{3,7},{4,0},{5,1},{6,2},{7,3},{8,12},{9,13},{10,... | collective-permute-start | bytes 196616 | tf_op jit(solution)/shard_map/ppermute | solution.py:72
  24.7 1.5 %collective-permute-start.11 = (bf16[32,1024]{1,0:T(8,128)(2,1)S(1)}, bf16[32,1024]{1,0:T(8,128)(2,1)S(1)}, u32[]{:S(2)}, u32[]{:S(2)}) collective-permute-start(bf16[32,1024]{1,0:T(8,128)(2,1)S(1)} %get-tuple-element.59), channel_id=1, source_target_pairs={{0,6},{1,7},{2,4},{3,5},{4,2},{5,3},{6,0},{7,1},{8,14},{9,15},{10,... | collective-permute-start | bytes 196616 | tf_op jit(solution)/shard_map/ppermute | solution.py:72
  26.2 2.9 %fetch.1 = (bf16[1,768,2048]{2,1,0:T(8,128)(2,1)S(1)}, bf16[1,768,2048]{2,1,0:T(8,128)(2,1)S(1)}) custom-call(bf16[32,1024]{1,0:T(8,128)(2,1)S(1)} %get-tuple-element.56._.refs_0_, bf16[1,768,2048]{2,1,0:T(8,128)(2,1)} %up_in.1, bf16[1,768,2048]{2,1,0:T(8,128)(2,1)} %down_in.1), custom_call_target="tpu_custom_call" | custom-call | bytes 12582912 | tf_op jit(solution)/shard_map/fetch/pallas_call | solution.py:57
  29.1 0.7 %collective-permute-done.11.refs_3_ = bf16[32,1024]{1,0:T(8,128)(2,1)S(1)} collective-permute-done((bf16[32,1024]{1,0:T(8,128)(2,1)S(1)}, bf16[32,1024]{1,0:T(8,128)(2,1)S(1)}, u32[]{:S(2)}, u32[]{:S(2)}) %collective-permute-start.11) | collective-permute-done | bytes 65568 | tf_op jit(solution)/shard_map/ppermute | solution.py:72
  29.8 1.1 %spread.1 = (bf16[48,2048]{1,0:T(8,128)(2,1)S(1)}, bf16[48,2048]{1,0:T(8,128)(2,1)S(1)}, bf16[48,2048]{1,0:T(8,128)(2,1)S(1)}, bf16[48,2048]{1,0:T(8,128)(2,1)S(...) custom-call(bf16[32,1024]{1,0:T(8,128)(2,1)S(1)} %get-tuple-element., ...), custom_call_target="tpu_custom_call", output_to_operand_aliasing={{4}: (8, {}), {5}: (9, {})} | custom-call | flops 805306368 | bytes 4194304 | tf_op jit(solution)/shard_map/spread/pallas_call | solution.py:57
  31.0 0.5 collective-permute-start.17
  31.5 1.2 %collective-permute-start.13 = (bf16[48,2048]{1,0:T(8,128)(2,1)S(1)}, bf16[48,2048]{1,0:T(8,128)(2,1)S(1)}, u32[]{:S(2)}, u32[]{:S(2)}) collective-permute-start(bf16[48,2048]{1,0:T(8,128)(2,1)S(1)} %get-tuple-element.64), channel_id=1, source_target_pairs={{0,2},{1,3},{2,0},{3,1},{4,6},{5,7},{6,4},{7,5},{8,10},{9,11},{10,... | collective-permute-start | bytes 589832 | tf_op jit(solution)/shard_map/ppermute | solution.py:72
  32.7 0.9 %collective-permute-start.14 = (bf16[48,2048]{1,0:T(8,128)(2,1)S(1)}, bf16[48,2048]{1,0:T(8,128)(2,1)S(1)}, u32[]{:S(2)}, u32[]{:S(2)}) collective-permute-start(bf16[48,2048]{1,0:T(8,128)(2,1)S(1)} %get-tuple-element.65), channel_id=1, source_target_pairs={{0,4},{1,5},{2,6},{3,7},{4,0},{5,1},{6,2},{7,3},{8,12},{9,13},{10,... | collective-permute-start | bytes 589832 | tf_op jit(solution)/shard_map/ppermute | solution.py:72
  33.6 1.4 %collective-permute-start.15 = (bf16[48,2048]{1,0:T(8,128)(2,1)S(1)}, bf16[48,2048]{1,0:T(8,128)(2,1)S(1)}, u32[]{:S(2)}, u32[]{:S(2)}) collective-permute-start(bf16[48,2048]{1,0:T(8,128)(2,1)S(1)} %get-tuple-element.66), channel_id=1, source_target_pairs={{0,6},{1,7},{2,4},{3,5},{4,2},{5,3},{6,0},{7,1},{8,14},{9,15},{10,... | collective-permute-start | bytes 589832 | tf_op jit(solution)/shard_map/ppermute | solution.py:72
  35.0 4.3 %collective-permute-done.13.refs_1_ = bf16[48,2048]{1,0:T(8,128)(2,1)S(1)} collective-permute-done((bf16[48,2048]{1,0:T(8,128)(2,1)S(1)}, bf16[48,2048]{1,0:T(8,128)(2,1)S(1)}, u32[]{:S(2)}, u32[]{:S(2)}) %collective-permute-start.13) | collective-permute-done | bytes 196640 | tf_op jit(solution)/shard_map/ppermute | solution.py:72
  39.3 4.2 %collective-permute-done.14.refs_2_ = bf16[48,2048]{1,0:T(8,128)(2,1)S(1)} collective-permute-done((bf16[48,2048]{1,0:T(8,128)(2,1)S(1)}, bf16[48,2048]{1,0:T(8,128)(2,1)S(1)}, u32[]{:S(2)}, u32[]{:S(2)}) %collective-permute-start.14) | collective-permute-done | bytes 196640 | tf_op jit(solution)/shard_map/ppermute | solution.py:72
  43.5 4.5 %expert.1 = (bf16[4,2048]{1,0:T(4,128)(2,1)S(1)}, bf16[4,2048]{1,0:T(4,128)(2,1)S(1)}, bf16[4,2048]{1,0:T(4,128)(2,1)S(1)}, bf16[4,2048]{1,0:T(4,128)(2,1)S(1)}) custom-call(bf16[48,2048]{1,0:T(8,128)(2,1)S(1)} %get-tuple-element.63.refs_0_, bf16[48,2048]{1,0:T(8,128)(2,1)S(1)} %collective-permute-done.13.refs_1_, ...), custom_call_target="tpu_custom_call" | custom-call | flops 301989888 | bytes 18874368 | tf_op jit(solution)/shard_map/expert/pallas_call | solution.py:57
  48.0 0.9 %collective-permute-start.18 = (bf16[4,2048]{1,0:T(4,128)(2,1)S(1)}, bf16[4,2048]{1,0:T(4,128)(2,1)S(1)}, u32[]{:S(2)}, u32[]{:S(2)}) collective-permute-start(bf16[4,2048]{1,0:T(4,128)(2,1)S(1)} %get-tuple-element.74), channel_id=1, source_target_pairs={{0,2},{1,3},{2,0},{3,1},{4,6},{5,7},{6,4},{7,5},{8,10},{9,11},{10,... | collective-permute-start | bytes 49160 | tf_op jit(solution)/shard_map/ppermute | solution.py:72
  48.9 1.1 %collective-permute-start.19 = (bf16[4,2048]{1,0:T(4,128)(2,1)S(1)}, bf16[4,2048]{1,0:T(4,128)(2,1)S(1)}, u32[]{:S(2)}, u32[]{:S(2)}) collective-permute-start(bf16[4,2048]{1,0:T(4,128)(2,1)S(1)} %get-tuple-element.75), channel_id=1, source_target_pairs={{0,4},{1,5},{2,6},{3,7},{4,0},{5,1},{6,2},{7,3},{8,12},{9,13},{10,... | collective-permute-start | bytes 49160 | tf_op jit(solution)/shard_map/ppermute | solution.py:72
  50.0 1.5 %collective-permute-start.20 = (bf16[4,2048]{1,0:T(4,128)(2,1)S(1)}, bf16[4,2048]{1,0:T(4,128)(2,1)S(1)}, u32[]{:S(2)}, u32[]{:S(2)}) collective-permute-start(bf16[4,2048]{1,0:T(4,128)(2,1)S(1)} %get-tuple-element.76), channel_id=1, source_target_pairs={{0,6},{1,7},{2,4},{3,5},{4,2},{5,3},{6,0},{7,1},{8,14},{9,15},{10,... | collective-permute-start | bytes 49160 | tf_op jit(solution)/shard_map/ppermute | solution.py:72
  51.8 0.8 %collective-permute-done.19.refs_4_ = bf16[4,2048]{1,0:T(4,128)(2,1)S(1)} collective-permute-done((bf16[4,2048]{1,0:T(4,128)(2,1)S(1)}, bf16[4,2048]{1,0:T(4,128)(2,1)S(1)}, u32[]{:S(2)}, u32[]{:S(2)}) %collective-permute-start.19) | collective-permute-done | bytes 16416 | tf_op jit(solution)/shard_map/ppermute | solution.py:72
  52.6 2.0 %collective-permute-done.20.refs_5_ = bf16[4,2048]{1,0:T(4,128)(2,1)S(1)} collective-permute-done((bf16[4,2048]{1,0:T(4,128)(2,1)S(1)}, bf16[4,2048]{1,0:T(4,128)(2,1)S(1)}, u32[]{:S(2)}, u32[]{:S(2)}) %collective-permute-start.20) | collective-permute-done | bytes 16416 | tf_op jit(solution)/shard_map/ppermute | solution.py:72
  54.6 0.8 %combine.1 = bf16[32,2048]{1,0:T(8,128)(2,1)} custom-call(f32[32,2048]{1,0:T(8,128)S(1)} %hidden.1.refs_0_, f32[32,16]{1,0:T(8,128)S(1)} %get-tuple-element.67.refs_1_, bf16[4,2048]{1,0:T(4,128)(2,1)S(1)} %get-tuple-element.73.refs_2_, bf16[4,2048]{1,0:T(4,128)(2,1)S(1)} %collective-permute-done.18.refs_3_, ...), custom_call_target="tpu_custom_call" | custom-call | bytes 393216 | tf_op jit(solution)/shard_map/combine/pallas_call | solution.py:57
  (21 shorter events, 0.9 us)
Async XLA Ops:
  0.0 11.4 %collective-permute-start.3 = (bf16[2048,512]{1,0:T(8,128)(2,1)}, bf16[2048,512]{1,0:T(8,128)(2,1)S(1)}, u32[]{:S(2)}, u32[]{:S(2)}) collective-permute-start(bf16[2048,512]{1,0:T(8,128)(2,1)} %refs_14_.1), channel_id=1, source_target_pairs={{0,1},{1,0},{2,3},{3,2},{4,5},{5,4},{6,7},{7,6},{8,9},{9,8},{10,11... | collective-permute-start | bytes 6291464 | tf_op jit(solution)/shard_map/ppermute | solution.py:72
  0.5 10.9 %collective-permute-start.4 = (bf16[128,2048]{1,0:T(8,128)(2,1)}, bf16[128,2048]{1,0:T(8,128)(2,1)S(1)}, u32[]{:S(2)}, u32[]{:S(2)}) collective-permute-start(bf16[128,2048]{1,0:T(8,128)(2,1)} %refs_15_.1), channel_id=1, source_target_pairs={{0,1},{1,0},{2,3},{3,2},{4,5},{5,4},{6,7},{7,6},{8,9},{9,8},{10,11... | collective-permute-start | bytes 1572872 | tf_op jit(solution)/shard_map/ppermute | solution.py:72
  0.5 9.8 %collective-permute-start.2 = (bf16[32,2048]{1,0:T(8,128)(2,1)}, bf16[32,2048]{1,0:T(8,128)(2,1)S(1)}, u32[]{:S(2)}, u32[]{:S(2)}) collective-permute-start(bf16[32,2048]{1,0:T(8,128)(2,1)} %refs_4_.2), channel_id=1, source_target_pairs={{0,6},{1,7},{2,4},{3,5},{4,2},{5,3},{6,0},{7,1},{8,14},{9,15},{10,... | collective-permute-start | bytes 393224 | tf_op jit(solution)/shard_map/ppermute | solution.py:72
  4.4 6.7 %collective-permute-start.1 = (bf16[32,2048]{1,0:T(8,128)(2,1)}, bf16[32,2048]{1,0:T(8,128)(2,1)S(1)}, u32[]{:S(2)}, u32[]{:S(2)}) collective-permute-start(bf16[32,2048]{1,0:T(8,128)(2,1)} %refs_4_.2), channel_id=1, source_target_pairs={{0,4},{1,5},{2,6},{3,7},{4,0},{5,1},{6,2},{7,3},{8,12},{9,13},{10,... | collective-permute-start | bytes 393224 | tf_op jit(solution)/shard_map/ppermute | solution.py:72
  4.9 6.4 %collective-permute-start = (bf16[32,2048]{1,0:T(8,128)(2,1)}, bf16[32,2048]{1,0:T(8,128)(2,1)S(1)}, u32[]{:S(2)}, u32[]{:S(2)}) collective-permute-start(bf16[32,2048]{1,0:T(8,128)(2,1)} %refs_4_.2), channel_id=1, source_target_pairs={{0,2},{1,3},{2,0},{3,1},{4,6},{5,7},{6,4},{7,5},{8,10},{9,11},{10,... | collective-permute-start | bytes 393224 | tf_op jit(solution)/shard_map/ppermute | solution.py:72
  6.9 4.4 %copy-start = (bf16[32,2048]{1,0:T(8,128)(2,1)S(1)}, bf16[32,2048]{1,0:T(8,128)(2,1)}, u32[]{:S(2)}) copy-start(bf16[32,2048]{1,0:T(8,128)(2,1)} %refs_4_.2) | copy-start | bytes 393220
  12.5 8.0 %collective-permute-start.8 = (bf16[512,2048]{1,0:T(8,128)(2,1)S(1)}, bf16[512,2048]{1,0:T(8,128)(2,1)S(1)}, u32[]{:S(2)}, u32[]{:S(2)}) collective-permute-start(bf16[512,2048]{1,0:T(8,128)(2,1)S(1)} %get-tuple-element.53.refs_5_), channel_id=1, source_target_pairs={{0,1},{1,0},{2,3},{3,2},{4,5},{5,4},{6,7},{7,6},{8,9},{9,8},{10,11... | collective-permute-start | bytes 6291464 | tf_op jit(solution)/shard_map/ppermute | solution.py:72
  12.6 5.5 %collective-permute-start.5 = (bf16[32,1280]{1,0:T(8,128)(2,1)S(1)}, bf16[32,1280]{1,0:T(8,128)(2,1)S(1)}, u32[]{:S(2)}, u32[]{:S(2)}) collective-permute-start(bf16[32,1280]{1,0:T(8,128)(2,1)S(1)} %get-tuple-element.46), channel_id=1, source_target_pairs={{0,2},{1,3},{2,0},{3,1},{4,6},{5,7},{6,4},{7,5},{8,10},{9,11},{10,... | collective-permute-start | bytes 245768 | tf_op jit(solution)/shard_map/ppermute | solution.py:72
  14.2 5.4 %collective-permute-start.6 = (bf16[32,1280]{1,0:T(8,128)(2,1)S(1)}, bf16[32,1280]{1,0:T(8,128)(2,1)S(1)}, u32[]{:S(2)}, u32[]{:S(2)}) collective-permute-start(bf16[32,1280]{1,0:T(8,128)(2,1)S(1)} %get-tuple-element.47), channel_id=1, source_target_pairs={{0,4},{1,5},{2,6},{3,7},{4,0},{5,1},{6,2},{7,3},{8,12},{9,13},{10,... | collective-permute-start | bytes 245768 | tf_op jit(solution)/shard_map/ppermute | solution.py:72
  15.1 5.3 %collective-permute-start.7 = (bf16[32,1280]{1,0:T(8,128)(2,1)S(1)}, bf16[32,1280]{1,0:T(8,128)(2,1)S(1)}, u32[]{:S(2)}, u32[]{:S(2)}) collective-permute-start(bf16[32,1280]{1,0:T(8,128)(2,1)S(1)} %get-tuple-element.48), channel_id=1, source_target_pairs={{0,6},{1,7},{2,4},{3,5},{4,2},{5,3},{6,0},{7,1},{8,14},{9,15},{10,... | collective-permute-start | bytes 245768 | tf_op jit(solution)/shard_map/ppermute | solution.py:72
  22.6 7.3 %collective-permute-start.12 = (bf16[1,768,2048]{2,1,0:T(8,128)(2,1)S(1)}, bf16[1,768,2048]{2,1,0:T(8,128)(2,1)S(1)}, u32[]{:S(2)}, u32[]{:S(2)}) collective-permute-start(bf16[1,768,2048]{2,1,0:T(8,128)(2,1)S(1)} %get-tuple-element.60.refs_7_), channel_id=1, source_target_pairs={{0,1},{1,0},{2,3},{3,2},{4,5},{5,4},{6,7},{7,6},{8,9},{9,8},{10,11... | collective-permute-start | bytes 9437192 | tf_op jit(solution)/shard_map/ppermute | solution.py:72
  22.7 6.4 %collective-permute-start.9 = (bf16[32,1024]{1,0:T(8,128)(2,1)S(1)}, bf16[32,1024]{1,0:T(8,128)(2,1)S(1)}, u32[]{:S(2)}, u32[]{:S(2)}) collective-permute-start(bf16[32,1024]{1,0:T(8,128)(2,1)S(1)} %get-tuple-element.57), channel_id=1, source_target_pairs={{0,2},{1,3},{2,0},{3,1},{4,6},{5,7},{6,4},{7,5},{8,10},{9,11},{10,... | collective-permute-start | bytes 196616 | tf_op jit(solution)/shard_map/ppermute | solution.py:72
  23.7 5.3 %collective-permute-start.10 = (bf16[32,1024]{1,0:T(8,128)(2,1)S(1)}, bf16[32,1024]{1,0:T(8,128)(2,1)S(1)}, u32[]{:S(2)}, u32[]{:S(2)}) collective-permute-start(bf16[32,1024]{1,0:T(8,128)(2,1)S(1)} %get-tuple-element.58), channel_id=1, source_target_pairs={{0,4},{1,5},{2,6},{3,7},{4,0},{5,1},{6,2},{7,3},{8,12},{9,13},{10,... | collective-permute-start | bytes 196616 | tf_op jit(solution)/shard_map/ppermute | solution.py:72
  24.7 5.2 %collective-permute-start.11 = (bf16[32,1024]{1,0:T(8,128)(2,1)S(1)}, bf16[32,1024]{1,0:T(8,128)(2,1)S(1)}, u32[]{:S(2)}, u32[]{:S(2)}) collective-permute-start(bf16[32,1024]{1,0:T(8,128)(2,1)S(1)} %get-tuple-element.59), channel_id=1, source_target_pairs={{0,6},{1,7},{2,4},{3,5},{4,2},{5,3},{6,0},{7,1},{8,14},{9,15},{10,... | collective-permute-start | bytes 196616 | tf_op jit(solution)/shard_map/ppermute | solution.py:72
  31.0 12.6 %collective-permute-start.16 = (bf16[1,768,2048]{2,1,0:T(8,128)(2,1)S(1)}, bf16[1,768,2048]{2,1,0:T(8,128)(2,1)S(1)}, u32[]{:S(2)}, u32[]{:S(2)}) collective-permute-start(bf16[1,768,2048]{2,1,0:T(8,128)(2,1)S(1)} %get-tuple-element.71.refs_8_), channel_id=1, source_target_pairs={{0,1},{1,0},{2,3},{3,2},{4,5},{5,4},{6,7},{7,6},{8,9},{9,8},{10,11... | collective-permute-start | bytes 9437192 | tf_op jit(solution)/shard_map/ppermute | solution.py:72
  31.0 12.5 %collective-permute-start.17 = (bf16[1,768,2048]{2,1,0:T(8,128)(2,1)S(1)}, bf16[1,768,2048]{2,1,0:T(8,128)(2,1)S(1)}, u32[]{:S(2)}, u32[]{:S(2)}) collective-permute-start(bf16[1,768,2048]{2,1,0:T(8,128)(2,1)S(1)} %get-tuple-element.72.refs_9_), channel_id=1, source_target_pairs={{0,1},{1,0},{2,3},{3,2},{4,5},{5,4},{6,7},{7,6},{8,9},{9,8},{10,11... | collective-permute-start | bytes 9437192 | tf_op jit(solution)/shard_map/ppermute | solution.py:72
  31.5 7.8 %collective-permute-start.13 = (bf16[48,2048]{1,0:T(8,128)(2,1)S(1)}, bf16[48,2048]{1,0:T(8,128)(2,1)S(1)}, u32[]{:S(2)}, u32[]{:S(2)}) collective-permute-start(bf16[48,2048]{1,0:T(8,128)(2,1)S(1)} %get-tuple-element.64), channel_id=1, source_target_pairs={{0,2},{1,3},{2,0},{3,1},{4,6},{5,7},{6,4},{7,5},{8,10},{9,11},{10,... | collective-permute-start | bytes 589832 | tf_op jit(solution)/shard_map/ppermute | solution.py:72
  32.7 10.8 %collective-permute-start.14 = (bf16[48,2048]{1,0:T(8,128)(2,1)S(1)}, bf16[48,2048]{1,0:T(8,128)(2,1)S(1)}, u32[]{:S(2)}, u32[]{:S(2)}) collective-permute-start(bf16[48,2048]{1,0:T(8,128)(2,1)S(1)} %get-tuple-element.65), channel_id=1, source_target_pairs={{0,4},{1,5},{2,6},{3,7},{4,0},{5,1},{6,2},{7,3},{8,12},{9,13},{10,... | collective-permute-start | bytes 589832 | tf_op jit(solution)/shard_map/ppermute | solution.py:72
  33.6 9.9 %collective-permute-start.15 = (bf16[48,2048]{1,0:T(8,128)(2,1)S(1)}, bf16[48,2048]{1,0:T(8,128)(2,1)S(1)}, u32[]{:S(2)}, u32[]{:S(2)}) collective-permute-start(bf16[48,2048]{1,0:T(8,128)(2,1)S(1)} %get-tuple-element.66), channel_id=1, source_target_pairs={{0,6},{1,7},{2,4},{3,5},{4,2},{5,3},{6,0},{7,1},{8,14},{9,15},{10,... | collective-permute-start | bytes 589832 | tf_op jit(solution)/shard_map/ppermute | solution.py:72
  48.0 3.8 %collective-permute-start.18 = (bf16[4,2048]{1,0:T(4,128)(2,1)S(1)}, bf16[4,2048]{1,0:T(4,128)(2,1)S(1)}, u32[]{:S(2)}, u32[]{:S(2)}) collective-permute-start(bf16[4,2048]{1,0:T(4,128)(2,1)S(1)} %get-tuple-element.74), channel_id=1, source_target_pairs={{0,2},{1,3},{2,0},{3,1},{4,6},{5,7},{6,4},{7,5},{8,10},{9,11},{10,... | collective-permute-start | bytes 49160 | tf_op jit(solution)/shard_map/ppermute | solution.py:72
  48.9 3.7 %collective-permute-start.19 = (bf16[4,2048]{1,0:T(4,128)(2,1)S(1)}, bf16[4,2048]{1,0:T(4,128)(2,1)S(1)}, u32[]{:S(2)}, u32[]{:S(2)}) collective-permute-start(bf16[4,2048]{1,0:T(4,128)(2,1)S(1)} %get-tuple-element.75), channel_id=1, source_target_pairs={{0,4},{1,5},{2,6},{3,7},{4,0},{5,1},{6,2},{7,3},{8,12},{9,13},{10,... | collective-permute-start | bytes 49160 | tf_op jit(solution)/shard_map/ppermute | solution.py:72
  50.0 4.6 %collective-permute-start.20 = (bf16[4,2048]{1,0:T(4,128)(2,1)S(1)}, bf16[4,2048]{1,0:T(4,128)(2,1)S(1)}, u32[]{:S(2)}, u32[]{:S(2)}) collective-permute-start(bf16[4,2048]{1,0:T(4,128)(2,1)S(1)} %get-tuple-element.76), channel_id=1, source_target_pairs={{0,6},{1,7},{2,4},{3,5},{4,2},{5,3},{6,0},{7,1},{8,14},{9,15},{10,... | collective-permute-start | bytes 49160 | tf_op jit(solution)/shard_map/ppermute | solution.py:72
where the time goes:
time: 55.6 us; the launch traced here: 55.4 us
  starting transfers between devices  19.8 us (36%)
  Pallas kernels  17.8 us (32%)
  waiting for transfers between devices  15.7 us (28%)
  between operations  2.08 us (4%)
    ppermute x21, starting transfers between devices, hop(): lax.ppermute(value, 'tensor', [(i, i ^ step) for i in range(devices)])  19.8 us
    pallas_call x9, Pallas kernels, call(): pl.pallas_call(kernel, out_shape=outs, in_specs=specs, out_specs=[pl.Bloc...  17.8 us
    ppermute x21, waiting for transfers between devices, hop(): lax.ppermute(value, 'tensor', [(i, i ^ step) for i in range(devices)])  15.7 us
  transfers between devices with their start and end apart: 21, of which 10 were waited for; matrix products, arithmetic and copies ran while one was open for 0% of the time, Pallas kernels for 15%

commit v1 on v0

--- a/solution.py
+++ b/solution.py
@@ -204,16 +204,14 @@
         rank = rank_ref[rel : rel + 1, :]
         chosen = (slot_of == (row_slot ^ (rel // 2))) & hit & (rank == row_rank)
         pick_ref[rel * rows : (rel + 1) * rows, :] = chosen.astype(F32)
-        if rel < 2:
-            named = ids == (me ^ rel).astype(F32)
-            weight = jnp.sum(jnp.where(named, gates, 0.0), axis=0, keepdims=True)
-            weight = jnp.sum(jnp.where(chosen, weight, 0.0), axis=1, keepdims=True)
-            weight_ref[rel * rows : (rel + 1) * rows, :] = jnp.broadcast_to(
-                weight, (rows, weight_ref.shape[1])
-            )
+        named = ids == (me ^ rel).astype(F32)
+        weight = jnp.sum(jnp.where(named, gates, 0.0), axis=0, keepdims=True)
         for place in range(per):
             at = rel * per + place
-            own_ref[at : at + 1, :] = (in_first & hit & (rank == float(place))).astype(F32)
+            own = in_first & hit & (rank == float(place))
+            own_ref[at : at + 1, :] = own.astype(F32)
+            one = jnp.sum(jnp.where(own, weight, 0.0), axis=1, keepdims=True)
+            weight_ref[at : at + 1, :] = jnp.broadcast_to(one, (1, weight_ref.shape[1]))
     first = (iota((tokens, new), 0) == iota((tokens, new), 1)).astype(F32)
     combine_ref[...] = lax.dot_general(
         first.astype(BF16),
@@ -296,7 +294,8 @@
 def spread_kernel(chips, *refs):
     got = refs[:chips]
     pick_ref, w_ref, w_sib = refs[chips : chips + 3]
-    outs = refs[chips + 6 : 2 * chips + 6]
+    for_experts = refs[chips + 4 : 2 * chips + 4]
+    for_slots = refs[2 * chips + 4 : 3 * chips + 4]
     rows_ref = refs[-1]
     new = got[0].shape[0]
     depth, width = w_ref.shape
@@ -313,26 +312,23 @@
         part = dot(left[:, :depth], w_ref[:, at : at + tile])
         part = (part + dot(left[:, depth:], w_sib[:, at : at + tile])).astype(BF16)
         for j in range(chips):
-            outs[j][:, at : at + tile] = part[j * each : (j + 1) * each]
-
-
-def fetch_kernel(_, up_in, down_in, up_out, down_out, sems):
-    copies = [
-        pltpu.make_async_copy(up_in, up_out, sems.at[0]),
-        pltpu.make_async_copy(down_in, down_out, sems.at[1]),
-    ]
-    for copy in copies:
-        copy.start()
-    for copy in copies:
-        copy.wait()
+            block = part[j * each : (j + 1) * each]
+            for_slots[j][:, at : at + tile] = block[:new]
+            for_experts[j][:, at : at + tile] = block[new:]
+
+
+def fetch_kernel(_, source, target, sem):
+    copy = pltpu.make_async_copy(source, target, sem.at[0])
+    copy.start()
+    copy.wait()
 
 
 def select_kernel(chips, *refs):
     blocks = refs[:chips]
     pick_ref, _ = refs[chips : chips + 2]
-    sources = refs[chips + 2 : chips + 3]
-    picked_ref = refs[chips + 3]
-    targets = refs[chips + 4 : chips + 5]
+    sources = refs[chips + 2 : chips + 4]
+    picked_ref = refs[chips + 4]
+    targets = refs[chips + 5 : chips + 7]
     sems = refs[-1]
     copies = [
         pltpu.make_async_copy(source, target, sems.at[which])
@@ -350,42 +346,55 @@
 def hidden_kernel(chips, *refs):
     got = refs[:chips]
     own_ref, out_ref = refs[chips:]
-    new = own_ref.shape[0]
     total = own_ref[...].astype(F32)
     for j in range(chips):
-        total = total + got[j][0:new, :].astype(F32)
+        total = total + got[j][...].astype(F32)
     out_ref[...] = total
 
 
-def expert_kernel(chips, per, *refs):
+def rows_kernel(chips, *refs):
     got = refs[:chips]
-    picked_ref, weight_ref, gain_ref = refs[chips : chips + 3]
-    weights = refs[chips + 3 : chips + 9]
-    outs = refs[chips + 9 :]
-    rows = chips * per
+    picked_ref, gain_ref, own_ref, other_ref = refs[chips:]
     hidden = picked_ref[...]
-    new = got[0].shape[0] - 2 * rows
     for j in range(chips):
-        hidden = hidden + got[j][new:, :].astype(F32)
-    normed = norm_rows(hidden) * gain_ref[...]
-    for core in range(2):
-        gate_ref, up_ref, down_ref = weights[3 * core : 3 * core + 3]
-        right = normed[core * rows : (core + 1) * rows].astype(BF16)
-        gate = dot_last(gate_ref[0], right)
-        up = dot_last(up_ref[0], right)
-        inner = (gate / (1.0 + jnp.exp(-gate)) * up).astype(BF16)
-        result = dot_first(inner, down_ref[0])
-        result = (result * weight_ref[core * rows : (core + 1) * rows, 0:1]).astype(BF16)
-        for j in range(chips):
-            outs[j][core * per : (core + 1) * per, :] = result[j * per : (j + 1) * per]
+        hidden = hidden + got[j][...].astype(F32)
+    normed = (norm_rows(hidden) * gain_ref[...]).astype(BF16)
+    half = own_ref.shape[0]
+    own_ref[...] = normed[:half]
+    other_ref[...] = normed[half:]
+
+
+def expert_kernel(own_ref, other_ref, gate_ref, up_ref, down_ref, own_out, other_out):
+    left = jnp.concatenate([own_ref[...].astype(F32), other_ref[...].astype(F32)], axis=0)
+    left = left.astype(BF16)
+    gate = dot_last(left, gate_ref[0])
+    up = dot_last(left, up_ref[0])
+    inner = (gate / (1.0 + jnp.exp(-gate)) * up).astype(BF16)
+    result = dot(inner, down_ref[0])
+    half = own_ref.shape[0]
+    own_out[...] = result[:half].astype(BF16)
+    other_out[...] = result[half:].astype(BF16)
+
+
+def pack_kernel(chips, per, own_ref, other_ref, *outs):
+    own, other = own_ref[...].astype(F32), other_ref[...].astype(F32)
+    for j in range(chips):
+        at = slice(j * per, (j + 1) * per)
+        outs[j][...] = jnp.concatenate([own[at], other[at]], axis=0).astype(BF16)
 
 
 def combine_kernel(chips, *refs):
-    hidden_ref, combine_ref = refs[:2]
-    got = refs[2 : 2 + chips]
-    out_ref = refs[2 + chips]
+    hidden_ref, combine_ref, weight_ref = refs[:3]
+    got = refs[3 : 3 + chips]
+    out_ref = refs[3 + chips]
     rows = jnp.concatenate([block[...].astype(F32) for block in got], axis=0)
-    moe = dot(combine_ref[...].astype(BF16), rows.astype(BF16))
+    moe = lax.dot_general(
+        combine_ref[...],
+        rows * weight_ref[:, 0:1],
+        (((1,), (0,)), ((), ())),
+        precision=lax.Precision.HIGHEST,
+        preferred_element_type=F32,
+    )
     out_ref[...] = (hidden_ref[...] + moe).astype(BF16)
 
 
@@ -445,7 +454,7 @@
             in_vmem((4, new, head), F32),
             in_vmem((chips * rows, tokens), F32),
             in_vmem((new, devices * per), F32),
-            in_vmem((rows, 128), F32),
+            in_vmem((devices * per, 128), F32),
         ]
         + [in_vmem(weight.shape, weight.dtype) for weight in weights],
         [
@@ -506,12 +515,12 @@
     wo_sib = hop(wo, 1)
 
     got = exchange(projected)
-    picked, wg = call(
+    picked, wg, wu = call(
         functools.partial(select_kernel, chips),
         "select",
-        [in_vmem((rows, width), F32)] + [in_vmem(w.shape, w.dtype) for w in (w_gate,)],
+        [in_vmem((rows, width), F32)] + [in_vmem(w.shape, w.dtype) for w in (w_gate, w_up)],
         [(block, vmem) for block in blocks]
-        + [(pick, vmem), (projected[0], anywhere), (w_gate, hbm)],
+        + [(pick, vmem), (projected[0], anywhere), (w_gate, hbm), (w_up, hbm)],
         [pltpu.SemaphoreType.DMA((2,))],
         limit=8,
         flops=2 * rows * width * tokens,
@@ -526,66 +535,74 @@
         pieces = jnp.stack(pieces)[lax.axis_index("tensor") ^ jnp.arange(devices)]
         pieces = pieces.transpose(1, 0, 2).reshape(new, 2 * kv_heads, head)
         kv_ready = [(pieces.transpose(1, 0, 2), vmem)]
-    at = chips + len(kv_ready) + 5
-    *attended, wg = call(
+    attended = call(
         functools.partial(attend_kernel, chips, q_width, bool(kv_ready)),
         "attend",
-        [in_vmem((new, 2 * q_width), BF16)] * chips
-        + [in_vmem(w.shape, w.dtype) for w in (wg,)],
+        [in_vmem((new, 2 * q_width), BF16)] * chips,
         [(block, vmem) for block in got]
         + kv_ready
         + [(keys, vmem), (values, vmem), (mask, vmem), (rot, vmem)]
-        + [(wo_sib, anywhere), (wg, vmem)],
+        + [(wo_sib, anywhere), (wg, anywhere)],
         [] if kv_ready else [pltpu.VMEM((devices, new, head), BF16)],
         limit=16,
-        same={at: chips},
         flops=8 * new * chips * q_width * span,
         moved=4 * span * kv_heads * head,
     )
-    wg_sib = hop(wg, 1)
     heads = exchange(attended)
-    wu, wd = call(
+    wd = call(
         fetch_kernel,
         "fetch",
-        [in_vmem(w.shape, w.dtype) for w in (w_up, w_down)],
-        [(attended[0], anywhere), (w_up, hbm), (w_down, hbm)],
-        [pltpu.SemaphoreType.DMA((2,))],
+        [in_vmem(w_down.shape, w_down.dtype)],
+        [(attended[0], anywhere), (w_down, hbm)],
+        [pltpu.SemaphoreType.DMA((1,))],
         limit=8,
-        moved=8 * width * w_gate.shape[1],
-    )
-
-    *partial, wu, wd = call(
+        moved=4 * width * w_gate.shape[1],
+    )[0]
+
+    partial = call(
         functools.partial(spread_kernel, chips),
         "spread",
-        [in_vmem((new + rows, width), BF16)] * chips
-        + [in_vmem(w.shape, w.dtype) for w in (wu, wd)],
-        [(block, vmem) for block in heads]
-        + [(pick, vmem), (wo, vmem), (wo_sib, vmem), (wg_sib, anywhere), (wu, vmem), (wd, vmem)],
+        [in_vmem((rows, width), BF16)] * chips + [in_vmem((new, width), BF16)] * chips,
+        [(block, vmem) for block in heads] + [(pick, vmem), (wo, vmem), (wo_sib, vmem), (wd, anywhere)],
         [pltpu.VMEM((chips, new + rows, 2 * q_width), BF16)],
-        same={chips + 4: chips, chips + 5: chips + 1},
         limit=16,
         flops=4 * chips * (new + rows) * width * q_width,
         moved=4 * q_width * width,
     )
-    wu_sib, wd_sib = hop(wu, 1), hop(wd, 1)
-    partials = exchange(partial)
+    for_experts = exchange(partial[:chips])
+    for_slots = exchange(partial[chips:])
+
+    own, other = call(
+        functools.partial(rows_kernel, chips),
+        "rows",
+        [in_vmem((rows // 2, width), BF16)] * 2,
+        [(block, vmem) for block in for_experts] + [(picked, vmem), (ffn, vmem)],
+        limit=8,
+        moved=2 * chips * rows * width,
+    )
+    own_out, other_out = call(
+        expert_kernel,
+        "expert",
+        [in_vmem((rows // 2, width), BF16)] * 2,
+        [(own, vmem), (hop(other, 1), vmem), (wg, vmem), (wu, vmem), (wd, vmem)],
+        limit=16,
+        flops=6 * rows * width * w_gate.shape[1],
+        moved=6 * width * w_gate.shape[1],
+    )
     results = call(
-        functools.partial(expert_kernel, chips, per),
-        "expert",
+        functools.partial(pack_kernel, chips, per),
+        "pack",
         [in_vmem((2 * per, width), BF16)] * chips,
-        [(block, vmem) for block in partials]
-        + [(picked, vmem), (weight, vmem), (ffn, vmem)]
-        + [(w, vmem) for w in (wg, wu, wd, wg_sib, wu_sib, wd_sib)],
-        limit=16,
-        flops=12 * rows * width * w_gate.shape[1],
-        moved=12 * width * w_gate.shape[1],
+        [(own_out, vmem), (hop(other_out, 1), vmem)],
+        limit=8,
+        moved=4 * rows * width,
     )
     returned = exchange(results)
     hidden = call(
         functools.partial(hidden_kernel, chips),
         "hidden",
         [in_vmem((new, width), F32)],
-        [(block, vmem) for block in partials] + [(residual_in, vmem)],
+        [(block, vmem) for block in for_slots] + [(residual_in, vmem)],
         limit=8,
         moved=2 * chips * new * width,
     )[0]
@@ -593,7 +610,8 @@
         functools.partial(combine_kernel, chips),
         "combine",
         [jax.ShapeDtypeStruct((new, width), BF16)],
-        [(hidden, vmem), (combine, vmem)] + [(block, vmem) for block in returned],
+        [(hidden, vmem), (combine, vmem), (weight, vmem)]
+        + [(block, vmem) for block in returned],
         limit=8,
         moved=6 * new * width,
     )[0]

time: 55.6 us -> 51.7 us (0.930)
  waiting for transfers between devices: 15.7 us -> 10.5 us
  starting transfers between devices: 19.8 us -> 23 us
  Pallas kernels: 17.8 us -> 16 us
    ppermute x21 -> x23, waiting for transfers between devices: 15.7 us -> 10.5 us  [hop(): lax.ppermute(value, 'tensor', [(i, i ^ step) for i in range(devices)])]
    ppermute x21 -> x23, starting transfers between devices: 19.8 us -> 23 us  [hop(): lax.ppermute(value, 'tensor', [(i, i ^ step) for i in range(devices)])]
    pallas_call x9 -> x11, Pallas kernels: 17.8 us -> 16 us  [call(): pl.pallas_call(kernel, out_shape=outs, in_specs=specs, out_specs=[pl.Bloc...]
  transfers between devices with their start and end apart: 21 -> 23, of which waited for: 10 -> 12; matrix products, arithmetic and copies ran while one was open for 0% -> 0% of each run, Pallas kernels for 15% -> 20%
where the time goes in v1:
time: 51.7 us; the launch traced here: 51.6 us
  starting transfers between devices  23 us (44%)
  Pallas kernels  16 us (31%)
  waiting for transfers between devices  10.5 us (20%)
  between operations  2.08 us (4%)
    ppermute x23, starting transfers between devices, hop(): lax.ppermute(value, 'tensor', [(i, i ^ step) for i in range(devices)])  23 us
    pallas_call x11, Pallas kernels, call(): pl.pallas_call(kernel, out_shape=outs, in_specs=specs, out_specs=[pl.Bloc...  16 us
    ppermute x23, waiting for transfers between devices, hop(): lax.ppermute(value, 'tensor', [(i, i ^ step) for i in range(devices)])  10.5 us
  transfers between devices with their start and end apart: 23, of which 12 were waited for; matrix products, arithmetic and copies ran while one was open for 0% of the time, Pallas kernels for 20%

profile of v1, /device:TPU:0, one launch (start us, length us, event | category | flops | bytes accessed | tf_op | source)
XLA Modules:
  0.0 51.6 jit_solution(16459202119906589979)
XLA Ops:
  0.5 3.9 %collective-permute-start.2 = (bf16[32,2048]{1,0:T(8,128)(2,1)}, bf16[32,2048]{1,0:T(8,128)(2,1)S(1)}, u32[]{:S(2)}, u32[]{:S(2)}) collective-permute-start(bf16[32,2048]{1,0:T(8,128)(2,1)} %refs_4_.2), channel_id=1, source_target_pairs={{0,6},{1,7},{2,4},{3,5},{4,2},{5,3},{6,0},{7,1},{8,14},{9,15},{10,... | collective-permute-start | bytes 393224 | tf_op jit(solution)/shard_map/ppermute | solution.py:72
  6.9 3.4 %prep.1 = (bf16[4,640,128]{2,1,0:T(8,128)(2,1)S(1)}, bf16[4,640,128]{2,1,0:T(8,128)(2,1)S(1)}, f32[32,640]{1,0:T(8,128)S(1)}, f32[4,32,128]{2,1,0:T(8,128)S(1)},...) custom-call(bf16[1,1024,512]{2,1,0:T(8,128)(2,1)} %refs_0_.3, ...), custom_call_target="tpu_custom_call" | custom-call | bytes 2621440 | tf_op jit(solution)/shard_map/prep/pallas_call | solution.py:57
  10.3 0.8 %collective-permute-done.1.refs_2_ = bf16[32,2048]{1,0:T(8,128)(2,1)S(1)} collective-permute-done((bf16[32,2048]{1,0:T(8,128)(2,1)}, bf16[32,2048]{1,0:T(8,128)(2,1)S(1)}, u32[]{:S(2)}, u32[]{:S(2)}) %collective-permute-start.1) | collective-permute-done | bytes 131104 | tf_op jit(solution)/shard_map/ppermute | solution.py:72
  11.4 1.1 %project.1 = (bf16[32,1280]{1,0:T(8,128)(2,1)S(1)}, bf16[32,1280]{1,0:T(8,128)(2,1)S(1)}, bf16[32,1280]{1,0:T(8,128)(2,1)S(1)}, bf16[32,1280]{1,0:T(8,128)(2,1)S(1)}, bf16[512,2048]{1,0:T(8,128)(2,1)S(1)}) custom-call(bf16[32,2048]{1,0:T(8,128)(2,1)S(1)} %copy-done, ...), custom_call_target="tpu_custom_call", output_to_operand_aliasing={{4}: (9, {})} | custom-call | flops 671088640 | bytes 5242880 | tf_op jit(solution)/shard_map/project/pallas_call | solution.py:57
  12.6 1.6 %collective-permute-start.5 = (bf16[32,1280]{1,0:T(8,128)(2,1)S(1)}, bf16[32,1280]{1,0:T(8,128)(2,1)S(1)}, u32[]{:S(2)}, u32[]{:S(2)}) collective-permute-start(bf16[32,1280]{1,0:T(8,128)(2,1)S(1)} %get-tuple-element.50), channel_id=1, source_target_pairs={{0,2},{1,3},{2,0},{3,1},{4,6},{5,7},{6,4},{7,5},{8,10},{9,11},{10,... | collective-permute-start | bytes 245768 | tf_op jit(solution)/shard_map/ppermute | solution.py:72
  14.2 0.9 %collective-permute-start.6 = (bf16[32,1280]{1,0:T(8,128)(2,1)S(1)}, bf16[32,1280]{1,0:T(8,128)(2,1)S(1)}, u32[]{:S(2)}, u32[]{:S(2)}) collective-permute-start(bf16[32,1280]{1,0:T(8,128)(2,1)S(1)} %get-tuple-element.51), channel_id=1, source_target_pairs={{0,4},{1,5},{2,6},{3,7},{4,0},{5,1},{6,2},{7,3},{8,12},{9,13},{10,... | collective-permute-start | bytes 245768 | tf_op jit(solution)/shard_map/ppermute | solution.py:72
  15.1 1.0 %collective-permute-start.7 = (bf16[32,1280]{1,0:T(8,128)(2,1)S(1)}, bf16[32,1280]{1,0:T(8,128)(2,1)S(1)}, u32[]{:S(2)}, u32[]{:S(2)}) collective-permute-start(bf16[32,1280]{1,0:T(8,128)(2,1)S(1)} %get-tuple-element.52), channel_id=1, source_target_pairs={{0,6},{1,7},{2,4},{3,5},{4,2},{5,3},{6,0},{7,1},{8,14},{9,15},{10,... | collective-permute-start | bytes 245768 | tf_op jit(solution)/shard_map/ppermute | solution.py:72
  16.1 2.9 %select.1 = (f32[16,2048]{1,0:T(8,128)S(1)}, bf16[1,768,2048]{2,1,0:T(8,128)(2,1)S(1)}, bf16[1,768,2048]{2,1,0:T(8,128)(2,1)S(1)}) custom-call(bf16[32,2048]{1,0:T(8,128)(2,1)S(1)} %copy-done, bf16[32,2048]{1,0:T(8,128)(2,1)S(1)} %collective-permute-done.refs_1_, bf16[32,2048]{1,0:T(8,128)(2,1)S(1)} %collective-permute-done.1.refs_2_, ...), custom_call_target="tpu_custom_call" | custom-call | flops 8388608 | bytes 12582912 | tf_op jit(solution)/shard_map/select/pallas_call | solution.py:57
  19.6 0.9 %collective-permute-done.7.refs_3_ = bf16[32,1280]{1,0:T(8,128)(2,1)S(1)} collective-permute-done((bf16[32,1280]{1,0:T(8,128)(2,1)S(1)}, bf16[32,1280]{1,0:T(8,128)(2,1)S(1)}, u32[]{:S(2)}, u32[]{:S(2)}) %collective-permute-start.7) | collective-permute-done | bytes 81952 | tf_op jit(solution)/shard_map/ppermute | solution.py:72
  20.5 2.1 %attend.1 = (bf16[32,1024]{1,0:T(8,128)(2,1)S(1)}, bf16[32,1024]{1,0:T(8,128)(2,1)S(1)}, bf16[32,1024]{1,0:T(8,128)(2,1)S(1)}, bf16[32,1024]{1,0:T(8,128)(2,1)S(1)}) custom-call(bf16[32,1280]{1,0:T(8,128)(2,1)S(1)} %get-tuple-element.49.refs_5_.refs_0_, bf16[32,1280]{1,0:T(8,128)(2,1)S(1)} %collective-permute-done.5.refs_1_, ...), custom_call_target="tpu_custom_call" | custom-call | flops 335544320 | bytes 1310720 | tf_op jit(solution)/shard_map/attend/pallas_call | solution.py:57
  22.6 1.1 %collective-permute-start.9 = (bf16[32,1024]{1,0:T(8,128)(2,1)S(1)}, bf16[32,1024]{1,0:T(8,128)(2,1)S(1)}, u32[]{:S(2)}, u32[]{:S(2)}) collective-permute-start(bf16[32,1024]{1,0:T(8,128)(2,1)S(1)} %get-tuple-element.61), channel_id=1, source_target_pairs={{0,2},{1,3},{2,0},{3,1},{4,6},{5,7},{6,4},{7,5},{8,10},{9,11},{10,... | collective-permute-start | bytes 196616 | tf_op jit(solution)/shard_map/ppermute | solution.py:72
  23.7 0.9 %collective-permute-start.10 = (bf16[32,1024]{1,0:T(8,128)(2,1)S(1)}, bf16[32,1024]{1,0:T(8,128)(2,1)S(1)}, u32[]{:S(2)}, u32[]{:S(2)}) collective-permute-start(bf16[32,1024]{1,0:T(8,128)(2,1)S(1)} %get-tuple-element.62), channel_id=1, source_target_pairs={{0,4},{1,5},{2,6},{3,7},{4,0},{5,1},{6,2},{7,3},{8,12},{9,13},{10,... | collective-permute-start | bytes 196616 | tf_op jit(solution)/shard_map/ppermute | solution.py:72
  24.6 1.5 %collective-permute-start.11 = (bf16[32,1024]{1,0:T(8,128)(2,1)S(1)}, bf16[32,1024]{1,0:T(8,128)(2,1)S(1)}, u32[]{:S(2)}, u32[]{:S(2)}) collective-permute-start(bf16[32,1024]{1,0:T(8,128)(2,1)S(1)} %get-tuple-element.63), channel_id=1, source_target_pairs={{0,6},{1,7},{2,4},{3,5},{4,2},{5,3},{6,0},{7,1},{8,14},{9,15},{10,... | collective-permute-start | bytes 196616 | tf_op jit(solution)/shard_map/ppermute | solution.py:72
  26.1 1.9 %fetch.1.refs_7_.down_ref = bf16[1,768,2048]{2,1,0:T(8,128)(2,1)S(1)} custom-call(bf16[32,1024]{1,0:T(8,128)(2,1)S(1)} %get-tuple-element.60._.refs_0_, bf16[1,768,2048]{2,1,0:T(8,128)(2,1)} %source.1), custom_call_target="tpu_custom_call" | custom-call | bytes 6291456 | tf_op jit(solution)/shard_map/fetch/pallas_call | solution.py:57
  28.3 1.4 %collective-permute-done.11.refs_3_ = bf16[32,1024]{1,0:T(8,128)(2,1)S(1)} collective-permute-done((bf16[32,1024]{1,0:T(8,128)(2,1)S(1)}, bf16[32,1024]{1,0:T(8,128)(2,1)S(1)}, u32[]{:S(2)}, u32[]{:S(2)}) %collective-permute-start.11) | collective-permute-done | bytes 65568 | tf_op jit(solution)/shard_map/ppermute | solution.py:72
  29.8 1.1 %spread.1 = (bf16[16,2048]{1,0:T(8,128)(2,1)S(1)}, bf16[16,2048]{1,0:T(8,128)(2,1)S(1)}, bf16[16,2048]{1,0:T(8,128)(2,1)S(1)}, bf16[16,2048]{1,0:T(8,128)(2,1)S(...) custom-call(bf16[32,1024]{1,0:T(8,128)(2,1)S(1)} %get-tuple-element., ...), custom_call_target="tpu_custom_call" | custom-call | flops 805306368 | bytes 4194304 | tf_op jit(solution)/shard_map/spread/pallas_call | solution.py:57
  30.9 1.2 %collective-permute-start.15 = (bf16[16,2048]{1,0:T(8,128)(2,1)S(1)}, bf16[16,2048]{1,0:T(8,128)(2,1)S(1)}, u32[]{:S(2)}, u32[]{:S(2)}) collective-permute-start(bf16[16,2048]{1,0:T(8,128)(2,1)S(1)} %get-tuple-element.71), channel_id=1, source_target_pairs={{0,2},{1,3},{2,0},{3,1},{4,6},{5,7},{6,4},{7,5},{8,10},{9,11},{10,... | collective-permute-start | bytes 196616 | tf_op jit(solution)/shard_map/ppermute | solution.py:72
  32.1 0.9 %collective-permute-start.16 = (bf16[16,2048]{1,0:T(8,128)(2,1)S(1)}, bf16[16,2048]{1,0:T(8,128)(2,1)S(1)}, u32[]{:S(2)}, u32[]{:S(2)}) collective-permute-start(bf16[16,2048]{1,0:T(8,128)(2,1)S(1)} %get-tuple-element.72), channel_id=1, source_target_pairs={{0,4},{1,5},{2,6},{3,7},{4,0},{5,1},{6,2},{7,3},{8,12},{9,13},{10,... | collective-permute-start | bytes 196616 | tf_op jit(solution)/shard_map/ppermute | solution.py:72
  33.0 1.4 %collective-permute-start.17 = (bf16[16,2048]{1,0:T(8,128)(2,1)S(1)}, bf16[16,2048]{1,0:T(8,128)(2,1)S(1)}, u32[]{:S(2)}, u32[]{:S(2)}) collective-permute-start(bf16[16,2048]{1,0:T(8,128)(2,1)S(1)} %get-tuple-element.73), channel_id=1, source_target_pairs={{0,6},{1,7},{2,4},{3,5},{4,2},{5,3},{6,0},{7,1},{8,14},{9,15},{10,... | collective-permute-start | bytes 196616 | tf_op jit(solution)/shard_map/ppermute | solution.py:72
  34.4 1.1 %collective-permute-start.12 = (bf16[32,2048]{1,0:T(8,128)(2,1)S(1)}, bf16[32,2048]{1,0:T(8,128)(2,1)S(1)}, u32[]{:S(2)}, u32[]{:S(2)}) collective-permute-start(bf16[32,2048]{1,0:T(8,128)(2,1)S(1)} %get-tuple-element.65), channel_id=1, source_target_pairs={{0,2},{1,3},{2,0},{3,1},{4,6},{5,7},{6,4},{7,5},{8,10},{9,11},{10,... | collective-permute-start | bytes 393224 | tf_op jit(solution)/shard_map/ppermute | solution.py:72
  35.6 0.9 %collective-permute-start.13 = (bf16[32,2048]{1,0:T(8,128)(2,1)S(1)}, bf16[32,2048]{1,0:T(8,128)(2,1)S(1)}, u32[]{:S(2)}, u32[]{:S(2)}) collective-permute-start(bf16[32,2048]{1,0:T(8,128)(2,1)S(1)} %get-tuple-element.66), channel_id=1, source_target_pairs={{0,4},{1,5},{2,6},{3,7},{4,0},{5,1},{6,2},{7,3},{8,12},{9,13},{10,... | collective-permute-start | bytes 393224 | tf_op jit(solution)/shard_map/ppermute | solution.py:72
  36.5 1.4 %collective-permute-start.14 = (bf16[32,2048]{1,0:T(8,128)(2,1)S(1)}, bf16[32,2048]{1,0:T(8,128)(2,1)S(1)}, u32[]{:S(2)}, u32[]{:S(2)}) collective-permute-start(bf16[32,2048]{1,0:T(8,128)(2,1)S(1)} %get-tuple-element.67), channel_id=1, source_target_pairs={{0,6},{1,7},{2,4},{3,5},{4,2},{5,3},{6,0},{7,1},{8,14},{9,15},{10,... | collective-permute-start | bytes 393224 | tf_op jit(solution)/shard_map/ppermute | solution.py:72
  37.9 1.0 %collective-permute-done.16.refs_2_ = bf16[16,2048]{1,0:T(8,128)(2,1)S(1)} collective-permute-done((bf16[16,2048]{1,0:T(8,128)(2,1)S(1)}, bf16[16,2048]{1,0:T(8,128)(2,1)S(1)}, u32[]{:S(2)}, u32[]{:S(2)}) %collective-permute-start.16) | collective-permute-done | bytes 65568 | tf_op jit(solution)/shard_map/ppermute | solution.py:72
  39.2 1.2 %collective-permute-done.18.other_ref = bf16[8,2048]{1,0:T(8,128)(2,1)S(1)} collective-permute-done((bf16[8,2048]{1,0:T(8,128)(2,1)S(1)}, bf16[8,2048]{1,0:T(8,128)(2,1)S(1)}, u32[]{:S(2)}, u32[]{:S(2)}) %collective-permute-start.18) | collective-permute-done | bytes 32800 | tf_op jit(solution)/shard_map/ppermute | solution.py:72
  40.3 2.2 %expert.1 = (bf16[8,2048]{1,0:T(8,128)(2,1)S(1)}, bf16[8,2048]{1,0:T(8,128)(2,1)S(1)}) custom-call(bf16[8,2048]{1,0:T(8,128)(2,1)S(1)} %get-tuple-element.76.own_ref, bf16[8,2048]{1,0:T(8,128)(2,1)S(1)} %collective-permute-done.18.other_ref, bf16[1,768,2048]{2,1,0:T(8,128)(2,1)S(1)} %get-tuple-element.59.refs_9_.gate_ref, ...), custom_call_target="tpu_custom_call" | custom-call | flops 150994944 | bytes 9437184 | tf_op jit(solution)/shard_map/expert/pallas_call | solution.py:57
  42.7 1.0 %collective-permute-done.19.other_ref = bf16[8,2048]{1,0:T(8,128)(2,1)S(1)} collective-permute-done((bf16[8,2048]{1,0:T(8,128)(2,1)S(1)}, bf16[8,2048]{1,0:T(8,128)(2,1)S(1)}, u32[]{:S(2)}, u32[]{:S(2)}) %collective-permute-start.19) | collective-permute-done | bytes 32800 | tf_op jit(solution)/shard_map/ppermute | solution.py:72
  43.8 1.1 %collective-permute-start.20 = (bf16[4,2048]{1,0:T(4,128)(2,1)S(1)}, bf16[4,2048]{1,0:T(4,128)(2,1)S(1)}, u32[]{:S(2)}, u32[]{:S(2)}) collective-permute-start(bf16[4,2048]{1,0:T(4,128)(2,1)S(1)} %get-tuple-element.82), channel_id=1, source_target_pairs={{0,2},{1,3},{2,0},{3,1},{4,6},{5,7},{6,4},{7,5},{8,10},{9,11},{10,... | collective-permute-start | bytes 49160 | tf_op jit(solution)/shard_map/ppermute | solution.py:72
  44.9 0.9 %collective-permute-start.21 = (bf16[4,2048]{1,0:T(4,128)(2,1)S(1)}, bf16[4,2048]{1,0:T(4,128)(2,1)S(1)}, u32[]{:S(2)}, u32[]{:S(2)}) collective-permute-start(bf16[4,2048]{1,0:T(4,128)(2,1)S(1)} %get-tuple-element.83), channel_id=1, source_target_pairs={{0,4},{1,5},{2,6},{3,7},{4,0},{5,1},{6,2},{7,3},{8,12},{9,13},{10,... | collective-permute-start | bytes 49160 | tf_op jit(solution)/shard_map/ppermute | solution.py:72
  45.8 1.5 %collective-permute-start.22 = (bf16[4,2048]{1,0:T(4,128)(2,1)S(1)}, bf16[4,2048]{1,0:T(4,128)(2,1)S(1)}, u32[]{:S(2)}, u32[]{:S(2)}) collective-permute-start(bf16[4,2048]{1,0:T(4,128)(2,1)S(1)} %get-tuple-element.84), channel_id=1, source_target_pairs={{0,6},{1,7},{2,4},{3,5},{4,2},{5,3},{6,0},{7,1},{8,14},{9,15},{10,... | collective-permute-start | bytes 49160 | tf_op jit(solution)/shard_map/ppermute | solution.py:72
  47.6 1.1 %collective-permute-done.21.refs_5_ = bf16[4,2048]{1,0:T(4,128)(2,1)S(1)} collective-permute-done((bf16[4,2048]{1,0:T(4,128)(2,1)S(1)}, bf16[4,2048]{1,0:T(4,128)(2,1)S(1)}, u32[]{:S(2)}, u32[]{:S(2)}) %collective-permute-start.21) | collective-permute-done | bytes 16416 | tf_op jit(solution)/shard_map/ppermute | solution.py:72
  48.7 1.8 %collective-permute-done.22.refs_6_ = bf16[4,2048]{1,0:T(4,128)(2,1)S(1)} collective-permute-done((bf16[4,2048]{1,0:T(4,128)(2,1)S(1)}, bf16[4,2048]{1,0:T(4,128)(2,1)S(1)}, u32[]{:S(2)}, u32[]{:S(2)}) %collective-permute-start.22) | collective-permute-done | bytes 16416 | tf_op jit(solution)/shard_map/ppermute | solution.py:72
  50.5 1.1 %combine.1 = bf16[32,2048]{1,0:T(8,128)(2,1)} custom-call(f32[32,2048]{1,0:T(8,128)S(1)} %hidden.1.refs_0_, f32[32,16]{1,0:T(8,128)S(1)} %get-tuple-element.68.refs_1_, f32[16,128]{1,0:T(8,128)S(1)} %get-tuple-element.69.refs_2_, bf16[4,2048]{1,0:T(4,128)(2,1)S(1)} %get-tuple-element.81.refs_3_, bf16[4,2048]{1,0:T(4,128)(2,1)S(1)} %collective-permute-done.20.refs_4_, ...), custom_call_target="tpu_custom_call" | custom-call | bytes 393216 | tf_op jit(solution)/shard_map/combine/pallas_call | solution.py:57
  (27 shorter events, 2.9 us)
Async XLA Ops:
  0.0 11.4 %collective-permute-start.3 = (bf16[2048,512]{1,0:T(8,128)(2,1)}, bf16[2048,512]{1,0:T(8,128)(2,1)S(1)}, u32[]{:S(2)}, u32[]{:S(2)}) collective-permute-start(bf16[2048,512]{1,0:T(8,128)(2,1)} %refs_14_.1), channel_id=1, source_target_pairs={{0,1},{1,0},{2,3},{3,2},{4,5},{5,4},{6,7},{7,6},{8,9},{9,8},{10,11... | collective-permute-start | bytes 6291464 | tf_op jit(solution)/shard_map/ppermute | solution.py:72
  0.5 10.9 %collective-permute-start.4 = (bf16[128,2048]{1,0:T(8,128)(2,1)}, bf16[128,2048]{1,0:T(8,128)(2,1)S(1)}, u32[]{:S(2)}, u32[]{:S(2)}) collective-permute-start(bf16[128,2048]{1,0:T(8,128)(2,1)} %refs_15_.1), channel_id=1, source_target_pairs={{0,1},{1,0},{2,3},{3,2},{4,5},{5,4},{6,7},{7,6},{8,9},{9,8},{10,11... | collective-permute-start | bytes 1572872 | tf_op jit(solution)/shard_map/ppermute | solution.py:72
  0.5 9.8 %collective-permute-start.2 = (bf16[32,2048]{1,0:T(8,128)(2,1)}, bf16[32,2048]{1,0:T(8,128)(2,1)S(1)}, u32[]{:S(2)}, u32[]{:S(2)}) collective-permute-start(bf16[32,2048]{1,0:T(8,128)(2,1)} %refs_4_.2), channel_id=1, source_target_pairs={{0,6},{1,7},{2,4},{3,5},{4,2},{5,3},{6,0},{7,1},{8,14},{9,15},{10,... | collective-permute-start | bytes 393224 | tf_op jit(solution)/shard_map/ppermute | solution.py:72
  4.4 6.7 %collective-permute-start.1 = (bf16[32,2048]{1,0:T(8,128)(2,1)}, bf16[32,2048]{1,0:T(8,128)(2,1)S(1)}, u32[]{:S(2)}, u32[]{:S(2)}) collective-permute-start(bf16[32,2048]{1,0:T(8,128)(2,1)} %refs_4_.2), channel_id=1, source_target_pairs={{0,4},{1,5},{2,6},{3,7},{4,0},{5,1},{6,2},{7,3},{8,12},{9,13},{10,... | collective-permute-start | bytes 393224 | tf_op jit(solution)/shard_map/ppermute | solution.py:72
  4.9 6.4 %collective-permute-start = (bf16[32,2048]{1,0:T(8,128)(2,1)}, bf16[32,2048]{1,0:T(8,128)(2,1)S(1)}, u32[]{:S(2)}, u32[]{:S(2)}) collective-permute-start(bf16[32,2048]{1,0:T(8,128)(2,1)} %refs_4_.2), channel_id=1, source_target_pairs={{0,2},{1,3},{2,0},{3,1},{4,6},{5,7},{6,4},{7,5},{8,10},{9,11},{10,... | collective-permute-start | bytes 393224 | tf_op jit(solution)/shard_map/ppermute | solution.py:72
  6.9 4.4 %copy-start = (bf16[32,2048]{1,0:T(8,128)(2,1)S(1)}, bf16[32,2048]{1,0:T(8,128)(2,1)}, u32[]{:S(2)}) copy-start(bf16[32,2048]{1,0:T(8,128)(2,1)} %refs_4_.2) | copy-start | bytes 393220
  12.5 8.0 %collective-permute-start.8 = (bf16[512,2048]{1,0:T(8,128)(2,1)S(1)}, bf16[512,2048]{1,0:T(8,128)(2,1)S(1)}, u32[]{:S(2)}, u32[]{:S(2)}) collective-permute-start(bf16[512,2048]{1,0:T(8,128)(2,1)S(1)} %get-tuple-element.57.refs_5_), channel_id=1, source_target_pairs={{0,1},{1,0},{2,3},{3,2},{4,5},{5,4},{6,7},{7,6},{8,9},{9,8},{10,11... | collective-permute-start | bytes 6291464 | tf_op jit(solution)/shard_map/ppermute | solution.py:72
  12.6 6.4 %collective-permute-start.5 = (bf16[32,1280]{1,0:T(8,128)(2,1)S(1)}, bf16[32,1280]{1,0:T(8,128)(2,1)S(1)}, u32[]{:S(2)}, u32[]{:S(2)}) collective-permute-start(bf16[32,1280]{1,0:T(8,128)(2,1)S(1)} %get-tuple-element.50), channel_id=1, source_target_pairs={{0,2},{1,3},{2,0},{3,1},{4,6},{5,7},{6,4},{7,5},{8,10},{9,11},{10,... | collective-permute-start | bytes 245768 | tf_op jit(solution)/shard_map/ppermute | solution.py:72
  14.2 5.4 %collective-permute-start.6 = (bf16[32,1280]{1,0:T(8,128)(2,1)S(1)}, bf16[32,1280]{1,0:T(8,128)(2,1)S(1)}, u32[]{:S(2)}, u32[]{:S(2)}) collective-permute-start(bf16[32,1280]{1,0:T(8,128)(2,1)S(1)} %get-tuple-element.51), channel_id=1, source_target_pairs={{0,4},{1,5},{2,6},{3,7},{4,0},{5,1},{6,2},{7,3},{8,12},{9,13},{10,... | collective-permute-start | bytes 245768 | tf_op jit(solution)/shard_map/ppermute | solution.py:72
  15.1 5.3 %collective-permute-start.7 = (bf16[32,1280]{1,0:T(8,128)(2,1)S(1)}, bf16[32,1280]{1,0:T(8,128)(2,1)S(1)}, u32[]{:S(2)}, u32[]{:S(2)}) collective-permute-start(bf16[32,1280]{1,0:T(8,128)(2,1)S(1)} %get-tuple-element.52), channel_id=1, source_target_pairs={{0,6},{1,7},{2,4},{3,5},{4,2},{5,3},{6,0},{7,1},{8,14},{9,15},{10,... | collective-permute-start | bytes 245768 | tf_op jit(solution)/shard_map/ppermute | solution.py:72
  22.6 5.5 %collective-permute-start.9 = (bf16[32,1024]{1,0:T(8,128)(2,1)S(1)}, bf16[32,1024]{1,0:T(8,128)(2,1)S(1)}, u32[]{:S(2)}, u32[]{:S(2)}) collective-permute-start(bf16[32,1024]{1,0:T(8,128)(2,1)S(1)} %get-tuple-element.61), channel_id=1, source_target_pairs={{0,2},{1,3},{2,0},{3,1},{4,6},{5,7},{6,4},{7,5},{8,10},{9,11},{10,... | collective-permute-start | bytes 196616 | tf_op jit(solution)/shard_map/ppermute | solution.py:72
  23.7 4.7 %collective-permute-start.10 = (bf16[32,1024]{1,0:T(8,128)(2,1)S(1)}, bf16[32,1024]{1,0:T(8,128)(2,1)S(1)}, u32[]{:S(2)}, u32[]{:S(2)}) collective-permute-start(bf16[32,1024]{1,0:T(8,128)(2,1)S(1)} %get-tuple-element.62), channel_id=1, source_target_pairs={{0,4},{1,5},{2,6},{3,7},{4,0},{5,1},{6,2},{7,3},{8,12},{9,13},{10,... | collective-permute-start | bytes 196616 | tf_op jit(solution)/shard_map/ppermute | solution.py:72
  24.6 5.2 %collective-permute-start.11 = (bf16[32,1024]{1,0:T(8,128)(2,1)S(1)}, bf16[32,1024]{1,0:T(8,128)(2,1)S(1)}, u32[]{:S(2)}, u32[]{:S(2)}) collective-permute-start(bf16[32,1024]{1,0:T(8,128)(2,1)S(1)} %get-tuple-element.63), channel_id=1, source_target_pairs={{0,6},{1,7},{2,4},{3,5},{4,2},{5,3},{6,0},{7,1},{8,14},{9,15},{10,... | collective-permute-start | bytes 196616 | tf_op jit(solution)/shard_map/ppermute | solution.py:72
  30.9 5.7 %collective-permute-start.15 = (bf16[16,2048]{1,0:T(8,128)(2,1)S(1)}, bf16[16,2048]{1,0:T(8,128)(2,1)S(1)}, u32[]{:S(2)}, u32[]{:S(2)}) collective-permute-start(bf16[16,2048]{1,0:T(8,128)(2,1)S(1)} %get-tuple-element.71), channel_id=1, source_target_pairs={{0,2},{1,3},{2,0},{3,1},{4,6},{5,7},{6,4},{7,5},{8,10},{9,11},{10,... | collective-permute-start | bytes 196616 | tf_op jit(solution)/shard_map/ppermute | solution.py:72
  32.1 6.8 %collective-permute-start.16 = (bf16[16,2048]{1,0:T(8,128)(2,1)S(1)}, bf16[16,2048]{1,0:T(8,128)(2,1)S(1)}, u32[]{:S(2)}, u32[]{:S(2)}) collective-permute-start(bf16[16,2048]{1,0:T(8,128)(2,1)S(1)} %get-tuple-element.72), channel_id=1, source_target_pairs={{0,4},{1,5},{2,6},{3,7},{4,0},{5,1},{6,2},{7,3},{8,12},{9,13},{10,... | collective-permute-start | bytes 196616 | tf_op jit(solution)/shard_map/ppermute | solution.py:72
  33.0 5.9 %collective-permute-start.17 = (bf16[16,2048]{1,0:T(8,128)(2,1)S(1)}, bf16[16,2048]{1,0:T(8,128)(2,1)S(1)}, u32[]{:S(2)}, u32[]{:S(2)}) collective-permute-start(bf16[16,2048]{1,0:T(8,128)(2,1)S(1)} %get-tuple-element.73), channel_id=1, source_target_pairs={{0,6},{1,7},{2,4},{3,5},{4,2},{5,3},{6,0},{7,1},{8,14},{9,15},{10,... | collective-permute-start | bytes 196616 | tf_op jit(solution)/shard_map/ppermute | solution.py:72
  34.4 11.4 %collective-permute-start.12 = (bf16[32,2048]{1,0:T(8,128)(2,1)S(1)}, bf16[32,2048]{1,0:T(8,128)(2,1)S(1)}, u32[]{:S(2)}, u32[]{:S(2)}) collective-permute-start(bf16[32,2048]{1,0:T(8,128)(2,1)S(1)} %get-tuple-element.65), channel_id=1, source_target_pairs={{0,2},{1,3},{2,0},{3,1},{4,6},{5,7},{6,4},{7,5},{8,10},{9,11},{10,... | collective-permute-start | bytes 393224 | tf_op jit(solution)/shard_map/ppermute | solution.py:72
  35.6 11.8 %collective-permute-start.13 = (bf16[32,2048]{1,0:T(8,128)(2,1)S(1)}, bf16[32,2048]{1,0:T(8,128)(2,1)S(1)}, u32[]{:S(2)}, u32[]{:S(2)}) collective-permute-start(bf16[32,2048]{1,0:T(8,128)(2,1)S(1)} %get-tuple-element.66), channel_id=1, source_target_pairs={{0,4},{1,5},{2,6},{3,7},{4,0},{5,1},{6,2},{7,3},{8,12},{9,13},{10,... | collective-permute-start | bytes 393224 | tf_op jit(solution)/shard_map/ppermute | solution.py:72
  36.5 10.8 %collective-permute-start.14 = (bf16[32,2048]{1,0:T(8,128)(2,1)S(1)}, bf16[32,2048]{1,0:T(8,128)(2,1)S(1)}, u32[]{:S(2)}, u32[]{:S(2)}) collective-permute-start(bf16[32,2048]{1,0:T(8,128)(2,1)S(1)} %get-tuple-element.67), channel_id=1, source_target_pairs={{0,6},{1,7},{2,4},{3,5},{4,2},{5,3},{6,0},{7,1},{8,14},{9,15},{10,... | collective-permute-start | bytes 393224 | tf_op jit(solution)/shard_map/ppermute | solution.py:72
  39.1 1.3 %collective-permute-start.18 = (bf16[8,2048]{1,0:T(8,128)(2,1)S(1)}, bf16[8,2048]{1,0:T(8,128)(2,1)S(1)}, u32[]{:S(2)}, u32[]{:S(2)}) collective-permute-start(bf16[8,2048]{1,0:T(8,128)(2,1)S(1)} %get-tuple-element.77), channel_id=1, source_target_pairs={{0,1},{1,0},{2,3},{3,2},{4,5},{5,4},{6,7},{7,6},{8,9},{9,8},{10,11... | collective-permute-start | bytes 98312 | tf_op jit(solution)/shard_map/ppermute | solution.py:72
  42.5 1.2 %collective-permute-start.19 = (bf16[8,2048]{1,0:T(8,128)(2,1)S(1)}, bf16[8,2048]{1,0:T(8,128)(2,1)S(1)}, u32[]{:S(2)}, u32[]{:S(2)}) collective-permute-start(bf16[8,2048]{1,0:T(8,128)(2,1)S(1)} %get-tuple-element.80), channel_id=1, source_target_pairs={{0,1},{1,0},{2,3},{3,2},{4,5},{5,4},{6,7},{7,6},{8,9},{9,8},{10,11... | collective-permute-start | bytes 98312 | tf_op jit(solution)/shard_map/ppermute | solution.py:72
  43.8 3.8 %collective-permute-start.20 = (bf16[4,2048]{1,0:T(4,128)(2,1)S(1)}, bf16[4,2048]{1,0:T(4,128)(2,1)S(1)}, u32[]{:S(2)}, u32[]{:S(2)}) collective-permute-start(bf16[4,2048]{1,0:T(4,128)(2,1)S(1)} %get-tuple-element.82), channel_id=1, source_target_pairs={{0,2},{1,3},{2,0},{3,1},{4,6},{5,7},{6,4},{7,5},{8,10},{9,11},{10,... | collective-permute-start | bytes 49160 | tf_op jit(solution)/shard_map/ppermute | solution.py:72
  44.9 3.7 %collective-permute-start.21 = (bf16[4,2048]{1,0:T(4,128)(2,1)S(1)}, bf16[4,2048]{1,0:T(4,128)(2,1)S(1)}, u32[]{:S(2)}, u32[]{:S(2)}) collective-permute-start(bf16[4,2048]{1,0:T(4,128)(2,1)S(1)} %get-tuple-element.83), channel_id=1, source_target_pairs={{0,4},{1,5},{2,6},{3,7},{4,0},{5,1},{6,2},{7,3},{8,12},{9,13},{10,... | collective-permute-start | bytes 49160 | tf_op jit(solution)/shard_map/ppermute | solution.py:72
  45.8 4.6 %collective-permute-start.22 = (bf16[4,2048]{1,0:T(4,128)(2,1)S(1)}, bf16[4,2048]{1,0:T(4,128)(2,1)S(1)}, u32[]{:S(2)}, u32[]{:S(2)}) collective-permute-start(bf16[4,2048]{1,0:T(4,128)(2,1)S(1)} %get-tuple-element.84), channel_id=1, source_target_pairs={{0,6},{1,7},{2,4},{3,5},{4,2},{5,3},{6,0},{7,1},{8,14},{9,15},{10,... | collective-permute-start | bytes 49160 | tf_op jit(solution)/shard_map/ppermute | solution.py:72

commit v2 on v1

--- a/solution.py
+++ b/solution.py
@@ -73,25 +73,25 @@
 
 
 def exchange(blocks):
-    return [blocks[0]] + [hop(blocks[j], 2 * j) for j in range(1, len(blocks))]
+    got = [hop(blocks[j], 2 * j) for j in reversed(range(1, len(blocks)))]
+    return [blocks[0]] + got[::-1]
 
 
 def window_rows(path_len):
     return -(-(WIN + 2 * (path_len - 1) + 16) // 16) * 16
 
 
-def prep_kernel(path_len, per, n_weights, *refs):
+def prep_kernel(path_len, n_weights, *refs):
     key_cache, value_cache, prefix_ref, accepted_ref, kind_ref = refs[:5]
-    small_in = refs[5:12]
-    sources = refs[12 : 12 + n_weights]
-    refs = refs[12 + n_weights :]
-    keys_ref, values_ref, mask_ref, rot_ref, pick_ref, combine_ref, weight_ref = refs[:7]
-    targets = refs[7 : 7 + n_weights]
-    refs = refs[7 + n_weights :]
-    path_ref, parents_ref, ids_ref, gates_ref, freq_ref, q_gain_ref, k_gain_ref = refs[:7]
-    hit_ref, rank_ref, own_ref, small_sems, cache_sems, weight_sems = refs[7:]
-
-    me = lax.axis_index("tensor")
+    small_in = refs[5:10]
+    sources = refs[10 : 10 + n_weights]
+    refs = refs[10 + n_weights :]
+    keys_ref, values_ref, mask_ref, rot_ref = refs[:4]
+    targets = refs[4 : 4 + n_weights]
+    refs = refs[4 + n_weights :]
+    path_ref, parents_ref, freq_ref, q_gain_ref, k_gain_ref = refs[:5]
+    small_sems, cache_sems, weight_sems = refs[5:]
+
     new = mask_ref.shape[0]
     kv_heads, span, head = keys_ref.shape
     cache_len = key_cache.shape[1]
@@ -101,16 +101,19 @@
 
     small = [
         pltpu.make_async_copy(source, target, small_sems.at[which])
-        for which, (source, target) in enumerate(zip(small_in, refs[:7]))
+        for which, (source, target) in enumerate(zip(small_in, refs[:5]))
     ]
     for copy in small:
         copy.start()
+    copies = [
+        pltpu.make_async_copy(source, target, weight_sems.at[which])
+        for which, (source, target) in enumerate(zip(sources, targets))
+    ]
     prefix = prefix_ref[0]
     accepted = accepted_ref[0]
     total = prefix + accepted
     low = jnp.maximum(total - WIN, 0)
     start = pl.multiple_of(jnp.minimum((low // 16) * 16, cache_len - wide), 16)
-    copies = []
     for which, (cache, buf) in enumerate(((key_cache, keys_ref), (value_cache, values_ref))):
         for kv in range(kv_heads):
             cols = pl.ds(kv * head, head)
@@ -128,8 +131,6 @@
                     cache_sems.at[which, kv, 1],
                 )
             )
-    for which, (source, target) in enumerate(zip(sources, targets)):
-        copies.append(pltpu.make_async_copy(source, target, weight_sems.at[which]))
     for copy in copies:
         copy.start()
 
@@ -172,7 +173,28 @@
         gain = jnp.broadcast_to(gain_ref[...], angle.shape)
         rot_ref[2 * which] = cosine * gain
         rot_ref[2 * which + 1] = sine * pltpu.roll(gain, head // 2, 1)
-
+    for copy in copies:
+        copy.wait()
+
+
+def route_kernel(per, new, n_weights, *refs):
+    small_in = refs[1:3]
+    sources = refs[3 : 3 + n_weights]
+    refs = refs[3 + n_weights :]
+    pick_ref, combine_ref, weight_ref = refs[:3]
+    targets = refs[3 : 3 + n_weights]
+    ids_ref, gates_ref, hit_ref, rank_ref, own_ref, sems = refs[3 + n_weights :]
+    sources, targets = (*small_in, *sources), (ids_ref, gates_ref, *targets)
+    copies = [
+        pltpu.make_async_copy(source, target, sems.at[which])
+        for which, (source, target) in enumerate(zip(sources, targets))
+    ]
+    for copy in copies:
+        copy.start()
+    for copy in copies[:2]:
+        copy.wait()
+
+    me = lax.axis_index("tensor")
     all_tokens = ids_ref.shape[1]
     devices = hit_ref.shape[0]
     chips = devices // 2
@@ -219,25 +241,22 @@
         (((0,), (1,)), ((), ())),
         preferred_element_type=F32,
     )
-    for copy in copies:
+    for copy in copies[2:]:
         copy.wait()
 
 
-def project_kernel(chips, *refs):
-    blocks = refs[:chips]
-    gain_ref, wq_ref, wkv_ref, wq_sib, wkv_sib, _ = refs[chips : chips + 6]
-    outs = refs[chips + 6 : 2 * chips + 6]
-    normed = refs[-1]
+def project_kernel(count, *refs):
+    blocks = refs[:count]
+    gain_ref, wq_ref, wkv_ref, wq_sib, wkv_sib = refs[count : count + 5]
+    outs = refs[count + 5 :]
     rows = blocks[0].shape[0]
     gain = gain_ref[...]
-    for j in range(chips):
-        values = norm_rows(blocks[j][...].astype(F32)) * gain
-        normed[j * rows : (j + 1) * rows, :] = values.astype(BF16)
-    values = normed[...]
+    values = [(norm_rows(block[...].astype(F32)) * gain).astype(BF16) for block in blocks]
+    values = jnp.concatenate(values, axis=0)
 
     def put(result, at):
         result = result.astype(BF16)
-        for j in range(chips):
+        for j in range(count):
             outs[j][:, at : at + result.shape[1]] = result[j * rows : (j + 1) * rows]
 
     wide, narrow = wq_ref.shape[1], wkv_ref.shape[0]
@@ -251,7 +270,7 @@
     got = refs[:chips]
     at = chips + 1 if kv_ready else chips
     keys_ref, values_ref, mask_ref, rot_ref = refs[at : at + 4]
-    outs = refs[at + 6 : at + 6 + chips]
+    outs = refs[at + 5 : at + 5 + chips]
     fresh_ref = refs[chips] if kv_ready else refs[-1]
     me = lax.axis_index("tensor")
     chip = me // 2
@@ -291,36 +310,21 @@
             outs[j][:, h * head : (h + 1) * head] = result[h * new : (h + 1) * new]
 
 
-def spread_kernel(chips, *refs):
+def spread_kernel(chips, picks, *refs):
     got = refs[:chips]
-    pick_ref, w_ref, w_sib = refs[chips : chips + 3]
-    for_experts = refs[chips + 4 : 2 * chips + 4]
-    for_slots = refs[2 * chips + 4 : 3 * chips + 4]
-    rows_ref = refs[-1]
-    new = got[0].shape[0]
+    w_ref, w_sib = refs[chips : chips + 2]
+    outs = refs[-chips:]
     depth, width = w_ref.shape
-    each = rows_ref.shape[1]
-    heads = jnp.concatenate([got[j][...] for j in range(chips)], axis=0)
-    picked = dot(pick_ref[...].astype(BF16), heads).astype(BF16)
-    extra = each - new
-    for j in range(chips):
-        rows_ref[j, 0:new, :] = got[j][...]
-        rows_ref[j, new:each, :] = picked[j * extra : (j + 1) * extra]
-    left = rows_ref[...].reshape(chips * each, 2 * depth)
+    left = jnp.concatenate([got[j][...] for j in range(chips)], axis=0)
+    if picks:
+        left = dot(refs[chips + 2][...].astype(BF16), left).astype(BF16)
+    each = left.shape[0] // chips
     tile = min(512, width)
     for at in range(0, width, tile):
         part = dot(left[:, :depth], w_ref[:, at : at + tile])
         part = (part + dot(left[:, depth:], w_sib[:, at : at + tile])).astype(BF16)
         for j in range(chips):
-            block = part[j * each : (j + 1) * each]
-            for_slots[j][:, at : at + tile] = block[:new]
-            for_experts[j][:, at : at + tile] = block[new:]
-
-
-def fetch_kernel(_, source, target, sem):
-    copy = pltpu.make_async_copy(source, target, sem.at[0])
-    copy.start()
-    copy.wait()
+            outs[j][:, at : at + tile] = part[j * each : (j + 1) * each]
 
 
 def select_kernel(chips, *refs):
@@ -354,7 +358,7 @@
 
 def rows_kernel(chips, *refs):
     got = refs[:chips]
-    picked_ref, gain_ref, own_ref, other_ref = refs[chips:]
+    picked_ref, gain_ref, _, own_ref, other_ref = refs[chips:]
     hidden = picked_ref[...]
     for j in range(chips):
         hidden = hidden + got[j][...].astype(F32)
@@ -443,20 +447,17 @@
     freq = ROPE_BASE ** (-2.0 * np.arange(head // 2) / head)
     freq = jnp.asarray(np.concatenate([freq, freq])[None, :], F32)
     span = -(-(new + 16 + window_rows(path_len)) // 128) * 128
-    weights = [attn_gain[None, :], ffn_gain[None, :], w_query, w_keyval, w_out]
-    prepared = call(
-        functools.partial(prep_kernel, path_len, per, len(weights)),
+    weights = [attn_gain[None, :], w_query, w_keyval]
+    keys, values, mask, rot, gain, wq, wkv = call(
+        functools.partial(prep_kernel, path_len, len(weights)),
         "prep",
         [
             in_vmem((kv_heads, span, head), BF16),
             in_vmem((kv_heads, span, head), BF16),
             in_vmem((new, span), F32),
             in_vmem((4, new, head), F32),
-            in_vmem((chips * rows, tokens), F32),
-            in_vmem((new, devices * per), F32),
-            in_vmem((devices * per, 128), F32),
         ]
-        + [in_vmem(weight.shape, weight.dtype) for weight in weights],
+        + [in_vmem(w.shape, w.dtype) for w in weights],
         [
             (key_cache, hbm),
             (value_cache, hbm),
@@ -465,66 +466,63 @@
             (slot_kinds, smem),
             (accept_path, hbm),
             (parents, hbm),
-            (expert_ids.T, hbm),
-            (gate_probs.T, hbm),
             (freq, hbm),
             (query_gain[None, :], hbm),
             (key_gain[None, :], hbm),
         ]
-        + [(weight, hbm) for weight in weights],
+        + [(w, hbm) for w in weights],
         [
             pltpu.SMEM((1, path_len), jnp.int32),
             pltpu.VMEM((1, new), jnp.int32),
-            pltpu.VMEM((top, all_tokens), jnp.int32),
-            pltpu.VMEM((top, all_tokens), F32),
             pltpu.VMEM((1, head), F32),
             pltpu.VMEM((1, head), F32),
             pltpu.VMEM((1, head), F32),
-            pltpu.VMEM((devices, tokens), F32),
-            pltpu.VMEM((devices, tokens), F32),
-            pltpu.VMEM((devices * per, tokens), F32),
-            pltpu.SemaphoreType.DMA((7,)),
+            pltpu.SemaphoreType.DMA((5,)),
             pltpu.SemaphoreType.DMA((2, kv_heads, 2)),
             pltpu.SemaphoreType.DMA((len(weights),)),
         ],
         limit=16,
         moved=4 * span * kv_heads * head * 2,
     )
-    keys, values, mask, rot, pick, combine, weight, gain, ffn, wq, wkv, wo = prepared
-
-    *projected, wo = call(
-        functools.partial(project_kernel, chips),
-        "project",
-        [in_vmem((new, 2 * (q_width + new_width)), BF16)] * chips
-        + [in_vmem(wo.shape, wo.dtype)],
-        [(block, vmem) for block in blocks]
-        + [
-            (gain, vmem),
-            (wq, vmem),
-            (wkv, vmem),
-            (wq_sib, vmem),
-            (wkv_sib, vmem),
-            (wo, vmem),
+
+    def project(some):
+        return call(
+            functools.partial(project_kernel, len(some)),
+            "project",
+            [in_vmem((new, 2 * (q_width + new_width)), BF16)] * len(some),
+            [(block, vmem) for block in some]
+            + [(w, vmem) for w in (gain, wq, wkv, wq_sib, wkv_sib)],
+            limit=16,
+            flops=4 * len(some) * new * width * (q_width + new_width),
+            moved=4 * width * (q_width + new_width),
+        )
+
+    projected = project(blocks[:-1])
+    got = [projected[0]] + [hop(projected[j], 2 * j) for j in range(1, chips - 1)]
+    got.append(hop(project(blocks[-1:])[0], 2 * (chips - 1)))
+
+    weights = [ffn_gain[None, :], w_out, w_down]
+    pick, combine, weight, ffn, wo, wd = call(
+        functools.partial(route_kernel, per, new, len(weights)),
+        "route",
+        [
+            in_vmem((chips * rows, tokens), F32),
+            in_vmem((new, devices * per), F32),
+            in_vmem((devices * per, 128), F32),
+        ]
+        + [in_vmem(w.shape, w.dtype) for w in weights],
+        [(projected[0], anywhere), (expert_ids.T, hbm), (gate_probs.T, hbm)]
+        + [(w, hbm) for w in weights],
+        [
+            pltpu.VMEM((top, all_tokens), jnp.int32),
+            pltpu.VMEM((top, all_tokens), F32),
+            pltpu.VMEM((devices, tokens), F32),
+            pltpu.VMEM((devices, tokens), F32),
+            pltpu.VMEM((devices * per, tokens), F32),
+            pltpu.SemaphoreType.DMA((2 + len(weights),)),
         ],
-        [pltpu.VMEM((tokens, width), BF16)],
         limit=16,
-        same={chips + 5: chips},
-        flops=4 * tokens * width * (q_width + new_width),
-        moved=4 * width * (q_width + new_width),
-    )
-    wo_sib = hop(wo, 1)
-
-    got = exchange(projected)
-    picked, wg, wu = call(
-        functools.partial(select_kernel, chips),
-        "select",
-        [in_vmem((rows, width), F32)] + [in_vmem(w.shape, w.dtype) for w in (w_gate, w_up)],
-        [(block, vmem) for block in blocks]
-        + [(pick, vmem), (projected[0], anywhere), (w_gate, hbm), (w_up, hbm)],
-        [pltpu.SemaphoreType.DMA((2,))],
-        limit=8,
-        flops=2 * rows * width * tokens,
-        moved=8 * width * w_gate.shape[1],
+        moved=4 * width * (q_width + w_down.shape[1]),
     )
     kv_ready = []
     if new_width != head:
@@ -535,48 +533,56 @@
         pieces = jnp.stack(pieces)[lax.axis_index("tensor") ^ jnp.arange(devices)]
         pieces = pieces.transpose(1, 0, 2).reshape(new, 2 * kv_heads, head)
         kv_ready = [(pieces.transpose(1, 0, 2), vmem)]
-    attended = call(
+    *attended, wo = call(
         functools.partial(attend_kernel, chips, q_width, bool(kv_ready)),
         "attend",
-        [in_vmem((new, 2 * q_width), BF16)] * chips,
+        [in_vmem((new, 2 * q_width), BF16)] * chips + [in_vmem(wo.shape, wo.dtype)],
         [(block, vmem) for block in got]
         + kv_ready
         + [(keys, vmem), (values, vmem), (mask, vmem), (rot, vmem)]
-        + [(wo_sib, anywhere), (wg, anywhere)],
+        + [(wo, vmem)],
         [] if kv_ready else [pltpu.VMEM((devices, new, head), BF16)],
         limit=16,
+        same={chips + len(kv_ready) + 4: chips},
         flops=8 * new * chips * q_width * span,
         moved=4 * span * kv_heads * head,
     )
+    wo_sib = hop(wo, 1)
     heads = exchange(attended)
-    wd = call(
-        fetch_kernel,
-        "fetch",
-        [in_vmem(w_down.shape, w_down.dtype)],
-        [(attended[0], anywhere), (w_down, hbm)],
-        [pltpu.SemaphoreType.DMA((1,))],
+    picked, wg, wu = call(
+        functools.partial(select_kernel, chips),
+        "select",
+        [in_vmem((rows, width), F32)] + [in_vmem(w.shape, w.dtype) for w in (w_gate, w_up)],
+        [(block, vmem) for block in blocks]
+        + [(pick, vmem), (attended[0], anywhere), (w_gate, hbm), (w_up, hbm)],
+        [pltpu.SemaphoreType.DMA((2,))],
         limit=8,
-        moved=4 * width * w_gate.shape[1],
-    )[0]
-
-    partial = call(
-        functools.partial(spread_kernel, chips),
-        "spread",
-        [in_vmem((rows, width), BF16)] * chips + [in_vmem((new, width), BF16)] * chips,
-        [(block, vmem) for block in heads] + [(pick, vmem), (wo, vmem), (wo_sib, vmem), (wd, anywhere)],
-        [pltpu.VMEM((chips, new + rows, 2 * q_width), BF16)],
-        limit=16,
-        flops=4 * chips * (new + rows) * width * q_width,
-        moved=4 * q_width * width,
-    )
-    for_experts = exchange(partial[:chips])
-    for_slots = exchange(partial[chips:])
+        flops=2 * rows * width * tokens,
+        moved=8 * width * w_gate.shape[1],
+    )
+
+    def spread(name, each, more):
+        return call(
+            functools.partial(spread_kernel, chips, name == "experts"),
+            name,
+            [in_vmem((each, width), BF16)] * chips,
+            [(block, vmem) for block in heads] + [(wo, vmem), (wo_sib, vmem)] + more,
+            limit=16,
+            flops=4 * chips * each * width * q_width,
+            moved=4 * q_width * width,
+        )
+
+    partial = spread("experts", rows, [(pick, vmem), (wg, anywhere)])
+    for_experts = exchange(partial)
+    partial = spread("slots", new, [(partial[0], anywhere)])
+    for_slots = exchange(partial)
 
     own, other = call(
         functools.partial(rows_kernel, chips),
         "rows",
         [in_vmem((rows // 2, width), BF16)] * 2,
-        [(block, vmem) for block in for_experts] + [(picked, vmem), (ffn, vmem)],
+        [(block, vmem) for block in for_experts]
+        + [(picked, vmem), (ffn, vmem), (partial[0], anywhere)],
         limit=8,
         moved=2 * chips * rows * width,
     )

time: 51.7 us -> 52.8 us (1.021)
  Pallas kernels: 16 us -> 18.5 us
  waiting for transfers between devices: 10.5 us -> 8.84 us
    pallas_call x11 -> x13, Pallas kernels: 16 us -> 18.5 us  [call(): pl.pallas_call(kernel, out_shape=outs, in_specs=specs, out_specs=[pl.Bloc...]
    ppermute x23, waiting for transfers between devices: 10.5 us -> 8.84 us  [hop(): lax.ppermute(value, 'tensor', [(i, i ^ step) for i in range(devices)])]
  transfers between devices with their start and end apart: 23 -> 23, of which waited for: 12 -> 7; matrix products, arithmetic and copies ran while one was open for 0% -> 0% of each run, Pallas kernels for 20% -> 27%
where the time goes in v2:
time: 52.8 us; the launch traced here: 52.6 us
  starting transfers between devices  23.1 us (44%)
  Pallas kernels  18.5 us (35%)
  waiting for transfers between devices  8.84 us (17%)
  between operations  2.13 us (4%)
    ppermute x23, starting transfers between devices, hop(): lax.ppermute(value, 'tensor', [(i, i ^ step) for i in range(devices)])  23.1 us
    pallas_call x13, Pallas kernels, call(): pl.pallas_call(kernel, out_shape=outs, in_specs=specs, out_specs=[pl.Bloc...  18.5 us
    ppermute x23, waiting for transfers between devices, hop(): lax.ppermute(value, 'tensor', [(i, i ^ step) for i in range(devices)])  8.84 us
  transfers between devices with their start and end apart: 23, of which 7 were waited for; matrix products, arithmetic and copies ran while one was open for 0% of the time, Pallas kernels for 27%

profile of v2, /device:TPU:0, one launch (start us, length us, event | category | flops | bytes accessed | tf_op | source)
XLA Modules:
  0.0 52.6 jit_solution(46726117847891401)
XLA Ops:
  0.0 0.5 collective-permute-start.2
  0.5 3.0 %collective-permute-start.1 = (bf16[32,2048]{1,0:T(8,128)(2,1)}, bf16[32,2048]{1,0:T(8,128)(2,1)S(1)}, u32[]{:S(2)}, u32[]{:S(2)}) collective-permute-start(bf16[32,2048]{1,0:T(8,128)(2,1)} %refs_4_.4), channel_id=1, source_target_pairs={{0,4},{1,5},{2,6},{3,7},{4,0},{5,1},{6,2},{7,3},{8,12},{9,13},{10,... | collective-permute-start | bytes 393224 | tf_op jit(solution)/shard_map/ppermute | solution.py:72
  3.5 1.5 %collective-permute-start = (bf16[32,2048]{1,0:T(8,128)(2,1)}, bf16[32,2048]{1,0:T(8,128)(2,1)S(1)}, u32[]{:S(2)}, u32[]{:S(2)}) collective-permute-start(bf16[32,2048]{1,0:T(8,128)(2,1)} %refs_4_.4), channel_id=1, source_target_pairs={{0,2},{1,3},{2,0},{3,1},{4,6},{5,7},{6,4},{7,5},{8,10},{9,11},{10,... | collective-permute-start | bytes 393224 | tf_op jit(solution)/shard_map/ppermute | solution.py:72
  6.9 3.2 %prep.1 = (bf16[4,640,128]{2,1,0:T(8,128)(2,1)S(1)}, bf16[4,640,128]{2,1,0:T(8,128)(2,1)S(1)}, f32[32,640]{1,0:T(8,128)S(1)}, f32[4,32,128]{2,1,0:T(8,128)S(1)},...) custom-call(bf16[1,1024,512]{2,1,0:T(8,128)(2,1)} %refs_0_.3, ...), custom_call_target="tpu_custom_call" | custom-call | bytes 2621440 | tf_op jit(solution)/shard_map/prep/pallas_call | solution.py:57
  10.2 1.3 %project.2 = (bf16[32,1280]{1,0:T(8,128)(2,1)S(1)}, bf16[32,1280]{1,0:T(8,128)(2,1)S(1)}, bf16[32,1280]{1,0:T(8,128)(2,1)S(1)}) custom-call(bf16[32,2048]{1,0:T(8,128)(2,1)S(1)} %copy-done, bf16[32,2048]{1,0:T(8,128)(2,1)S(1)} %collective-permute-done.refs_1_, bf16[32,2048]{1,0:T(8,128)(2,1)S(1)} %collective-permute-done.1.refs_2_, ...), custom_call_target="tpu_custom_call" | custom-call | flops 503316480 | bytes 5242880 | tf_op jit(solution)/shard_map/project/pallas_call | solution.py:57
  11.5 2.0 %collective-permute-start.4 = (bf16[32,1280]{1,0:T(8,128)(2,1)S(1)}, bf16[32,1280]{1,0:T(8,128)(2,1)S(1)}, u32[]{:S(2)}, u32[]{:S(2)}) collective-permute-start(bf16[32,1280]{1,0:T(8,128)(2,1)S(1)} %get-tuple-element.49), channel_id=1, source_target_pairs={{0,2},{1,3},{2,0},{3,1},{4,6},{5,7},{6,4},{7,5},{8,10},{9,11},{10,... | collective-permute-start | bytes 245768 | tf_op jit(solution)/shard_map/ppermute | solution.py:72
  13.5 1.5 %collective-permute-start.5 = (bf16[32,1280]{1,0:T(8,128)(2,1)S(1)}, bf16[32,1280]{1,0:T(8,128)(2,1)S(1)}, u32[]{:S(2)}, u32[]{:S(2)}) collective-permute-start(bf16[32,1280]{1,0:T(8,128)(2,1)S(1)} %get-tuple-element.50), channel_id=1, source_target_pairs={{0,4},{1,5},{2,6},{3,7},{4,0},{5,1},{6,2},{7,3},{8,12},{9,13},{10,... | collective-permute-start | bytes 245768 | tf_op jit(solution)/shard_map/ppermute | solution.py:72
  15.0 1.2 %project.3 = bf16[32,1280]{1,0:T(8,128)(2,1)S(1)} custom-call(bf16[32,2048]{1,0:T(8,128)(2,1)S(1)} %collective-permute-done.6.refs_0_.refs_3_, f32[1,2048]{1,0:T(1,128)S(1)} %get-tuple-element.45.refs_3_.refs_1_, bf16[2048,512]{1,0:T(8,128)(2,1)S(1)} %get-tuple-element.46.refs_4_.refs_2_, bf16[128,2048]{1,0:T(8,128)(2,1)S(1)} %get-tuple-element.47.refs_5_.refs_3_, ...), custom_call_target="tpu_custom_call" | custom-call | flops 167772160 | bytes 5242880 | tf_op jit(solution)/shard_map/project/pallas_call | solution.py:57
  16.3 2.6 %route.1 = (f32[64,128]{1,0:T(8,128)S(1)}, f32[32,16]{1,0:T(8,128)S(1)}, f32[16,128]{1,0:T(8,128)S(1)}, f32[1,2048]{1,0:T(1,128)S(1)}, bf16[512,2048]{1,0:T(8,128)(2,1)S(1)}, /*index=5*/bf16[1,768,2048]{2,1,0:T(8,128)(2,1)S(1)}) custom-call(bf16[32,1280]{1,0:T(8,128)(2,1)S(1)} %get-tuple-element.48.refs_0_, s32[8,256]{1,0:T(8,128)} %bitcast.7, ...), custom_call_target="tpu_custom_call" | custom-call | bytes 10485760 | tf_op jit(solution)/shard_map/route/pallas_call | solution.py:57
  18.9 2.7 %collective-permute-done.7.refs_3_ = bf16[32,1280]{1,0:T(8,128)(2,1)S(1)} collective-permute-done((bf16[32,1280]{1,0:T(8,128)(2,1)S(1)}, bf16[32,1280]{1,0:T(8,128)(2,1)S(1)}, u32[]{:S(2)}, u32[]{:S(2)}) %collective-permute-start.7) | collective-permute-done | bytes 81952 | tf_op jit(solution)/shard_map/ppermute | solution.py:72
  21.6 2.1 %attend.1 = (bf16[32,1024]{1,0:T(8,128)(2,1)S(1)}, bf16[32,1024]{1,0:T(8,128)(2,1)S(1)}, bf16[32,1024]{1,0:T(8,128)(2,1)S(1)}, bf16[32,1024]{1,0:T(8,128)(2,1)S(1)}, bf16[512,2048]{1,0:T(8,128)(2,1)S(1)}) custom-call(bf16[32,1280]{1,0:T(8,128)(2,1)S(1)} %get-tuple-element.48.refs_0_, ...), custom_call_target="tpu_custom_call", output_to_operand_aliasing={{4}: (8, {})} | custom-call | flops 335544320 | bytes 1310720 | tf_op jit(solution)/shard_map/attend/pallas_call | solution.py:57
  23.8 0.6 %collective-permute-start.8 = (bf16[32,1024]{1,0:T(8,128)(2,1)S(1)}, bf16[32,1024]{1,0:T(8,128)(2,1)S(1)}, u32[]{:S(2)}, u32[]{:S(2)}) collective-permute-start(bf16[32,1024]{1,0:T(8,128)(2,1)S(1)} %get-tuple-element.57), channel_id=1, source_target_pairs={{0,2},{1,3},{2,0},{3,1},{4,6},{5,7},{6,4},{7,5},{8,10},{9,11},{10,... | collective-permute-start | bytes 196616 | tf_op jit(solution)/shard_map/ppermute | solution.py:72
  24.7 2.7 %collective-permute-start.10 = (bf16[32,1024]{1,0:T(8,128)(2,1)S(1)}, bf16[32,1024]{1,0:T(8,128)(2,1)S(1)}, u32[]{:S(2)}, u32[]{:S(2)}) collective-permute-start(bf16[32,1024]{1,0:T(8,128)(2,1)S(1)} %get-tuple-element.59), channel_id=1, source_target_pairs={{0,6},{1,7},{2,4},{3,5},{4,2},{5,3},{6,0},{7,1},{8,14},{9,15},{10,... | collective-permute-start | bytes 196616 | tf_op jit(solution)/shard_map/ppermute | solution.py:72
  27.3 2.9 %select.1 = (f32[16,2048]{1,0:T(8,128)S(1)}, bf16[1,768,2048]{2,1,0:T(8,128)(2,1)S(1)}, bf16[1,768,2048]{2,1,0:T(8,128)(2,1)S(1)}) custom-call(bf16[32,2048]{1,0:T(8,128)(2,1)S(1)} %copy-done, bf16[32,2048]{1,0:T(8,128)(2,1)S(1)} %collective-permute-done.refs_1_, bf16[32,2048]{1,0:T(8,128)(2,1)S(1)} %collective-permute-done.1.refs_2_, ...), custom_call_target="tpu_custom_call" | custom-call | flops 8388608 | bytes 12582912 | tf_op jit(solution)/shard_map/select/pallas_call | solution.py:57
  30.3 1.0 %experts.1 = (bf16[16,2048]{1,0:T(8,128)(2,1)S(1)}, bf16[16,2048]{1,0:T(8,128)(2,1)S(1)}, bf16[16,2048]{1,0:T(8,128)(2,1)S(1)}, bf16[16,2048]{1,0:T(8,128)(2,1)S(1)}) custom-call(bf16[32,1024]{1,0:T(8,128)(2,1)S(1)} %get-tuple-element.56.refs_5_.refs_0_, bf16[32,1024]{1,0:T(8,128)(2,1)S(1)} %collective-permute-done.8.refs_1_, ...), custom_call_target="tpu_custom_call" | custom-call | flops 268435456 | bytes 4194304 | tf_op jit(solution)/shard_map/experts/pallas_call | solution.py:57
  31.3 1.4 %collective-permute-start.15 = (bf16[16,2048]{1,0:T(8,128)(2,1)S(1)}, bf16[16,2048]{1,0:T(8,128)(2,1)S(1)}, u32[]{:S(2)}, u32[]{:S(2)}) collective-permute-start(bf16[16,2048]{1,0:T(8,128)(2,1)S(1)} %get-tuple-element.70), channel_id=1, source_target_pairs={{0,2},{1,3},{2,0},{3,1},{4,6},{5,7},{6,4},{7,5},{8,10},{9,11},{10,... | collective-permute-start | bytes 196616 | tf_op jit(solution)/shard_map/ppermute | solution.py:72
  32.6 1.5 %collective-permute-start.16 = (bf16[16,2048]{1,0:T(8,128)(2,1)S(1)}, bf16[16,2048]{1,0:T(8,128)(2,1)S(1)}, u32[]{:S(2)}, u32[]{:S(2)}) collective-permute-start(bf16[16,2048]{1,0:T(8,128)(2,1)S(1)} %get-tuple-element.71), channel_id=1, source_target_pairs={{0,4},{1,5},{2,6},{3,7},{4,0},{5,1},{6,2},{7,3},{8,12},{9,13},{10,... | collective-permute-start | bytes 196616 | tf_op jit(solution)/shard_map/ppermute | solution.py:72
  34.1 0.7 %collective-permute-start.17 = (bf16[16,2048]{1,0:T(8,128)(2,1)S(1)}, bf16[16,2048]{1,0:T(8,128)(2,1)S(1)}, u32[]{:S(2)}, u32[]{:S(2)}) collective-permute-start(bf16[16,2048]{1,0:T(8,128)(2,1)S(1)} %get-tuple-element.72), channel_id=1, source_target_pairs={{0,6},{1,7},{2,4},{3,5},{4,2},{5,3},{6,0},{7,1},{8,14},{9,15},{10,... | collective-permute-start | bytes 196616 | tf_op jit(solution)/shard_map/ppermute | solution.py:72
  34.8 0.7 %slots.1 = (bf16[32,2048]{1,0:T(8,128)(2,1)S(1)}, bf16[32,2048]{1,0:T(8,128)(2,1)S(1)}, bf16[32,2048]{1,0:T(8,128)(2,1)S(1)}, bf16[32,2048]{1,0:T(8,128)(2,1)S(1)}) custom-call(bf16[32,1024]{1,0:T(8,128)(2,1)S(1)} %get-tuple-element.56.refs_5_.refs_0_, bf16[32,1024]{1,0:T(8,128)(2,1)S(1)} %collective-permute-done.8.refs_1_, ...), custom_call_target="tpu_custom_call" | custom-call | flops 536870912 | bytes 4194304 | tf_op jit(solution)/shard_map/slots/pallas_call | solution.py:57
  35.5 1.4 %collective-permute-start.12 = (bf16[32,2048]{1,0:T(8,128)(2,1)S(1)}, bf16[32,2048]{1,0:T(8,128)(2,1)S(1)}, u32[]{:S(2)}, u32[]{:S(2)}) collective-permute-start(bf16[32,2048]{1,0:T(8,128)(2,1)S(1)} %get-tuple-element.65), channel_id=1, source_target_pairs={{0,2},{1,3},{2,0},{3,1},{4,6},{5,7},{6,4},{7,5},{8,10},{9,11},{10,... | collective-permute-start | bytes 393224 | tf_op jit(solution)/shard_map/ppermute | solution.py:72
  36.9 1.5 %collective-permute-start.13 = (bf16[32,2048]{1,0:T(8,128)(2,1)S(1)}, bf16[32,2048]{1,0:T(8,128)(2,1)S(1)}, u32[]{:S(2)}, u32[]{:S(2)}) collective-permute-start(bf16[32,2048]{1,0:T(8,128)(2,1)S(1)} %get-tuple-element.66), channel_id=1, source_target_pairs={{0,4},{1,5},{2,6},{3,7},{4,0},{5,1},{6,2},{7,3},{8,12},{9,13},{10,... | collective-permute-start | bytes 393224 | tf_op jit(solution)/shard_map/ppermute | solution.py:72
  38.4 0.7 %collective-permute-start.14 = (bf16[32,2048]{1,0:T(8,128)(2,1)S(1)}, bf16[32,2048]{1,0:T(8,128)(2,1)S(1)}, u32[]{:S(2)}, u32[]{:S(2)}) collective-permute-start(bf16[32,2048]{1,0:T(8,128)(2,1)S(1)} %get-tuple-element.67), channel_id=1, source_target_pairs={{0,6},{1,7},{2,4},{3,5},{4,2},{5,3},{6,0},{7,1},{8,14},{9,15},{10,... | collective-permute-start | bytes 393224 | tf_op jit(solution)/shard_map/ppermute | solution.py:72
  39.1 0.4 collective-permute-done.17.refs_3_
  39.7 1.2 %collective-permute-done.18.other_ref = bf16[8,2048]{1,0:T(8,128)(2,1)S(1)} collective-permute-done((bf16[8,2048]{1,0:T(8,128)(2,1)S(1)}, bf16[8,2048]{1,0:T(8,128)(2,1)S(1)}, u32[]{:S(2)}, u32[]{:S(2)}) %collective-permute-start.18) | collective-permute-done | bytes 32800 | tf_op jit(solution)/shard_map/ppermute | solution.py:72
  40.9 2.2 %expert.1 = (bf16[8,2048]{1,0:T(8,128)(2,1)S(1)}, bf16[8,2048]{1,0:T(8,128)(2,1)S(1)}) custom-call(bf16[8,2048]{1,0:T(8,128)(2,1)S(1)} %get-tuple-element.75.own_ref, bf16[8,2048]{1,0:T(8,128)(2,1)S(1)} %collective-permute-done.18.other_ref, bf16[1,768,2048]{2,1,0:T(8,128)(2,1)S(1)} %get-tuple-element.62.refs_7_.gate_ref, ...), custom_call_target="tpu_custom_call" | custom-call | flops 150994944 | bytes 9437184 | tf_op jit(solution)/shard_map/expert/pallas_call | solution.py:57
  43.3 1.0 %collective-permute-done.19.other_ref = bf16[8,2048]{1,0:T(8,128)(2,1)S(1)} collective-permute-done((bf16[8,2048]{1,0:T(8,128)(2,1)S(1)}, bf16[8,2048]{1,0:T(8,128)(2,1)S(1)}, u32[]{:S(2)}, u32[]{:S(2)}) %collective-permute-start.19) | collective-permute-done | bytes 32800 | tf_op jit(solution)/shard_map/ppermute | solution.py:72
  44.4 1.1 %collective-permute-start.20 = (bf16[4,2048]{1,0:T(4,128)(2,1)S(1)}, bf16[4,2048]{1,0:T(4,128)(2,1)S(1)}, u32[]{:S(2)}, u32[]{:S(2)}) collective-permute-start(bf16[4,2048]{1,0:T(4,128)(2,1)S(1)} %get-tuple-element.82), channel_id=1, source_target_pairs={{0,2},{1,3},{2,0},{3,1},{4,6},{5,7},{6,4},{7,5},{8,10},{9,11},{10,... | collective-permute-start | bytes 49160 | tf_op jit(solution)/shard_map/ppermute | solution.py:72
  45.4 1.4 %collective-permute-start.21 = (bf16[4,2048]{1,0:T(4,128)(2,1)S(1)}, bf16[4,2048]{1,0:T(4,128)(2,1)S(1)}, u32[]{:S(2)}, u32[]{:S(2)}) collective-permute-start(bf16[4,2048]{1,0:T(4,128)(2,1)S(1)} %get-tuple-element.83), channel_id=1, source_target_pairs={{0,4},{1,5},{2,6},{3,7},{4,0},{5,1},{6,2},{7,3},{8,12},{9,13},{10,... | collective-permute-start | bytes 49160 | tf_op jit(solution)/shard_map/ppermute | solution.py:72
  46.9 1.1 %collective-permute-start.22 = (bf16[4,2048]{1,0:T(4,128)(2,1)S(1)}, bf16[4,2048]{1,0:T(4,128)(2,1)S(1)}, u32[]{:S(2)}, u32[]{:S(2)}) collective-permute-start(bf16[4,2048]{1,0:T(4,128)(2,1)S(1)} %get-tuple-element.84), channel_id=1, source_target_pairs={{0,6},{1,7},{2,4},{3,5},{4,2},{5,3},{6,0},{7,1},{8,14},{9,15},{10,... | collective-permute-start | bytes 49160 | tf_op jit(solution)/shard_map/ppermute | solution.py:72
  48.2 1.0 %collective-permute-done.21.refs_5_ = bf16[4,2048]{1,0:T(4,128)(2,1)S(1)} collective-permute-done((bf16[4,2048]{1,0:T(4,128)(2,1)S(1)}, bf16[4,2048]{1,0:T(4,128)(2,1)S(1)}, u32[]{:S(2)}, u32[]{:S(2)}) %collective-permute-start.21) | collective-permute-done | bytes 16416 | tf_op jit(solution)/shard_map/ppermute | solution.py:72
  49.2 2.3 %collective-permute-done.22.refs_6_ = bf16[4,2048]{1,0:T(4,128)(2,1)S(1)} collective-permute-done((bf16[4,2048]{1,0:T(4,128)(2,1)S(1)}, bf16[4,2048]{1,0:T(4,128)(2,1)S(1)}, u32[]{:S(2)}, u32[]{:S(2)}) %collective-permute-start.22) | collective-permute-done | bytes 16416 | tf_op jit(solution)/shard_map/ppermute | solution.py:72
  51.5 1.1 %combine.1 = bf16[32,2048]{1,0:T(8,128)(2,1)} custom-call(f32[32,2048]{1,0:T(8,128)S(1)} %hidden.1.refs_0_, f32[32,16]{1,0:T(8,128)S(1)} %get-tuple-element.68.refs_1_, f32[16,128]{1,0:T(8,128)S(1)} %get-tuple-element.69.refs_2_, bf16[4,2048]{1,0:T(4,128)(2,1)S(1)} %get-tuple-element.81.refs_3_, bf16[4,2048]{1,0:T(4,128)(2,1)S(1)} %collective-permute-done.20.refs_4_, ...), custom_call_target="tpu_custom_call" | custom-call | bytes 393216 | tf_op jit(solution)/shard_map/combine/pallas_call | solution.py:57
  (29 shorter events, 1.1 us)
Async XLA Ops:
  0.0 10.2 %collective-permute-start.2 = (bf16[2048,512]{1,0:T(8,128)(2,1)}, bf16[2048,512]{1,0:T(8,128)(2,1)S(1)}, u32[]{:S(2)}, u32[]{:S(2)}) collective-permute-start(bf16[2048,512]{1,0:T(8,128)(2,1)} %refs_11_.1), channel_id=1, source_target_pairs={{0,1},{1,0},{2,3},{3,2},{4,5},{5,4},{6,7},{7,6},{8,9},{9,8},{10,11... | collective-permute-start | bytes 6291464 | tf_op jit(solution)/shard_map/ppermute | solution.py:72
  0.5 9.7 %collective-permute-start.3 = (bf16[128,2048]{1,0:T(8,128)(2,1)}, bf16[128,2048]{1,0:T(8,128)(2,1)S(1)}, u32[]{:S(2)}, u32[]{:S(2)}) collective-permute-start(bf16[128,2048]{1,0:T(8,128)(2,1)} %refs_12_.1), channel_id=1, source_target_pairs={{0,1},{1,0},{2,3},{3,2},{4,5},{5,4},{6,7},{7,6},{8,9},{9,8},{10,11... | collective-permute-start | bytes 1572872 | tf_op jit(solution)/shard_map/ppermute | solution.py:72
  0.5 9.7 %collective-permute-start.1 = (bf16[32,2048]{1,0:T(8,128)(2,1)}, bf16[32,2048]{1,0:T(8,128)(2,1)S(1)}, u32[]{:S(2)}, u32[]{:S(2)}) collective-permute-start(bf16[32,2048]{1,0:T(8,128)(2,1)} %refs_4_.4), channel_id=1, source_target_pairs={{0,4},{1,5},{2,6},{3,7},{4,0},{5,1},{6,2},{7,3},{8,12},{9,13},{10,... | collective-permute-start | bytes 393224 | tf_op jit(solution)/shard_map/ppermute | solution.py:72
  3.5 6.7 %collective-permute-start = (bf16[32,2048]{1,0:T(8,128)(2,1)}, bf16[32,2048]{1,0:T(8,128)(2,1)S(1)}, u32[]{:S(2)}, u32[]{:S(2)}) collective-permute-start(bf16[32,2048]{1,0:T(8,128)(2,1)} %refs_4_.4), channel_id=1, source_target_pairs={{0,2},{1,3},{2,0},{3,1},{4,6},{5,7},{6,4},{7,5},{8,10},{9,11},{10,... | collective-permute-start | bytes 393224 | tf_op jit(solution)/shard_map/ppermute | solution.py:72
  5.0 10.1 %collective-permute-start.6 = (bf16[32,2048]{1,0:T(8,128)(2,1)}, bf16[32,2048]{1,0:T(8,128)(2,1)S(1)}, u32[]{:S(2)}, u32[]{:S(2)}) collective-permute-start(bf16[32,2048]{1,0:T(8,128)(2,1)} %refs_4_.4), channel_id=1, source_target_pairs={{0,6},{1,7},{2,4},{3,5},{4,2},{5,3},{6,0},{7,1},{8,14},{9,15},{10,... | collective-permute-start | bytes 393224 | tf_op jit(solution)/shard_map/ppermute | solution.py:72
  6.9 3.3 %copy-start = (bf16[32,2048]{1,0:T(8,128)(2,1)S(1)}, bf16[32,2048]{1,0:T(8,128)(2,1)}, u32[]{:S(2)}) copy-start(bf16[32,2048]{1,0:T(8,128)(2,1)} %refs_4_.4) | copy-start | bytes 393220
  11.5 7.4 %collective-permute-start.4 = (bf16[32,1280]{1,0:T(8,128)(2,1)S(1)}, bf16[32,1280]{1,0:T(8,128)(2,1)S(1)}, u32[]{:S(2)}, u32[]{:S(2)}) collective-permute-start(bf16[32,1280]{1,0:T(8,128)(2,1)S(1)} %get-tuple-element.49), channel_id=1, source_target_pairs={{0,2},{1,3},{2,0},{3,1},{4,6},{5,7},{6,4},{7,5},{8,10},{9,11},{10,... | collective-permute-start | bytes 245768 | tf_op jit(solution)/shard_map/ppermute | solution.py:72
  13.5 5.4 %collective-permute-start.5 = (bf16[32,1280]{1,0:T(8,128)(2,1)S(1)}, bf16[32,1280]{1,0:T(8,128)(2,1)S(1)}, u32[]{:S(2)}, u32[]{:S(2)}) collective-permute-start(bf16[32,1280]{1,0:T(8,128)(2,1)S(1)} %get-tuple-element.50), channel_id=1, source_target_pairs={{0,4},{1,5},{2,6},{3,7},{4,0},{5,1},{6,2},{7,3},{8,12},{9,13},{10,... | collective-permute-start | bytes 245768 | tf_op jit(solution)/shard_map/ppermute | solution.py:72
  16.2 5.4 %collective-permute-start.7 = (bf16[32,1280]{1,0:T(8,128)(2,1)S(1)}, bf16[32,1280]{1,0:T(8,128)(2,1)S(1)}, u32[]{:S(2)}, u32[]{:S(2)}) collective-permute-start(bf16[32,1280]{1,0:T(8,128)(2,1)S(1)} %project.3), channel_id=1, source_target_pairs={{0,6},{1,7},{2,4},{3,5},{4,2},{5,3},{6,0},{7,1},{8,14},{9,15},{10,... | collective-permute-start | bytes 245768 | tf_op jit(solution)/shard_map/ppermute | solution.py:72
  23.7 6.5 %collective-permute-start.11 = (bf16[512,2048]{1,0:T(8,128)(2,1)S(1)}, bf16[512,2048]{1,0:T(8,128)(2,1)S(1)}, u32[]{:S(2)}, u32[]{:S(2)}) collective-permute-start(bf16[512,2048]{1,0:T(8,128)(2,1)S(1)} %get-tuple-element.60.refs_4_), channel_id=1, source_target_pairs={{0,1},{1,0},{2,3},{3,2},{4,5},{5,4},{6,7},{7,6},{8,9},{9,8},{10,11... | collective-permute-start | bytes 6291464 | tf_op jit(solution)/shard_map/ppermute | solution.py:72
  23.8 6.4 %collective-permute-start.8 = (bf16[32,1024]{1,0:T(8,128)(2,1)S(1)}, bf16[32,1024]{1,0:T(8,128)(2,1)S(1)}, u32[]{:S(2)}, u32[]{:S(2)}) collective-permute-start(bf16[32,1024]{1,0:T(8,128)(2,1)S(1)} %get-tuple-element.57), channel_id=1, source_target_pairs={{0,2},{1,3},{2,0},{3,1},{4,6},{5,7},{6,4},{7,5},{8,10},{9,11},{10,... | collective-permute-start | bytes 196616 | tf_op jit(solution)/shard_map/ppermute | solution.py:72
  24.4 5.8 %collective-permute-start.9 = (bf16[32,1024]{1,0:T(8,128)(2,1)S(1)}, bf16[32,1024]{1,0:T(8,128)(2,1)S(1)}, u32[]{:S(2)}, u32[]{:S(2)}) collective-permute-start(bf16[32,1024]{1,0:T(8,128)(2,1)S(1)} %get-tuple-element.58), channel_id=1, source_target_pairs={{0,4},{1,5},{2,6},{3,7},{4,0},{5,1},{6,2},{7,3},{8,12},{9,13},{10,... | collective-permute-start | bytes 196616 | tf_op jit(solution)/shard_map/ppermute | solution.py:72
  24.7 5.6 %collective-permute-start.10 = (bf16[32,1024]{1,0:T(8,128)(2,1)S(1)}, bf16[32,1024]{1,0:T(8,128)(2,1)S(1)}, u32[]{:S(2)}, u32[]{:S(2)}) collective-permute-start(bf16[32,1024]{1,0:T(8,128)(2,1)S(1)} %get-tuple-element.59), channel_id=1, source_target_pairs={{0,6},{1,7},{2,4},{3,5},{4,2},{5,3},{6,0},{7,1},{8,14},{9,15},{10,... | collective-permute-start | bytes 196616 | tf_op jit(solution)/shard_map/ppermute | solution.py:72
  31.3 7.2 %collective-permute-start.15 = (bf16[16,2048]{1,0:T(8,128)(2,1)S(1)}, bf16[16,2048]{1,0:T(8,128)(2,1)S(1)}, u32[]{:S(2)}, u32[]{:S(2)}) collective-permute-start(bf16[16,2048]{1,0:T(8,128)(2,1)S(1)} %get-tuple-element.70), channel_id=1, source_target_pairs={{0,2},{1,3},{2,0},{3,1},{4,6},{5,7},{6,4},{7,5},{8,10},{9,11},{10,... | collective-permute-start | bytes 196616 | tf_op jit(solution)/shard_map/ppermute | solution.py:72
  32.6 6.5 %collective-permute-start.16 = (bf16[16,2048]{1,0:T(8,128)(2,1)S(1)}, bf16[16,2048]{1,0:T(8,128)(2,1)S(1)}, u32[]{:S(2)}, u32[]{:S(2)}) collective-permute-start(bf16[16,2048]{1,0:T(8,128)(2,1)S(1)} %get-tuple-element.71), channel_id=1, source_target_pairs={{0,4},{1,5},{2,6},{3,7},{4,0},{5,1},{6,2},{7,3},{8,12},{9,13},{10,... | collective-permute-start | bytes 196616 | tf_op jit(solution)/shard_map/ppermute | solution.py:72
  34.1 5.4 %collective-permute-start.17 = (bf16[16,2048]{1,0:T(8,128)(2,1)S(1)}, bf16[16,2048]{1,0:T(8,128)(2,1)S(1)}, u32[]{:S(2)}, u32[]{:S(2)}) collective-permute-start(bf16[16,2048]{1,0:T(8,128)(2,1)S(1)} %get-tuple-element.72), channel_id=1, source_target_pairs={{0,6},{1,7},{2,4},{3,5},{4,2},{5,3},{6,0},{7,1},{8,14},{9,15},{10,... | collective-permute-start | bytes 196616 | tf_op jit(solution)/shard_map/ppermute | solution.py:72
  35.5 11.3 %collective-permute-start.12 = (bf16[32,2048]{1,0:T(8,128)(2,1)S(1)}, bf16[32,2048]{1,0:T(8,128)(2,1)S(1)}, u32[]{:S(2)}, u32[]{:S(2)}) collective-permute-start(bf16[32,2048]{1,0:T(8,128)(2,1)S(1)} %get-tuple-element.65), channel_id=1, source_target_pairs={{0,2},{1,3},{2,0},{3,1},{4,6},{5,7},{6,4},{7,5},{8,10},{9,11},{10,... | collective-permute-start | bytes 393224 | tf_op jit(solution)/shard_map/ppermute | solution.py:72
  36.9 11.0 %collective-permute-start.13 = (bf16[32,2048]{1,0:T(8,128)(2,1)S(1)}, bf16[32,2048]{1,0:T(8,128)(2,1)S(1)}, u32[]{:S(2)}, u32[]{:S(2)}) collective-permute-start(bf16[32,2048]{1,0:T(8,128)(2,1)S(1)} %get-tuple-element.66), channel_id=1, source_target_pairs={{0,4},{1,5},{2,6},{3,7},{4,0},{5,1},{6,2},{7,3},{8,12},{9,13},{10,... | collective-permute-start | bytes 393224 | tf_op jit(solution)/shard_map/ppermute | solution.py:72
  38.4 9.5 %collective-permute-start.14 = (bf16[32,2048]{1,0:T(8,128)(2,1)S(1)}, bf16[32,2048]{1,0:T(8,128)(2,1)S(1)}, u32[]{:S(2)}, u32[]{:S(2)}) collective-permute-start(bf16[32,2048]{1,0:T(8,128)(2,1)S(1)} %get-tuple-element.67), channel_id=1, source_target_pairs={{0,6},{1,7},{2,4},{3,5},{4,2},{5,3},{6,0},{7,1},{8,14},{9,15},{10,... | collective-permute-start | bytes 393224 | tf_op jit(solution)/shard_map/ppermute | solution.py:72
  39.6 1.3 %collective-permute-start.18 = (bf16[8,2048]{1,0:T(8,128)(2,1)S(1)}, bf16[8,2048]{1,0:T(8,128)(2,1)S(1)}, u32[]{:S(2)}, u32[]{:S(2)}) collective-permute-start(bf16[8,2048]{1,0:T(8,128)(2,1)S(1)} %get-tuple-element.76), channel_id=1, source_target_pairs={{0,1},{1,0},{2,3},{3,2},{4,5},{5,4},{6,7},{7,6},{8,9},{9,8},{10,11... | collective-permute-start | bytes 98312 | tf_op jit(solution)/shard_map/ppermute | solution.py:72
  43.1 1.2 %collective-permute-start.19 = (bf16[8,2048]{1,0:T(8,128)(2,1)S(1)}, bf16[8,2048]{1,0:T(8,128)(2,1)S(1)}, u32[]{:S(2)}, u32[]{:S(2)}) collective-permute-start(bf16[8,2048]{1,0:T(8,128)(2,1)S(1)} %get-tuple-element.80), channel_id=1, source_target_pairs={{0,1},{1,0},{2,3},{3,2},{4,5},{5,4},{6,7},{7,6},{8,9},{9,8},{10,11... | collective-permute-start | bytes 98312 | tf_op jit(solution)/shard_map/ppermute | solution.py:72
  44.4 3.8 %collective-permute-start.20 = (bf16[4,2048]{1,0:T(4,128)(2,1)S(1)}, bf16[4,2048]{1,0:T(4,128)(2,1)S(1)}, u32[]{:S(2)}, u32[]{:S(2)}) collective-permute-start(bf16[4,2048]{1,0:T(4,128)(2,1)S(1)} %get-tuple-element.82), channel_id=1, source_target_pairs={{0,2},{1,3},{2,0},{3,1},{4,6},{5,7},{6,4},{7,5},{8,10},{9,11},{10,... | collective-permute-start | bytes 49160 | tf_op jit(solution)/shard_map/ppermute | solution.py:72
  45.4 3.7 %collective-permute-start.21 = (bf16[4,2048]{1,0:T(4,128)(2,1)S(1)}, bf16[4,2048]{1,0:T(4,128)(2,1)S(1)}, u32[]{:S(2)}, u32[]{:S(2)}) collective-permute-start(bf16[4,2048]{1,0:T(4,128)(2,1)S(1)} %get-tuple-element.83), channel_id=1, source_target_pairs={{0,4},{1,5},{2,6},{3,7},{4,0},{5,1},{6,2},{7,3},{8,12},{9,13},{10,... | collective-permute-start | bytes 49160 | tf_op jit(solution)/shard_map/ppermute | solution.py:72
  46.9 4.6 %collective-permute-start.22 = (bf16[4,2048]{1,0:T(4,128)(2,1)S(1)}, bf16[4,2048]{1,0:T(4,128)(2,1)S(1)}, u32[]{:S(2)}, u32[]{:S(2)}) collective-permute-start(bf16[4,2048]{1,0:T(4,128)(2,1)S(1)} %get-tuple-element.84), channel_id=1, source_target_pairs={{0,6},{1,7},{2,4},{3,5},{4,2},{5,3},{6,0},{7,1},{8,14},{9,15},{10,... | collective-permute-start | bytes 49160 | tf_op jit(solution)/shard_map/ppermute | solution.py:72

commit v3 on v2

--- a/solution.py
+++ b/solution.py
@@ -20,6 +20,10 @@
 F32 = jnp.float32
 BF16 = jnp.bfloat16
 MIB = 1 << 20
+
+
+def step(j):
+    return 2 * j + bin(j).count("1") % 2
 
 
 def iota(shape, dim):
@@ -73,8 +77,7 @@
 
 
 def exchange(blocks):
-    got = [hop(blocks[j], 2 * j) for j in reversed(range(1, len(blocks)))]
-    return [blocks[0]] + got[::-1]
+    return [blocks[0]] + [hop(blocks[j], step(j)) for j in range(1, len(blocks))]
 
 
 def window_rows(path_len):
@@ -200,7 +203,10 @@
     chips = devices // 2
     tokens = chips * new
     slot = iota((all_tokens, tokens), 1) // new
-    source = (me ^ (2 * slot)) * new + iota((all_tokens, tokens), 1) % new
+    odd = slot
+    for shift in (4, 2, 1):
+        odd = odd ^ (odd >> shift)
+    source = (me ^ (2 * slot + (odd & 1))) * new + iota((all_tokens, tokens), 1) % new
     order = (iota((all_tokens, tokens), 0) == source).astype(F32)
     ids = dot(ids_ref[...].astype(F32).astype(BF16), order.astype(BF16))
     gates = lax.dot_general(
@@ -211,7 +217,8 @@
         preferred_element_type=F32,
     )
     for rel in range(devices):
-        named = (ids == (me ^ rel).astype(F32)).astype(F32)
+        expert = (me ^ step(rel // 2) ^ (rel % 2)).astype(F32)
+        named = (ids == expert).astype(F32)
         hit_ref[rel : rel + 1, :] = jnp.max(named, axis=0, keepdims=True)
     before, later = iota((tokens, tokens), 0), iota((tokens, tokens), 1)
     earlier = (before < later) & (before // new == later // new)
@@ -226,14 +233,16 @@
         rank = rank_ref[rel : rel + 1, :]
         chosen = (slot_of == (row_slot ^ (rel // 2))) & hit & (rank == row_rank)
         pick_ref[rel * rows : (rel + 1) * rows, :] = chosen.astype(F32)
-        named = ids == (me ^ rel).astype(F32)
-        weight = jnp.sum(jnp.where(named, gates, 0.0), axis=0, keepdims=True)
+        if rel < 2:
+            named = ids == (me ^ rel).astype(F32)
+            weight = jnp.sum(jnp.where(named, gates, 0.0), axis=0, keepdims=True)
+            weight = jnp.sum(jnp.where(chosen, weight, 0.0), axis=1, keepdims=True)
+            weight_ref[rel * rows : (rel + 1) * rows, :] = jnp.broadcast_to(
+                weight, (rows, weight_ref.shape[1])
+            )
         for place in range(per):
             at = rel * per + place
-            own = in_first & hit & (rank == float(place))
-            own_ref[at : at + 1, :] = own.astype(F32)
-            one = jnp.sum(jnp.where(own, weight, 0.0), axis=1, keepdims=True)
-            weight_ref[at : at + 1, :] = jnp.broadcast_to(one, (1, weight_ref.shape[1]))
+            own_ref[at : at + 1, :] = (in_first & hit & (rank == float(place))).astype(F32)
     first = (iota((tokens, new), 0) == iota((tokens, new), 1)).astype(F32)
     combine_ref[...] = lax.dot_general(
         first.astype(BF16),
@@ -282,7 +291,7 @@
     if not kv_ready:
         for rel in range(2 * chips):
             left = 2 * q_width + (rel % 2) * head
-            fresh_ref[rel] = got[rel // 2][:, left : left + head]
+            fresh_ref[step(rel // 2) ^ (rel % 2)] = got[rel // 2][:, left : left + head]
 
     def rope(values, which):
         values = norm_rows(values.astype(F32))
@@ -376,29 +385,25 @@
     inner = (gate / (1.0 + jnp.exp(-gate)) * up).astype(BF16)
     result = dot(inner, down_ref[0])
     half = own_ref.shape[0]
-    own_out[...] = result[:half].astype(BF16)
+    own_out[...] = result[:half]
     other_out[...] = result[half:].astype(BF16)
 
 
-def pack_kernel(chips, per, own_ref, other_ref, *outs):
-    own, other = own_ref[...].astype(F32), other_ref[...].astype(F32)
+def pack_kernel(chips, per, own_ref, other_ref, weight_ref, *outs):
+    half = own_ref.shape[0]
+    own = own_ref[...] * weight_ref[:half, 0:1]
+    other = other_ref[...].astype(F32) * weight_ref[half:, 0:1]
     for j in range(chips):
         at = slice(j * per, (j + 1) * per)
         outs[j][...] = jnp.concatenate([own[at], other[at]], axis=0).astype(BF16)
 
 
 def combine_kernel(chips, *refs):
-    hidden_ref, combine_ref, weight_ref = refs[:3]
-    got = refs[3 : 3 + chips]
-    out_ref = refs[3 + chips]
+    hidden_ref, combine_ref = refs[:2]
+    got = refs[2 : 2 + chips]
+    out_ref = refs[2 + chips]
     rows = jnp.concatenate([block[...].astype(F32) for block in got], axis=0)
-    moe = lax.dot_general(
-        combine_ref[...],
-        rows * weight_ref[:, 0:1],
-        (((1,), (0,)), ((), ())),
-        precision=lax.Precision.HIGHEST,
-        preferred_element_type=F32,
-    )
+    moe = dot(combine_ref[...].astype(BF16), rows.astype(BF16))
     out_ref[...] = (hidden_ref[...] + moe).astype(BF16)
 
 
@@ -485,21 +490,17 @@
         moved=4 * span * kv_heads * head * 2,
     )
 
-    def project(some):
-        return call(
-            functools.partial(project_kernel, len(some)),
-            "project",
-            [in_vmem((new, 2 * (q_width + new_width)), BF16)] * len(some),
-            [(block, vmem) for block in some]
-            + [(w, vmem) for w in (gain, wq, wkv, wq_sib, wkv_sib)],
-            limit=16,
-            flops=4 * len(some) * new * width * (q_width + new_width),
-            moved=4 * width * (q_width + new_width),
-        )
-
-    projected = project(blocks[:-1])
-    got = [projected[0]] + [hop(projected[j], 2 * j) for j in range(1, chips - 1)]
-    got.append(hop(project(blocks[-1:])[0], 2 * (chips - 1)))
+    projected = call(
+        functools.partial(project_kernel, chips),
+        "project",
+        [in_vmem((new, 2 * (q_width + new_width)), BF16)] * chips,
+        [(block, vmem) for block in blocks]
+        + [(w, vmem) for w in (gain, wq, wkv, wq_sib, wkv_sib)],
+        limit=16,
+        flops=4 * tokens * width * (q_width + new_width),
+        moved=4 * width * (q_width + new_width),
+    )
+    got = exchange(projected)
 
     weights = [ffn_gain[None, :], w_out, w_down]
     pick, combine, weight, ffn, wo, wd = call(
@@ -508,7 +509,7 @@
         [
             in_vmem((chips * rows, tokens), F32),
             in_vmem((new, devices * per), F32),
-            in_vmem((devices * per, 128), F32),
+            in_vmem((rows, 128), F32),
         ]
         + [in_vmem(w.shape, w.dtype) for w in weights],
         [(projected[0], anywhere), (expert_ids.T, hbm), (gate_probs.T, hbm)]
@@ -526,10 +527,10 @@
     )
     kv_ready = []
     if new_width != head:
-        pieces = [
-            got[rel // 2][:, 2 * q_width + (rel % 2) * new_width :][:, :new_width]
-            for rel in range(devices)
-        ]
+        pieces = [None] * devices
+        for rel in range(devices):
+            left = 2 * q_width + (rel % 2) * new_width
+            pieces[step(rel // 2) ^ (rel % 2)] = got[rel // 2][:, left : left + new_width]
         pieces = jnp.stack(pieces)[lax.axis_index("tensor") ^ jnp.arange(devices)]
         pieces = pieces.transpose(1, 0, 2).reshape(new, 2 * kv_heads, head)
         kv_ready = [(pieces.transpose(1, 0, 2), vmem)]
@@ -589,7 +590,7 @@
     own_out, other_out = call(
         expert_kernel,
         "expert",
-        [in_vmem((rows // 2, width), BF16)] * 2,
+        [in_vmem((rows // 2, width), F32), in_vmem((rows // 2, width), BF16)],
         [(own, vmem), (hop(other, 1), vmem), (wg, vmem), (wu, vmem), (wd, vmem)],
         limit=16,
         flops=6 * rows * width * w_gate.shape[1],
@@ -599,7 +600,7 @@
         functools.partial(pack_kernel, chips, per),
         "pack",
         [in_vmem((2 * per, width), BF16)] * chips,
-        [(own_out, vmem), (hop(other_out, 1), vmem)],
+        [(own_out, vmem), (hop(other_out, 1), vmem), (weight, vmem)],
         limit=8,
         moved=4 * rows * width,
     )
@@ -616,8 +617,7 @@
         functools.partial(combine_kernel, chips),
         "combine",
         [jax.ShapeDtypeStruct((new, width), BF16)],
-        [(hidden, vmem), (combine, vmem), (weight, vmem)]
-        + [(block, vmem) for block in returned],
+        [(hidden, vmem), (combine, vmem)] + [(block, vmem) for block in returned],
         limit=8,
         moved=6 * new * width,
     )[0]

time: 52.8 us -> 50.1 us (0.949)
  starting transfers between devices: 23.1 us -> 21.4 us
  Pallas kernels: 18.5 us -> 17 us
  waiting for transfers between devices: 8.84 us -> 9.43 us
    ppermute x23, starting transfers between devices: 23.1 us -> 21.4 us  [hop(): lax.ppermute(value, 'tensor', [(i, i ^ step) for i in range(devices)])]
    pallas_call x13 -> x12, Pallas kernels: 18.5 us -> 17 us  [call(): pl.pallas_call(kernel, out_shape=outs, in_specs=specs, out_specs=[pl.Bloc...]
    ppermute x23, waiting for transfers between devices: 8.84 us -> 9.43 us  [hop(): lax.ppermute(value, 'tensor', [(i, i ^ step) for i in range(devices)])]
  transfers between devices with their start and end apart: 23 -> 23, of which waited for: 7 -> 7; matrix products, arithmetic and copies ran while one was open for 0% -> 0% of each run, Pallas kernels for 27% -> 24%
where the time goes in v3:
time: 50.1 us; the launch traced here: 49.9 us
  starting transfers between devices  21.4 us (43%)
  Pallas kernels  17 us (34%)
  waiting for transfers between devices  9.43 us (19%)
  between operations  2.11 us (4%)
    ppermute x23, starting transfers between devices, hop(): lax.ppermute(value, 'tensor', [(i, i ^ step) for i in range(devices)])  21.4 us
    pallas_call x12, Pallas kernels, call(): pl.pallas_call(kernel, out_shape=outs, in_specs=specs, out_specs=[pl.Bloc...  17 us
    ppermute x23, waiting for transfers between devices, hop(): lax.ppermute(value, 'tensor', [(i, i ^ step) for i in range(devices)])  9.43 us
  transfers between devices with their start and end apart: 23, of which 7 were waited for; matrix products, arithmetic and copies ran while one was open for 0% of the time, Pallas kernels for 24%

profile of v3, /device:TPU:0, one launch (start us, length us, event | category | flops | bytes accessed | tf_op | source)
XLA Modules:
  0.0 49.9 jit_solution(15381577904977149026)
XLA Ops:
  0.0 0.5 collective-permute-start.3
  0.5 3.9 %collective-permute-start.2 = (bf16[32,2048]{1,0:T(8,128)(2,1)}, bf16[32,2048]{1,0:T(8,128)(2,1)S(1)}, u32[]{:S(2)}, u32[]{:S(2)}) collective-permute-start(bf16[32,2048]{1,0:T(8,128)(2,1)} %refs_4_.4), channel_id=1, source_target_pairs={{0,6},{1,7},{2,4},{3,5},{4,2},{5,3},{6,0},{7,1},{8,14},{9,15},{10,... | collective-permute-start | bytes 393224 | tf_op jit(solution)/shard_map/ppermute | solution.py:76
  6.6 3.2 %prep.1 = (bf16[4,640,128]{2,1,0:T(8,128)(2,1)S(1)}, bf16[4,640,128]{2,1,0:T(8,128)(2,1)S(1)}, f32[32,640]{1,0:T(8,128)S(1)}, f32[4,32,128]{2,1,0:T(8,128)S(1)},...) custom-call(bf16[1,1024,512]{2,1,0:T(8,128)(2,1)} %refs_0_.3, ...), custom_call_target="tpu_custom_call" | custom-call | bytes 2621440 | tf_op jit(solution)/shard_map/prep/pallas_call | solution.py:61
  9.9 1.2 %collective-permute-done.1.refs_2_ = bf16[32,2048]{1,0:T(8,128)(2,1)S(1)} collective-permute-done((bf16[32,2048]{1,0:T(8,128)(2,1)}, bf16[32,2048]{1,0:T(8,128)(2,1)S(1)}, u32[]{:S(2)}, u32[]{:S(2)}) %collective-permute-start.1) | collective-permute-done | bytes 131104 | tf_op jit(solution)/shard_map/ppermute | solution.py:76
  11.1 1.1 %project.1 = (bf16[32,1280]{1,0:T(8,128)(2,1)S(1)}, bf16[32,1280]{1,0:T(8,128)(2,1)S(1)}, bf16[32,1280]{1,0:T(8,128)(2,1)S(1)}, bf16[32,1280]{1,0:T(8,128)(2,1)S(1)}) custom-call(bf16[32,2048]{1,0:T(8,128)(2,1)S(1)} %copy-done, bf16[32,2048]{1,0:T(8,128)(2,1)S(1)} %collective-permute-done.refs_1_, bf16[32,2048]{1,0:T(8,128)(2,1)S(1)} %collective-permute-done.1.refs_2_, ...), custom_call_target="tpu_custom_call" | custom-call | flops 671088640 | bytes 5242880 | tf_op jit(solution)/shard_map/project/pallas_call | solution.py:61
  12.3 1.5 %collective-permute-start.5 = (bf16[32,1280]{1,0:T(8,128)(2,1)S(1)}, bf16[32,1280]{1,0:T(8,128)(2,1)S(1)}, u32[]{:S(2)}, u32[]{:S(2)}) collective-permute-start(bf16[32,1280]{1,0:T(8,128)(2,1)S(1)} %get-tuple-element.50), channel_id=1, source_target_pairs={{0,3},{1,2},{2,1},{3,0},{4,7},{5,6},{6,5},{7,4},{8,11},{9,10},{10,... | collective-permute-start | bytes 245768 | tf_op jit(solution)/shard_map/ppermute | solution.py:76
  13.7 0.6 %collective-permute-start.6 = (bf16[32,1280]{1,0:T(8,128)(2,1)S(1)}, bf16[32,1280]{1,0:T(8,128)(2,1)S(1)}, u32[]{:S(2)}, u32[]{:S(2)}) collective-permute-start(bf16[32,1280]{1,0:T(8,128)(2,1)S(1)} %get-tuple-element.51), channel_id=1, source_target_pairs={{0,5},{1,4},{2,7},{3,6},{4,1},{5,0},{6,3},{7,2},{8,13},{9,12},{10,... | collective-permute-start | bytes 245768 | tf_op jit(solution)/shard_map/ppermute | solution.py:76
  14.4 1.2 %collective-permute-start.7 = (bf16[32,1280]{1,0:T(8,128)(2,1)S(1)}, bf16[32,1280]{1,0:T(8,128)(2,1)S(1)}, u32[]{:S(2)}, u32[]{:S(2)}) collective-permute-start(bf16[32,1280]{1,0:T(8,128)(2,1)S(1)} %get-tuple-element.52), channel_id=1, source_target_pairs={{0,6},{1,7},{2,4},{3,5},{4,2},{5,3},{6,0},{7,1},{8,14},{9,15},{10,... | collective-permute-start | bytes 245768 | tf_op jit(solution)/shard_map/ppermute | solution.py:76
  15.5 2.6 %route.1 = (f32[64,128]{1,0:T(8,128)S(1)}, f32[32,16]{1,0:T(8,128)S(1)}, f32[16,128]{1,0:T(8,128)S(1)}, f32[1,2048]{1,0:T(1,128)S(1)}, bf16[512,2048]{1,0:T(8,128)(2,1)S(1)}, /*index=5*/bf16[1,768,2048]{2,1,0:T(8,128)(2,1)S(1)}) custom-call(bf16[32,1280]{1,0:T(8,128)(2,1)S(1)} %get-tuple-element.49.refs_0_, s32[8,256]{1,0:T(8,128)} %bitcast.7, ...), custom_call_target="tpu_custom_call" | custom-call | bytes 10485760 | tf_op jit(solution)/shard_map/route/pallas_call | solution.py:61
  18.2 1.9 %collective-permute-done.7.refs_3_ = bf16[32,1280]{1,0:T(8,128)(2,1)S(1)} collective-permute-done((bf16[32,1280]{1,0:T(8,128)(2,1)S(1)}, bf16[32,1280]{1,0:T(8,128)(2,1)S(1)}, u32[]{:S(2)}, u32[]{:S(2)}) %collective-permute-start.7) | collective-permute-done | bytes 81952 | tf_op jit(solution)/shard_map/ppermute | solution.py:76
  20.1 2.1 %attend.1 = (bf16[32,1024]{1,0:T(8,128)(2,1)S(1)}, bf16[32,1024]{1,0:T(8,128)(2,1)S(1)}, bf16[32,1024]{1,0:T(8,128)(2,1)S(1)}, bf16[32,1024]{1,0:T(8,128)(2,1)S(1)}, bf16[512,2048]{1,0:T(8,128)(2,1)S(1)}) custom-call(bf16[32,1280]{1,0:T(8,128)(2,1)S(1)} %get-tuple-element.49.refs_0_, ...), custom_call_target="tpu_custom_call", output_to_operand_aliasing={{4}: (8, {})} | custom-call | flops 335544320 | bytes 1310720 | tf_op jit(solution)/shard_map/attend/pallas_call | solution.py:61
  22.3 1.2 %collective-permute-start.8 = (bf16[32,1024]{1,0:T(8,128)(2,1)S(1)}, bf16[32,1024]{1,0:T(8,128)(2,1)S(1)}, u32[]{:S(2)}, u32[]{:S(2)}) collective-permute-start(bf16[32,1024]{1,0:T(8,128)(2,1)S(1)} %get-tuple-element.59), channel_id=1, source_target_pairs={{0,3},{1,2},{2,1},{3,0},{4,7},{5,6},{6,5},{7,4},{8,11},{9,10},{10,... | collective-permute-start | bytes 196616 | tf_op jit(solution)/shard_map/ppermute | solution.py:76
  23.5 0.6 %collective-permute-start.9 = (bf16[32,1024]{1,0:T(8,128)(2,1)S(1)}, bf16[32,1024]{1,0:T(8,128)(2,1)S(1)}, u32[]{:S(2)}, u32[]{:S(2)}) collective-permute-start(bf16[32,1024]{1,0:T(8,128)(2,1)S(1)} %get-tuple-element.60), channel_id=1, source_target_pairs={{0,5},{1,4},{2,7},{3,6},{4,1},{5,0},{6,3},{7,2},{8,13},{9,12},{10,... | collective-permute-start | bytes 196616 | tf_op jit(solution)/shard_map/ppermute | solution.py:76
  24.0 1.5 %collective-permute-start.10 = (bf16[32,1024]{1,0:T(8,128)(2,1)S(1)}, bf16[32,1024]{1,0:T(8,128)(2,1)S(1)}, u32[]{:S(2)}, u32[]{:S(2)}) collective-permute-start(bf16[32,1024]{1,0:T(8,128)(2,1)S(1)} %get-tuple-element.61), channel_id=1, source_target_pairs={{0,6},{1,7},{2,4},{3,5},{4,2},{5,3},{6,0},{7,1},{8,14},{9,15},{10,... | collective-permute-start | bytes 196616 | tf_op jit(solution)/shard_map/ppermute | solution.py:76
  25.5 2.9 %select.1 = (f32[16,2048]{1,0:T(8,128)S(1)}, bf16[1,768,2048]{2,1,0:T(8,128)(2,1)S(1)}, bf16[1,768,2048]{2,1,0:T(8,128)(2,1)S(1)}) custom-call(bf16[32,2048]{1,0:T(8,128)(2,1)S(1)} %copy-done, bf16[32,2048]{1,0:T(8,128)(2,1)S(1)} %collective-permute-done.refs_1_, bf16[32,2048]{1,0:T(8,128)(2,1)S(1)} %collective-permute-done.1.refs_2_, ...), custom_call_target="tpu_custom_call" | custom-call | flops 8388608 | bytes 12582912 | tf_op jit(solution)/shard_map/select/pallas_call | solution.py:61
  28.4 1.0 %collective-permute-done.10.refs_3_ = bf16[32,1024]{1,0:T(8,128)(2,1)S(1)} collective-permute-done((bf16[32,1024]{1,0:T(8,128)(2,1)S(1)}, bf16[32,1024]{1,0:T(8,128)(2,1)S(1)}, u32[]{:S(2)}, u32[]{:S(2)}) %collective-permute-start.10) | collective-permute-done | bytes 65568 | tf_op jit(solution)/shard_map/ppermute | solution.py:76
  29.4 1.0 %experts.1 = (bf16[16,2048]{1,0:T(8,128)(2,1)S(1)}, bf16[16,2048]{1,0:T(8,128)(2,1)S(1)}, bf16[16,2048]{1,0:T(8,128)(2,1)S(1)}, bf16[16,2048]{1,0:T(8,128)(2,1)S(1)}) custom-call(bf16[32,1024]{1,0:T(8,128)(2,1)S(1)} %get-tuple-element.58.refs_5_.refs_0_, bf16[32,1024]{1,0:T(8,128)(2,1)S(1)} %collective-permute-done.8.refs_1_, ...), custom_call_target="tpu_custom_call" | custom-call | flops 268435456 | bytes 4194304 | tf_op jit(solution)/shard_map/experts/pallas_call | solution.py:61
  30.4 0.4 collective-permute-start.15
  30.8 1.4 %collective-permute-start.16 = (bf16[16,2048]{1,0:T(8,128)(2,1)S(1)}, bf16[16,2048]{1,0:T(8,128)(2,1)S(1)}, u32[]{:S(2)}, u32[]{:S(2)}) collective-permute-start(bf16[16,2048]{1,0:T(8,128)(2,1)S(1)} %get-tuple-element.72), channel_id=1, source_target_pairs={{0,5},{1,4},{2,7},{3,6},{4,1},{5,0},{6,3},{7,2},{8,13},{9,12},{10,... | collective-permute-start | bytes 196616 | tf_op jit(solution)/shard_map/ppermute | solution.py:76
  32.2 1.4 %collective-permute-start.17 = (bf16[16,2048]{1,0:T(8,128)(2,1)S(1)}, bf16[16,2048]{1,0:T(8,128)(2,1)S(1)}, u32[]{:S(2)}, u32[]{:S(2)}) collective-permute-start(bf16[16,2048]{1,0:T(8,128)(2,1)S(1)} %get-tuple-element.73), channel_id=1, source_target_pairs={{0,6},{1,7},{2,4},{3,5},{4,2},{5,3},{6,0},{7,1},{8,14},{9,15},{10,... | collective-permute-start | bytes 196616 | tf_op jit(solution)/shard_map/ppermute | solution.py:76
  33.7 0.7 %slots.1 = (bf16[32,2048]{1,0:T(8,128)(2,1)S(1)}, bf16[32,2048]{1,0:T(8,128)(2,1)S(1)}, bf16[32,2048]{1,0:T(8,128)(2,1)S(1)}, bf16[32,2048]{1,0:T(8,128)(2,1)S(1)}) custom-call(bf16[32,1024]{1,0:T(8,128)(2,1)S(1)} %get-tuple-element.58.refs_5_.refs_0_, bf16[32,1024]{1,0:T(8,128)(2,1)S(1)} %collective-permute-done.8.refs_1_, ...), custom_call_target="tpu_custom_call" | custom-call | flops 536870912 | bytes 4194304 | tf_op jit(solution)/shard_map/slots/pallas_call | solution.py:61
  34.5 1.7 %collective-permute-start.13 = (bf16[32,2048]{1,0:T(8,128)(2,1)S(1)}, bf16[32,2048]{1,0:T(8,128)(2,1)S(1)}, u32[]{:S(2)}, u32[]{:S(2)}) collective-permute-start(bf16[32,2048]{1,0:T(8,128)(2,1)S(1)} %get-tuple-element.68), channel_id=1, source_target_pairs={{0,5},{1,4},{2,7},{3,6},{4,1},{5,0},{6,3},{7,2},{8,13},{9,12},{10,... | collective-permute-start | bytes 393224 | tf_op jit(solution)/shard_map/ppermute | solution.py:76
  36.2 1.4 %collective-permute-start.14 = (bf16[32,2048]{1,0:T(8,128)(2,1)S(1)}, bf16[32,2048]{1,0:T(8,128)(2,1)S(1)}, u32[]{:S(2)}, u32[]{:S(2)}) collective-permute-start(bf16[32,2048]{1,0:T(8,128)(2,1)S(1)} %get-tuple-element.69), channel_id=1, source_target_pairs={{0,6},{1,7},{2,4},{3,5},{4,2},{5,3},{6,0},{7,1},{8,14},{9,15},{10,... | collective-permute-start | bytes 393224 | tf_op jit(solution)/shard_map/ppermute | solution.py:76
  37.9 1.2 %collective-permute-done.18.other_ref = bf16[8,2048]{1,0:T(8,128)(2,1)S(1)} collective-permute-done((bf16[8,2048]{1,0:T(8,128)(2,1)S(1)}, bf16[8,2048]{1,0:T(8,128)(2,1)S(1)}, u32[]{:S(2)}, u32[]{:S(2)}) %collective-permute-start.18) | collective-permute-done | bytes 32800 | tf_op jit(solution)/shard_map/ppermute | solution.py:76
  39.1 2.2 %expert.1 = (f32[8,2048]{1,0:T(8,128)S(1)}, bf16[8,2048]{1,0:T(8,128)(2,1)S(1)}) custom-call(bf16[8,2048]{1,0:T(8,128)(2,1)S(1)} %get-tuple-element.76.own_ref, bf16[8,2048]{1,0:T(8,128)(2,1)S(1)} %collective-permute-done.18.other_ref, bf16[1,768,2048]{2,1,0:T(8,128)(2,1)S(1)} %get-tuple-element.64.refs_7_.gate_ref, ...), custom_call_target="tpu_custom_call" | custom-call | flops 150994944 | bytes 9437184 | tf_op jit(solution)/shard_map/expert/pallas_call | solution.py:61
  41.4 1.0 %collective-permute-done.19.other_ref = bf16[8,2048]{1,0:T(8,128)(2,1)S(1)} collective-permute-done((bf16[8,2048]{1,0:T(8,128)(2,1)S(1)}, bf16[8,2048]{1,0:T(8,128)(2,1)S(1)}, u32[]{:S(2)}, u32[]{:S(2)}) %collective-permute-start.19) | collective-permute-done | bytes 32800 | tf_op jit(solution)/shard_map/ppermute | solution.py:76
  42.6 0.9 %collective-permute-start.20 = (bf16[4,2048]{1,0:T(4,128)(2,1)S(1)}, bf16[4,2048]{1,0:T(4,128)(2,1)S(1)}, u32[]{:S(2)}, u32[]{:S(2)}) collective-permute-start(bf16[4,2048]{1,0:T(4,128)(2,1)S(1)} %get-tuple-element.84), channel_id=1, source_target_pairs={{0,3},{1,2},{2,1},{3,0},{4,7},{5,6},{6,5},{7,4},{8,11},{9,10},{10,... | collective-permute-start | bytes 49160 | tf_op jit(solution)/shard_map/ppermute | solution.py:76
  43.5 0.9 %collective-permute-start.21 = (bf16[4,2048]{1,0:T(4,128)(2,1)S(1)}, bf16[4,2048]{1,0:T(4,128)(2,1)S(1)}, u32[]{:S(2)}, u32[]{:S(2)}) collective-permute-start(bf16[4,2048]{1,0:T(4,128)(2,1)S(1)} %get-tuple-element.85), channel_id=1, source_target_pairs={{0,5},{1,4},{2,7},{3,6},{4,1},{5,0},{6,3},{7,2},{8,13},{9,12},{10,... | collective-permute-start | bytes 49160 | tf_op jit(solution)/shard_map/ppermute | solution.py:76
  44.4 1.4 %collective-permute-start.22 = (bf16[4,2048]{1,0:T(4,128)(2,1)S(1)}, bf16[4,2048]{1,0:T(4,128)(2,1)S(1)}, u32[]{:S(2)}, u32[]{:S(2)}) collective-permute-start(bf16[4,2048]{1,0:T(4,128)(2,1)S(1)} %get-tuple-element.86), channel_id=1, source_target_pairs={{0,6},{1,7},{2,4},{3,5},{4,2},{5,3},{6,0},{7,1},{8,14},{9,15},{10,... | collective-permute-start | bytes 49160 | tf_op jit(solution)/shard_map/ppermute | solution.py:76
  46.0 0.7 %collective-permute-done.21.refs_4_ = bf16[4,2048]{1,0:T(4,128)(2,1)S(1)} collective-permute-done((bf16[4,2048]{1,0:T(4,128)(2,1)S(1)}, bf16[4,2048]{1,0:T(4,128)(2,1)S(1)}, u32[]{:S(2)}, u32[]{:S(2)}) %collective-permute-start.21) | collective-permute-done | bytes 16416 | tf_op jit(solution)/shard_map/ppermute | solution.py:76
  46.7 2.4 %collective-permute-done.22.refs_5_ = bf16[4,2048]{1,0:T(4,128)(2,1)S(1)} collective-permute-done((bf16[4,2048]{1,0:T(4,128)(2,1)S(1)}, bf16[4,2048]{1,0:T(4,128)(2,1)S(1)}, u32[]{:S(2)}, u32[]{:S(2)}) %collective-permute-start.22) | collective-permute-done | bytes 16416 | tf_op jit(solution)/shard_map/ppermute | solution.py:76
  49.1 0.8 %combine.1 = bf16[32,2048]{1,0:T(8,128)(2,1)} custom-call(f32[32,2048]{1,0:T(8,128)S(1)} %hidden.1.refs_0_, f32[32,16]{1,0:T(8,128)S(1)} %get-tuple-element.70.refs_1_, bf16[4,2048]{1,0:T(4,128)(2,1)S(1)} %get-tuple-element.83.refs_2_, bf16[4,2048]{1,0:T(4,128)(2,1)S(1)} %collective-permute-done.20.refs_3_, ...), custom_call_target="tpu_custom_call" | custom-call | bytes 393216 | tf_op jit(solution)/shard_map/combine/pallas_call | solution.py:61
  (28 shorter events, 1.2 us)
Async XLA Ops:
  0.0 11.1 %collective-permute-start.3 = (bf16[2048,512]{1,0:T(8,128)(2,1)}, bf16[2048,512]{1,0:T(8,128)(2,1)S(1)}, u32[]{:S(2)}, u32[]{:S(2)}) collective-permute-start(bf16[2048,512]{1,0:T(8,128)(2,1)} %refs_11_.1), channel_id=1, source_target_pairs={{0,1},{1,0},{2,3},{3,2},{4,5},{5,4},{6,7},{7,6},{8,9},{9,8},{10,11... | collective-permute-start | bytes 6291464 | tf_op jit(solution)/shard_map/ppermute | solution.py:76
  0.5 10.6 %collective-permute-start.4 = (bf16[128,2048]{1,0:T(8,128)(2,1)}, bf16[128,2048]{1,0:T(8,128)(2,1)S(1)}, u32[]{:S(2)}, u32[]{:S(2)}) collective-permute-start(bf16[128,2048]{1,0:T(8,128)(2,1)} %refs_12_.1), channel_id=1, source_target_pairs={{0,1},{1,0},{2,3},{3,2},{4,5},{5,4},{6,7},{7,6},{8,9},{9,8},{10,11... | collective-permute-start | bytes 1572872 | tf_op jit(solution)/shard_map/ppermute | solution.py:76
  0.5 9.4 %collective-permute-start.2 = (bf16[32,2048]{1,0:T(8,128)(2,1)}, bf16[32,2048]{1,0:T(8,128)(2,1)S(1)}, u32[]{:S(2)}, u32[]{:S(2)}) collective-permute-start(bf16[32,2048]{1,0:T(8,128)(2,1)} %refs_4_.4), channel_id=1, source_target_pairs={{0,6},{1,7},{2,4},{3,5},{4,2},{5,3},{6,0},{7,1},{8,14},{9,15},{10,... | collective-permute-start | bytes 393224 | tf_op jit(solution)/shard_map/ppermute | solution.py:76
  4.4 6.7 %collective-permute-start.1 = (bf16[32,2048]{1,0:T(8,128)(2,1)}, bf16[32,2048]{1,0:T(8,128)(2,1)S(1)}, u32[]{:S(2)}, u32[]{:S(2)}) collective-permute-start(bf16[32,2048]{1,0:T(8,128)(2,1)} %refs_4_.4), channel_id=1, source_target_pairs={{0,5},{1,4},{2,7},{3,6},{4,1},{5,0},{6,3},{7,2},{8,13},{9,12},{10,... | collective-permute-start | bytes 393224 | tf_op jit(solution)/shard_map/ppermute | solution.py:76
  4.4 6.7 %collective-permute-start = (bf16[32,2048]{1,0:T(8,128)(2,1)}, bf16[32,2048]{1,0:T(8,128)(2,1)S(1)}, u32[]{:S(2)}, u32[]{:S(2)}) collective-permute-start(bf16[32,2048]{1,0:T(8,128)(2,1)} %refs_4_.4), channel_id=1, source_target_pairs={{0,3},{1,2},{2,1},{3,0},{4,7},{5,6},{6,5},{7,4},{8,11},{9,10},{10,... | collective-permute-start | bytes 393224 | tf_op jit(solution)/shard_map/ppermute | solution.py:76
  6.6 4.5 %copy-start = (bf16[32,2048]{1,0:T(8,128)(2,1)S(1)}, bf16[32,2048]{1,0:T(8,128)(2,1)}, u32[]{:S(2)}) copy-start(bf16[32,2048]{1,0:T(8,128)(2,1)} %refs_4_.4) | copy-start | bytes 393220
  12.3 5.9 %collective-permute-start.5 = (bf16[32,1280]{1,0:T(8,128)(2,1)S(1)}, bf16[32,1280]{1,0:T(8,128)(2,1)S(1)}, u32[]{:S(2)}, u32[]{:S(2)}) collective-permute-start(bf16[32,1280]{1,0:T(8,128)(2,1)S(1)} %get-tuple-element.50), channel_id=1, source_target_pairs={{0,3},{1,2},{2,1},{3,0},{4,7},{5,6},{6,5},{7,4},{8,11},{9,10},{10,... | collective-permute-start | bytes 245768 | tf_op jit(solution)/shard_map/ppermute | solution.py:76
  13.7 4.4 %collective-permute-start.6 = (bf16[32,1280]{1,0:T(8,128)(2,1)S(1)}, bf16[32,1280]{1,0:T(8,128)(2,1)S(1)}, u32[]{:S(2)}, u32[]{:S(2)}) collective-permute-start(bf16[32,1280]{1,0:T(8,128)(2,1)S(1)} %get-tuple-element.51), channel_id=1, source_target_pairs={{0,5},{1,4},{2,7},{3,6},{4,1},{5,0},{6,3},{7,2},{8,13},{9,12},{10,... | collective-permute-start | bytes 245768 | tf_op jit(solution)/shard_map/ppermute | solution.py:76
  14.4 5.7 %collective-permute-start.7 = (bf16[32,1280]{1,0:T(8,128)(2,1)S(1)}, bf16[32,1280]{1,0:T(8,128)(2,1)S(1)}, u32[]{:S(2)}, u32[]{:S(2)}) collective-permute-start(bf16[32,1280]{1,0:T(8,128)(2,1)S(1)} %get-tuple-element.52), channel_id=1, source_target_pairs={{0,6},{1,7},{2,4},{3,5},{4,2},{5,3},{6,0},{7,1},{8,14},{9,15},{10,... | collective-permute-start | bytes 245768 | tf_op jit(solution)/shard_map/ppermute | solution.py:76
  22.2 7.2 %collective-permute-start.11 = (bf16[512,2048]{1,0:T(8,128)(2,1)S(1)}, bf16[512,2048]{1,0:T(8,128)(2,1)S(1)}, u32[]{:S(2)}, u32[]{:S(2)}) collective-permute-start(bf16[512,2048]{1,0:T(8,128)(2,1)S(1)} %get-tuple-element.62.refs_4_), channel_id=1, source_target_pairs={{0,1},{1,0},{2,3},{3,2},{4,5},{5,4},{6,7},{7,6},{8,9},{9,8},{10,11... | collective-permute-start | bytes 6291464 | tf_op jit(solution)/shard_map/ppermute | solution.py:76
  22.3 6.1 %collective-permute-start.8 = (bf16[32,1024]{1,0:T(8,128)(2,1)S(1)}, bf16[32,1024]{1,0:T(8,128)(2,1)S(1)}, u32[]{:S(2)}, u32[]{:S(2)}) collective-permute-start(bf16[32,1024]{1,0:T(8,128)(2,1)S(1)} %get-tuple-element.59), channel_id=1, source_target_pairs={{0,3},{1,2},{2,1},{3,0},{4,7},{5,6},{6,5},{7,4},{8,11},{9,10},{10,... | collective-permute-start | bytes 196616 | tf_op jit(solution)/shard_map/ppermute | solution.py:76
  23.5 4.9 %collective-permute-start.9 = (bf16[32,1024]{1,0:T(8,128)(2,1)S(1)}, bf16[32,1024]{1,0:T(8,128)(2,1)S(1)}, u32[]{:S(2)}, u32[]{:S(2)}) collective-permute-start(bf16[32,1024]{1,0:T(8,128)(2,1)S(1)} %get-tuple-element.60), channel_id=1, source_target_pairs={{0,5},{1,4},{2,7},{3,6},{4,1},{5,0},{6,3},{7,2},{8,13},{9,12},{10,... | collective-permute-start | bytes 196616 | tf_op jit(solution)/shard_map/ppermute | solution.py:76
  24.0 5.3 %collective-permute-start.10 = (bf16[32,1024]{1,0:T(8,128)(2,1)S(1)}, bf16[32,1024]{1,0:T(8,128)(2,1)S(1)}, u32[]{:S(2)}, u32[]{:S(2)}) collective-permute-start(bf16[32,1024]{1,0:T(8,128)(2,1)S(1)} %get-tuple-element.61), channel_id=1, source_target_pairs={{0,6},{1,7},{2,4},{3,5},{4,2},{5,3},{6,0},{7,1},{8,14},{9,15},{10,... | collective-permute-start | bytes 196616 | tf_op jit(solution)/shard_map/ppermute | solution.py:76
  30.4 5.8 %collective-permute-start.15 = (bf16[16,2048]{1,0:T(8,128)(2,1)S(1)}, bf16[16,2048]{1,0:T(8,128)(2,1)S(1)}, u32[]{:S(2)}, u32[]{:S(2)}) collective-permute-start(bf16[16,2048]{1,0:T(8,128)(2,1)S(1)} %get-tuple-element.71), channel_id=1, source_target_pairs={{0,3},{1,2},{2,1},{3,0},{4,7},{5,6},{6,5},{7,4},{8,11},{9,10},{10,... | collective-permute-start | bytes 196616 | tf_op jit(solution)/shard_map/ppermute | solution.py:76
  30.8 6.9 %collective-permute-start.16 = (bf16[16,2048]{1,0:T(8,128)(2,1)S(1)}, bf16[16,2048]{1,0:T(8,128)(2,1)S(1)}, u32[]{:S(2)}, u32[]{:S(2)}) collective-permute-start(bf16[16,2048]{1,0:T(8,128)(2,1)S(1)} %get-tuple-element.72), channel_id=1, source_target_pairs={{0,5},{1,4},{2,7},{3,6},{4,1},{5,0},{6,3},{7,2},{8,13},{9,12},{10,... | collective-permute-start | bytes 196616 | tf_op jit(solution)/shard_map/ppermute | solution.py:76
  32.2 5.5 %collective-permute-start.17 = (bf16[16,2048]{1,0:T(8,128)(2,1)S(1)}, bf16[16,2048]{1,0:T(8,128)(2,1)S(1)}, u32[]{:S(2)}, u32[]{:S(2)}) collective-permute-start(bf16[16,2048]{1,0:T(8,128)(2,1)S(1)} %get-tuple-element.73), channel_id=1, source_target_pairs={{0,6},{1,7},{2,4},{3,5},{4,2},{5,3},{6,0},{7,1},{8,14},{9,15},{10,... | collective-permute-start | bytes 196616 | tf_op jit(solution)/shard_map/ppermute | solution.py:76
  34.4 10.0 %collective-permute-start.12 = (bf16[32,2048]{1,0:T(8,128)(2,1)S(1)}, bf16[32,2048]{1,0:T(8,128)(2,1)S(1)}, u32[]{:S(2)}, u32[]{:S(2)}) collective-permute-start(bf16[32,2048]{1,0:T(8,128)(2,1)S(1)} %get-tuple-element.67), channel_id=1, source_target_pairs={{0,3},{1,2},{2,1},{3,0},{4,7},{5,6},{6,5},{7,4},{8,11},{9,10},{10,... | collective-permute-start | bytes 393224 | tf_op jit(solution)/shard_map/ppermute | solution.py:76
  34.5 11.4 %collective-permute-start.13 = (bf16[32,2048]{1,0:T(8,128)(2,1)S(1)}, bf16[32,2048]{1,0:T(8,128)(2,1)S(1)}, u32[]{:S(2)}, u32[]{:S(2)}) collective-permute-start(bf16[32,2048]{1,0:T(8,128)(2,1)S(1)} %get-tuple-element.68), channel_id=1, source_target_pairs={{0,5},{1,4},{2,7},{3,6},{4,1},{5,0},{6,3},{7,2},{8,13},{9,12},{10,... | collective-permute-start | bytes 393224 | tf_op jit(solution)/shard_map/ppermute | solution.py:76
  36.2 9.7 %collective-permute-start.14 = (bf16[32,2048]{1,0:T(8,128)(2,1)S(1)}, bf16[32,2048]{1,0:T(8,128)(2,1)S(1)}, u32[]{:S(2)}, u32[]{:S(2)}) collective-permute-start(bf16[32,2048]{1,0:T(8,128)(2,1)S(1)} %get-tuple-element.69), channel_id=1, source_target_pairs={{0,6},{1,7},{2,4},{3,5},{4,2},{5,3},{6,0},{7,1},{8,14},{9,15},{10,... | collective-permute-start | bytes 393224 | tf_op jit(solution)/shard_map/ppermute | solution.py:76
  37.8 1.3 %collective-permute-start.18 = (bf16[8,2048]{1,0:T(8,128)(2,1)S(1)}, bf16[8,2048]{1,0:T(8,128)(2,1)S(1)}, u32[]{:S(2)}, u32[]{:S(2)}) collective-permute-start(bf16[8,2048]{1,0:T(8,128)(2,1)S(1)} %get-tuple-element.77), channel_id=1, source_target_pairs={{0,1},{1,0},{2,3},{3,2},{4,5},{5,4},{6,7},{7,6},{8,9},{9,8},{10,11... | collective-permute-start | bytes 98312 | tf_op jit(solution)/shard_map/ppermute | solution.py:76
  41.3 1.2 %collective-permute-start.19 = (bf16[8,2048]{1,0:T(8,128)(2,1)S(1)}, bf16[8,2048]{1,0:T(8,128)(2,1)S(1)}, u32[]{:S(2)}, u32[]{:S(2)}) collective-permute-start(bf16[8,2048]{1,0:T(8,128)(2,1)S(1)} %get-tuple-element.81), channel_id=1, source_target_pairs={{0,1},{1,0},{2,3},{3,2},{4,5},{5,4},{6,7},{7,6},{8,9},{9,8},{10,11... | collective-permute-start | bytes 98312 | tf_op jit(solution)/shard_map/ppermute | solution.py:76
  42.6 3.4 %collective-permute-start.20 = (bf16[4,2048]{1,0:T(4,128)(2,1)S(1)}, bf16[4,2048]{1,0:T(4,128)(2,1)S(1)}, u32[]{:S(2)}, u32[]{:S(2)}) collective-permute-start(bf16[4,2048]{1,0:T(4,128)(2,1)S(1)} %get-tuple-element.84), channel_id=1, source_target_pairs={{0,3},{1,2},{2,1},{3,0},{4,7},{5,6},{6,5},{7,4},{8,11},{9,10},{10,... | collective-permute-start | bytes 49160 | tf_op jit(solution)/shard_map/ppermute | solution.py:76
  43.5 3.2 %collective-permute-start.21 = (bf16[4,2048]{1,0:T(4,128)(2,1)S(1)}, bf16[4,2048]{1,0:T(4,128)(2,1)S(1)}, u32[]{:S(2)}, u32[]{:S(2)}) collective-permute-start(bf16[4,2048]{1,0:T(4,128)(2,1)S(1)} %get-tuple-element.85), channel_id=1, source_target_pairs={{0,5},{1,4},{2,7},{3,6},{4,1},{5,0},{6,3},{7,2},{8,13},{9,12},{10,... | collective-permute-start | bytes 49160 | tf_op jit(solution)/shard_map/ppermute | solution.py:76
  44.4 4.6 %collective-permute-start.22 = (bf16[4,2048]{1,0:T(4,128)(2,1)S(1)}, bf16[4,2048]{1,0:T(4,128)(2,1)S(1)}, u32[]{:S(2)}, u32[]{:S(2)}) collective-permute-start(bf16[4,2048]{1,0:T(4,128)(2,1)S(1)} %get-tuple-element.86), channel_id=1, source_target_pairs={{0,6},{1,7},{2,4},{3,5},{4,2},{5,3},{6,0},{7,1},{8,14},{9,15},{10,... | collective-permute-start | bytes 49160 | tf_op jit(solution)/shard_map/ppermute | solution.py:76

commit v4 on v3

--- a/solution.py
+++ b/solution.py
@@ -275,46 +275,88 @@
     put(dot_last(values, wkv_sib[...]), 2 * wide + narrow)
 
 
+def rope(values, rot_ref, which):
+    values = norm_rows(values.astype(F32))
+    turn = pltpu.roll(values, values.shape[1] // 2, 1)
+    return (values * rot_ref[2 * which] + turn * rot_ref[2 * which + 1]).astype(BF16)
+
+
+def heads_of(block_ref, rot_ref, count):
+    head = rot_ref.shape[2]
+    parts = [rope(block_ref[:, h * head : (h + 1) * head], rot_ref, 0) for h in range(count)]
+    return jnp.concatenate(parts, axis=0)
+
+
+def attend_part(query, keys, values, mask, floor=None):
+    new, span = mask.shape
+    lines, head = query.shape
+    score = dot_last(query, keys) * (head ** (-0.5) * LOG2E)
+    score = (score.reshape(lines // new, new, span) + mask[None]).reshape(lines, span)
+    top = jnp.broadcast_to(jnp.max(score, axis=-1, keepdims=True), (lines, head))
+    if floor is not None:
+        top = jnp.maximum(top, floor)
+    expo = jnp.exp2(score - (top if span == head else top[:, 0:1])).astype(BF16)
+    return dot(expo, values), dot(expo, jnp.ones((span, head), BF16)), top
+
+
+def cache_kernel(chips, q_width, *refs):
+    got = refs[: chips - 1]
+    keys_ref, values_ref, mask_ref, rot_ref = refs[chips - 1 : chips + 3]
+    outs = refs[chips + 3 :]
+    chip = lax.axis_index("tensor") // 2
+    kv_heads, _, head = keys_ref.shape
+    per_chip = 2 * q_width // head
+    mask = mask_ref[...]
+    mask = jnp.where(iota(mask.shape, 1) < mask.shape[0], NEG_FILL, mask)
+    for j in range(chips - 1):
+        kv = (chip ^ j) * per_chip // (chips * per_chip // kv_heads)
+        query = heads_of(got[j], rot_ref, per_chip)
+        outs[2 * j][...] = query
+        parts = attend_part(query, keys_ref[kv], values_ref[kv], mask)
+        for at, part in enumerate(parts):
+            outs[2 * j + 1][at] = part
+
+
 def attend_kernel(chips, q_width, kv_ready, *refs):
     got = refs[:chips]
-    at = chips + 1 if kv_ready else chips
-    keys_ref, values_ref, mask_ref, rot_ref = refs[at : at + 4]
-    outs = refs[at + 5 : at + 5 + chips]
-    fresh_ref = refs[chips] if kv_ready else refs[-1]
+    cached = refs[chips : 3 * chips - 2]
+    refs = refs[3 * chips - 2 :]
+    fresh_ref = refs[0] if kv_ready else refs[-1]
+    keys_ref, values_ref, mask_ref, rot_ref = refs[kv_ready : kv_ready + 4]
+    outs = refs[kv_ready + 5 : kv_ready + 5 + chips]
     me = lax.axis_index("tensor")
     chip = me // 2
-    new = got[0].shape[0]
     kv_heads, span, head = keys_ref.shape
+    new = mask_ref.shape[0]
     per_chip = 2 * q_width // head
-    group = chips * per_chip // kv_heads
-
     if not kv_ready:
         for rel in range(2 * chips):
             left = 2 * q_width + (rel % 2) * head
             fresh_ref[step(rel // 2) ^ (rel % 2)] = got[rel // 2][:, left : left + head]
 
-    def rope(values, which):
-        values = norm_rows(values.astype(F32))
-        turned = pltpu.roll(values, head // 2, 1)
-        return (values * rot_ref[2 * which] + turned * rot_ref[2 * which + 1]).astype(BF16)
-
-    scale = head ** (-0.5) * LOG2E
-    for j in range(chips):
-        kv = (chip ^ j) * per_chip // group
+    allow = mask_ref[:, 0:head]
+    allow = jnp.where(iota(allow.shape, 1) < new, allow, NEG_FILL)
+    empty = jnp.zeros((head - new, head), BF16)
+    for j in reversed(range(chips)):
+        kv = (chip ^ j) * per_chip // (chips * per_chip // kv_heads)
         key_at, value_at = kv, kv + kv_heads
         if not kv_ready:
             key_at, value_at = me ^ key_at, me ^ value_at
-        keys = jnp.concatenate([rope(fresh_ref[key_at], 1), keys_ref[kv, new:span]], axis=0)
-        values = jnp.concatenate([fresh_ref[value_at], values_ref[kv, new:span]], axis=0)
-        query = jnp.concatenate(
-            [rope(got[j][:, h * head : (h + 1) * head], 0) for h in range(per_chip)], axis=0
-        )
-        score = dot_last(query, keys) * scale
-        score = score.reshape(per_chip, new, span) + mask_ref[...][None]
-        expo = jnp.exp2(score - jnp.max(score, axis=-1, keepdims=True))
-        denom = jnp.sum(expo, axis=-1, keepdims=True).reshape(per_chip * new, 1)
-        expo = expo.astype(BF16).reshape(per_chip * new, span)
-        result = (dot(expo, values) / denom).astype(BF16)
+        key, value = rope(fresh_ref[key_at], rot_ref, 1), fresh_ref[value_at]
+        if j == chips - 1:
+            keys = jnp.concatenate([key, keys_ref[kv, new:span]], axis=0)
+            values = jnp.concatenate([value, values_ref[kv, new:span]], axis=0)
+            query = heads_of(got[j], rot_ref, per_chip)
+            result, total, _ = attend_part(query, keys, values, mask_ref[...])
+        else:
+            query, before = cached[2 * j][...], cached[2 * j + 1]
+            keys = jnp.concatenate([key, empty], axis=0)
+            values = jnp.concatenate([value, empty], axis=0)
+            result, total, top = attend_part(query, keys, values, allow, before[2])
+            shrink = jnp.exp2(before[2] - top)
+            result = result + before[0] * shrink
+            total = total + before[1] * shrink
+        result = (result / total).astype(BF16)
         for h in range(per_chip):
             outs[j][:, h * head : (h + 1) * head] = result[h * new : (h + 1) * new]
 
@@ -534,18 +576,29 @@
         pieces = jnp.stack(pieces)[lax.axis_index("tensor") ^ jnp.arange(devices)]
         pieces = pieces.transpose(1, 0, 2).reshape(new, 2 * kv_heads, head)
         kv_ready = [(pieces.transpose(1, 0, 2), vmem)]
+    lines = 2 * q_width // head * new
+    cached = call(
+        functools.partial(cache_kernel, chips, q_width),
+        "cache",
+        [in_vmem((lines, head), BF16), in_vmem((3, lines, head), F32)] * (chips - 1),
+        [(block, vmem) for block in got[:-1]]
+        + [(keys, vmem), (values, vmem), (mask, vmem), (rot, vmem)],
+        limit=16,
+        flops=8 * new * (chips - 1) * q_width * span,
+        moved=4 * span * kv_heads * head,
+    )
     *attended, wo = call(
-        functools.partial(attend_kernel, chips, q_width, bool(kv_ready)),
+        functools.partial(attend_kernel, chips, q_width, len(kv_ready)),
         "attend",
         [in_vmem((new, 2 * q_width), BF16)] * chips + [in_vmem(wo.shape, wo.dtype)],
         [(block, vmem) for block in got]
+        + [(array, vmem) for array in cached]
         + kv_ready
-        + [(keys, vmem), (values, vmem), (mask, vmem), (rot, vmem)]
-        + [(wo, vmem)],
+        + [(keys, vmem), (values, vmem), (mask, vmem), (rot, vmem), (wo, vmem)],
         [] if kv_ready else [pltpu.VMEM((devices, new, head), BF16)],
         limit=16,
-        same={chips + len(kv_ready) + 4: chips},
-        flops=8 * new * chips * q_width * span,
+        same={chips + len(cached) + len(kv_ready) + 4: chips},
+        flops=8 * new * q_width * span,
         moved=4 * span * kv_heads * head,
     )
     wo_sib = hop(wo, 1)

time: 50.1 us -> 51.5 us (1.028)
  waiting for transfers between devices: 9.43 us -> 7.37 us
  starting transfers between devices: 21.4 us -> 23.3 us
  Pallas kernels: 17 us -> 18.5 us
    ppermute x23, waiting for transfers between devices: 9.43 us -> 7.37 us  [hop(): lax.ppermute(value, 'tensor', [(i, i ^ step) for i in range(devices)])]
    ppermute x23, starting transfers between devices: 21.4 us -> 23.3 us  [hop(): lax.ppermute(value, 'tensor', [(i, i ^ step) for i in range(devices)])]
    pallas_call x12 -> x13, Pallas kernels: 17 us -> 18.5 us  [call(): pl.pallas_call(kernel, out_shape=outs, in_specs=specs, out_specs=[pl.Bloc...]
  transfers between devices with their start and end apart: 23 -> 23, of which waited for: 7 -> 5; matrix products, arithmetic and copies ran while one was open for 0% -> 0% of each run, Pallas kernels for 24% -> 27%
where the time goes in v4:
time: 51.5 us; the launch traced here: 51.2 us
  starting transfers between devices  23.3 us (45%)
  Pallas kernels  18.5 us (36%)
  waiting for transfers between devices  7.37 us (14%)
  between operations  2.13 us (4%)
    ppermute x23, starting transfers between devices, hop(): lax.ppermute(value, 'tensor', [(i, i ^ step) for i in range(devices)])  23.3 us
    pallas_call x13, Pallas kernels, call(): pl.pallas_call(kernel, out_shape=outs, in_specs=specs, out_specs=[pl.Bloc...  18.5 us
    ppermute x23, waiting for transfers between devices, hop(): lax.ppermute(value, 'tensor', [(i, i ^ step) for i in range(devices)])  7.37 us
  transfers between devices with their start and end apart: 23, of which 5 were waited for; matrix products, arithmetic and copies ran while one was open for 0% of the time, Pallas kernels for 27%

profile of v4, /device:TPU:0, one launch (start us, length us, event | category | flops | bytes accessed | tf_op | source)
XLA Modules:
  0.0 51.2 jit_solution(6621067772694447669)
XLA Ops:
  0.0 0.5 collective-permute-start.3
  0.5 3.9 %collective-permute-start.2 = (bf16[32,2048]{1,0:T(8,128)(2,1)}, bf16[32,2048]{1,0:T(8,128)(2,1)S(1)}, u32[]{:S(2)}, u32[]{:S(2)}) collective-permute-start(bf16[32,2048]{1,0:T(8,128)(2,1)} %refs_4_.4), channel_id=1, source_target_pairs={{0,6},{1,7},{2,4},{3,5},{4,2},{5,3},{6,0},{7,1},{8,14},{9,15},{10,... | collective-permute-start | bytes 393224 | tf_op jit(solution)/shard_map/ppermute | solution.py:76
  4.4 0.3 collective-permute-start
  6.6 3.2 %prep.1 = (bf16[4,640,128]{2,1,0:T(8,128)(2,1)S(1)}, bf16[4,640,128]{2,1,0:T(8,128)(2,1)S(1)}, f32[32,640]{1,0:T(8,128)S(1)}, f32[4,32,128]{2,1,0:T(8,128)S(1)},...) custom-call(bf16[1,1024,512]{2,1,0:T(8,128)(2,1)} %refs_0_.3, ...), custom_call_target="tpu_custom_call" | custom-call | bytes 2621440 | tf_op jit(solution)/shard_map/prep/pallas_call | solution.py:61
  9.9 1.2 %collective-permute-done.1.refs_2_ = bf16[32,2048]{1,0:T(8,128)(2,1)S(1)} collective-permute-done((bf16[32,2048]{1,0:T(8,128)(2,1)}, bf16[32,2048]{1,0:T(8,128)(2,1)S(1)}, u32[]{:S(2)}, u32[]{:S(2)}) %collective-permute-start.1) | collective-permute-done | bytes 131104 | tf_op jit(solution)/shard_map/ppermute | solution.py:76
  11.1 1.1 %project.1 = (bf16[32,1280]{1,0:T(8,128)(2,1)S(1)}, bf16[32,1280]{1,0:T(8,128)(2,1)S(1)}, bf16[32,1280]{1,0:T(8,128)(2,1)S(1)}, bf16[32,1280]{1,0:T(8,128)(2,1)S(1)}) custom-call(bf16[32,2048]{1,0:T(8,128)(2,1)S(1)} %copy-done, bf16[32,2048]{1,0:T(8,128)(2,1)S(1)} %collective-permute-done.refs_1_, bf16[32,2048]{1,0:T(8,128)(2,1)S(1)} %collective-permute-done.1.refs_2_, ...), custom_call_target="tpu_custom_call" | custom-call | flops 671088640 | bytes 5242880 | tf_op jit(solution)/shard_map/project/pallas_call | solution.py:61
  12.3 1.5 %collective-permute-start.5 = (bf16[32,1280]{1,0:T(8,128)(2,1)S(1)}, bf16[32,1280]{1,0:T(8,128)(2,1)S(1)}, u32[]{:S(2)}, u32[]{:S(2)}) collective-permute-start(bf16[32,1280]{1,0:T(8,128)(2,1)S(1)} %get-tuple-element.56), channel_id=1, source_target_pairs={{0,3},{1,2},{2,1},{3,0},{4,7},{5,6},{6,5},{7,4},{8,11},{9,10},{10,... | collective-permute-start | bytes 245768 | tf_op jit(solution)/shard_map/ppermute | solution.py:76
  13.7 0.6 %collective-permute-start.6 = (bf16[32,1280]{1,0:T(8,128)(2,1)S(1)}, bf16[32,1280]{1,0:T(8,128)(2,1)S(1)}, u32[]{:S(2)}, u32[]{:S(2)}) collective-permute-start(bf16[32,1280]{1,0:T(8,128)(2,1)S(1)} %get-tuple-element.57), channel_id=1, source_target_pairs={{0,5},{1,4},{2,7},{3,6},{4,1},{5,0},{6,3},{7,2},{8,13},{9,12},{10,... | collective-permute-start | bytes 245768 | tf_op jit(solution)/shard_map/ppermute | solution.py:76
  14.4 1.2 %collective-permute-start.7 = (bf16[32,1280]{1,0:T(8,128)(2,1)S(1)}, bf16[32,1280]{1,0:T(8,128)(2,1)S(1)}, u32[]{:S(2)}, u32[]{:S(2)}) collective-permute-start(bf16[32,1280]{1,0:T(8,128)(2,1)S(1)} %get-tuple-element.58), channel_id=1, source_target_pairs={{0,6},{1,7},{2,4},{3,5},{4,2},{5,3},{6,0},{7,1},{8,14},{9,15},{10,... | collective-permute-start | bytes 245768 | tf_op jit(solution)/shard_map/ppermute | solution.py:76
  15.5 2.6 %route.1 = (f32[64,128]{1,0:T(8,128)S(1)}, f32[32,16]{1,0:T(8,128)S(1)}, f32[16,128]{1,0:T(8,128)S(1)}, f32[1,2048]{1,0:T(1,128)S(1)}, bf16[512,2048]{1,0:T(8,128)(2,1)S(1)}, /*index=5*/bf16[1,768,2048]{2,1,0:T(8,128)(2,1)S(1)}) custom-call(bf16[32,1280]{1,0:T(8,128)(2,1)S(1)} %get-tuple-element.55.refs_0_, s32[8,256]{1,0:T(8,128)} %bitcast.7, ...), custom_call_target="tpu_custom_call" | custom-call | bytes 10485760 | tf_op jit(solution)/shard_map/route/pallas_call | solution.py:61
  18.2 1.9 %cache.1 = (bf16[256,128]{1,0:T(8,128)(2,1)S(1)}, f32[3,256,128]{2,1,0:T(8,128)S(1)}, bf16[256,128]{1,0:T(8,128)(2,1)S(1)}, f32[3,256,128]{2,1,0:T(8,128)S(1)}, ...) custom-call(bf16[32,1280]{1,0:T(8,128)(2,1)S(1)} %get-tuple-element.55.refs_0_, ...), custom_call_target="tpu_custom_call" | custom-call | flops 251658240 | bytes 1310720 | tf_op jit(solution)/shard_map/cache/pallas_call | solution.py:61
  20.1 1.7 %attend.1 = (bf16[32,1024]{1,0:T(8,128)(2,1)S(1)}, bf16[32,1024]{1,0:T(8,128)(2,1)S(1)}, bf16[32,1024]{1,0:T(8,128)(2,1)S(1)}, bf16[32,1024]{1,0:T(8,128)(2,1)S(1)}, bf16[512,2048]{1,0:T(8,128)(2,1)S(1)}) custom-call(bf16[32,1280]{1,0:T(8,128)(2,1)S(1)} %get-tuple-element.55.refs_0_, ...), custom_call_target="tpu_custom_call", output_to_operand_aliasing={{4}: (14, {})} | custom-call | flops 83886080 | bytes 1310720 | tf_op jit(solution)/shard_map/attend/pallas_call | solution.py:61
  21.8 2.0 %collective-permute-start.11 = (bf16[512,2048]{1,0:T(8,128)(2,1)S(1)}, bf16[512,2048]{1,0:T(8,128)(2,1)S(1)}, u32[]{:S(2)}, u32[]{:S(2)}) collective-permute-start(bf16[512,2048]{1,0:T(8,128)(2,1)S(1)} %get-tuple-element.74.refs_4_), channel_id=1, source_target_pairs={{0,1},{1,0},{2,3},{3,2},{4,5},{5,4},{6,7},{7,6},{8,9},{9,8},{10,11... | collective-permute-start | bytes 6291464 | tf_op jit(solution)/shard_map/ppermute | solution.py:76
  23.8 1.7 %collective-permute-start.9 = (bf16[32,1024]{1,0:T(8,128)(2,1)S(1)}, bf16[32,1024]{1,0:T(8,128)(2,1)S(1)}, u32[]{:S(2)}, u32[]{:S(2)}) collective-permute-start(bf16[32,1024]{1,0:T(8,128)(2,1)S(1)} %get-tuple-element.72), channel_id=1, source_target_pairs={{0,5},{1,4},{2,7},{3,6},{4,1},{5,0},{6,3},{7,2},{8,13},{9,12},{10,... | collective-permute-start | bytes 196616 | tf_op jit(solution)/shard_map/ppermute | solution.py:76
  25.6 1.5 %collective-permute-start.10 = (bf16[32,1024]{1,0:T(8,128)(2,1)S(1)}, bf16[32,1024]{1,0:T(8,128)(2,1)S(1)}, u32[]{:S(2)}, u32[]{:S(2)}) collective-permute-start(bf16[32,1024]{1,0:T(8,128)(2,1)S(1)} %get-tuple-element.73), channel_id=1, source_target_pairs={{0,6},{1,7},{2,4},{3,5},{4,2},{5,3},{6,0},{7,1},{8,14},{9,15},{10,... | collective-permute-start | bytes 196616 | tf_op jit(solution)/shard_map/ppermute | solution.py:76
  27.1 2.9 %select.1 = (f32[16,2048]{1,0:T(8,128)S(1)}, bf16[1,768,2048]{2,1,0:T(8,128)(2,1)S(1)}, bf16[1,768,2048]{2,1,0:T(8,128)(2,1)S(1)}) custom-call(bf16[32,2048]{1,0:T(8,128)(2,1)S(1)} %copy-done, bf16[32,2048]{1,0:T(8,128)(2,1)S(1)} %collective-permute-done.refs_1_, bf16[32,2048]{1,0:T(8,128)(2,1)S(1)} %collective-permute-done.1.refs_2_, ...), custom_call_target="tpu_custom_call" | custom-call | flops 8388608 | bytes 12582912 | tf_op jit(solution)/shard_map/select/pallas_call | solution.py:61
  30.0 0.8 %collective-permute-done.10.refs_3_ = bf16[32,1024]{1,0:T(8,128)(2,1)S(1)} collective-permute-done((bf16[32,1024]{1,0:T(8,128)(2,1)S(1)}, bf16[32,1024]{1,0:T(8,128)(2,1)S(1)}, u32[]{:S(2)}, u32[]{:S(2)}) %collective-permute-start.10) | collective-permute-done | bytes 65568 | tf_op jit(solution)/shard_map/ppermute | solution.py:76
  30.7 1.0 %experts.1 = (bf16[16,2048]{1,0:T(8,128)(2,1)S(1)}, bf16[16,2048]{1,0:T(8,128)(2,1)S(1)}, bf16[16,2048]{1,0:T(8,128)(2,1)S(1)}, bf16[16,2048]{1,0:T(8,128)(2,1)S(1)}) custom-call(bf16[32,1024]{1,0:T(8,128)(2,1)S(1)} %get-tuple-element.70.refs_5_.refs_0_, bf16[32,1024]{1,0:T(8,128)(2,1)S(1)} %collective-permute-done.8.refs_1_, ...), custom_call_target="tpu_custom_call" | custom-call | flops 268435456 | bytes 4194304 | tf_op jit(solution)/shard_map/experts/pallas_call | solution.py:61
  31.9 1.7 %collective-permute-start.16 = (bf16[16,2048]{1,0:T(8,128)(2,1)S(1)}, bf16[16,2048]{1,0:T(8,128)(2,1)S(1)}, u32[]{:S(2)}, u32[]{:S(2)}) collective-permute-start(bf16[16,2048]{1,0:T(8,128)(2,1)S(1)} %get-tuple-element.84), channel_id=1, source_target_pairs={{0,5},{1,4},{2,7},{3,6},{4,1},{5,0},{6,3},{7,2},{8,13},{9,12},{10,... | collective-permute-start | bytes 196616 | tf_op jit(solution)/shard_map/ppermute | solution.py:76
  33.6 1.4 %collective-permute-start.17 = (bf16[16,2048]{1,0:T(8,128)(2,1)S(1)}, bf16[16,2048]{1,0:T(8,128)(2,1)S(1)}, u32[]{:S(2)}, u32[]{:S(2)}) collective-permute-start(bf16[16,2048]{1,0:T(8,128)(2,1)S(1)} %get-tuple-element.85), channel_id=1, source_target_pairs={{0,6},{1,7},{2,4},{3,5},{4,2},{5,3},{6,0},{7,1},{8,14},{9,15},{10,... | collective-permute-start | bytes 196616 | tf_op jit(solution)/shard_map/ppermute | solution.py:76
  35.0 0.7 %slots.1 = (bf16[32,2048]{1,0:T(8,128)(2,1)S(1)}, bf16[32,2048]{1,0:T(8,128)(2,1)S(1)}, bf16[32,2048]{1,0:T(8,128)(2,1)S(1)}, bf16[32,2048]{1,0:T(8,128)(2,1)S(1)}) custom-call(bf16[32,1024]{1,0:T(8,128)(2,1)S(1)} %get-tuple-element.70.refs_5_.refs_0_, bf16[32,1024]{1,0:T(8,128)(2,1)S(1)} %collective-permute-done.8.refs_1_, ...), custom_call_target="tpu_custom_call" | custom-call | flops 536870912 | bytes 4194304 | tf_op jit(solution)/shard_map/slots/pallas_call | solution.py:61
  35.8 1.8 %collective-permute-start.13 = (bf16[32,2048]{1,0:T(8,128)(2,1)S(1)}, bf16[32,2048]{1,0:T(8,128)(2,1)S(1)}, u32[]{:S(2)}, u32[]{:S(2)}) collective-permute-start(bf16[32,2048]{1,0:T(8,128)(2,1)S(1)} %get-tuple-element.80), channel_id=1, source_target_pairs={{0,5},{1,4},{2,7},{3,6},{4,1},{5,0},{6,3},{7,2},{8,13},{9,12},{10,... | collective-permute-start | bytes 393224 | tf_op jit(solution)/shard_map/ppermute | solution.py:76
  37.6 1.4 %collective-permute-start.14 = (bf16[32,2048]{1,0:T(8,128)(2,1)S(1)}, bf16[32,2048]{1,0:T(8,128)(2,1)S(1)}, u32[]{:S(2)}, u32[]{:S(2)}) collective-permute-start(bf16[32,2048]{1,0:T(8,128)(2,1)S(1)} %get-tuple-element.81), channel_id=1, source_target_pairs={{0,6},{1,7},{2,4},{3,5},{4,2},{5,3},{6,0},{7,1},{8,14},{9,15},{10,... | collective-permute-start | bytes 393224 | tf_op jit(solution)/shard_map/ppermute | solution.py:76
  39.2 1.2 %collective-permute-done.18.other_ref = bf16[8,2048]{1,0:T(8,128)(2,1)S(1)} collective-permute-done((bf16[8,2048]{1,0:T(8,128)(2,1)S(1)}, bf16[8,2048]{1,0:T(8,128)(2,1)S(1)}, u32[]{:S(2)}, u32[]{:S(2)}) %collective-permute-start.18) | collective-permute-done | bytes 32800 | tf_op jit(solution)/shard_map/ppermute | solution.py:76
  40.4 2.2 %expert.1 = (f32[8,2048]{1,0:T(8,128)S(1)}, bf16[8,2048]{1,0:T(8,128)(2,1)S(1)}) custom-call(bf16[8,2048]{1,0:T(8,128)(2,1)S(1)} %get-tuple-element.88.own_ref, bf16[8,2048]{1,0:T(8,128)(2,1)S(1)} %collective-permute-done.18.other_ref, bf16[1,768,2048]{2,1,0:T(8,128)(2,1)S(1)} %get-tuple-element.76.refs_7_.gate_ref, ...), custom_call_target="tpu_custom_call" | custom-call | flops 150994944 | bytes 9437184 | tf_op jit(solution)/shard_map/expert/pallas_call | solution.py:61
  42.6 0.2 collective-permute-start.19
  42.8 1.0 %collective-permute-done.19.other_ref = bf16[8,2048]{1,0:T(8,128)(2,1)S(1)} collective-permute-done((bf16[8,2048]{1,0:T(8,128)(2,1)S(1)}, bf16[8,2048]{1,0:T(8,128)(2,1)S(1)}, u32[]{:S(2)}, u32[]{:S(2)}) %collective-permute-start.19) | collective-permute-done | bytes 32800 | tf_op jit(solution)/shard_map/ppermute | solution.py:76
  43.9 0.2 collective-permute-start.20
  44.2 1.6 %collective-permute-start.21 = (bf16[4,2048]{1,0:T(4,128)(2,1)S(1)}, bf16[4,2048]{1,0:T(4,128)(2,1)S(1)}, u32[]{:S(2)}, u32[]{:S(2)}) collective-permute-start(bf16[4,2048]{1,0:T(4,128)(2,1)S(1)} %get-tuple-element.97), channel_id=1, source_target_pairs={{0,5},{1,4},{2,7},{3,6},{4,1},{5,0},{6,3},{7,2},{8,13},{9,12},{10,... | collective-permute-start | bytes 49160 | tf_op jit(solution)/shard_map/ppermute | solution.py:76
  45.8 1.4 %collective-permute-start.22 = (bf16[4,2048]{1,0:T(4,128)(2,1)S(1)}, bf16[4,2048]{1,0:T(4,128)(2,1)S(1)}, u32[]{:S(2)}, u32[]{:S(2)}) collective-permute-start(bf16[4,2048]{1,0:T(4,128)(2,1)S(1)} %get-tuple-element.98), channel_id=1, source_target_pairs={{0,6},{1,7},{2,4},{3,5},{4,2},{5,3},{6,0},{7,1},{8,14},{9,15},{10,... | collective-permute-start | bytes 49160 | tf_op jit(solution)/shard_map/ppermute | solution.py:76
  47.3 3.1 %collective-permute-done.22.refs_5_ = bf16[4,2048]{1,0:T(4,128)(2,1)S(1)} collective-permute-done((bf16[4,2048]{1,0:T(4,128)(2,1)S(1)}, bf16[4,2048]{1,0:T(4,128)(2,1)S(1)}, u32[]{:S(2)}, u32[]{:S(2)}) %collective-permute-start.22) | collective-permute-done | bytes 16416 | tf_op jit(solution)/shard_map/ppermute | solution.py:76
  50.4 0.8 %combine.1 = bf16[32,2048]{1,0:T(8,128)(2,1)} custom-call(f32[32,2048]{1,0:T(8,128)S(1)} %hidden.1.refs_0_, f32[32,16]{1,0:T(8,128)S(1)} %get-tuple-element.82.refs_1_, bf16[4,2048]{1,0:T(4,128)(2,1)S(1)} %get-tuple-element.95.refs_2_, bf16[4,2048]{1,0:T(4,128)(2,1)S(1)} %collective-permute-done.20.refs_3_, ...), custom_call_target="tpu_custom_call" | custom-call | bytes 393216 | tf_op jit(solution)/shard_map/combine/pallas_call | solution.py:61
  (29 shorter events, 0.7 us)
Async XLA Ops:
  0.0 11.1 %collective-permute-start.3 = (bf16[2048,512]{1,0:T(8,128)(2,1)}, bf16[2048,512]{1,0:T(8,128)(2,1)S(1)}, u32[]{:S(2)}, u32[]{:S(2)}) collective-permute-start(bf16[2048,512]{1,0:T(8,128)(2,1)} %refs_11_.1), channel_id=1, source_target_pairs={{0,1},{1,0},{2,3},{3,2},{4,5},{5,4},{6,7},{7,6},{8,9},{9,8},{10,11... | collective-permute-start | bytes 6291464 | tf_op jit(solution)/shard_map/ppermute | solution.py:76
  0.5 10.6 %collective-permute-start.4 = (bf16[128,2048]{1,0:T(8,128)(2,1)}, bf16[128,2048]{1,0:T(8,128)(2,1)S(1)}, u32[]{:S(2)}, u32[]{:S(2)}) collective-permute-start(bf16[128,2048]{1,0:T(8,128)(2,1)} %refs_12_.1), channel_id=1, source_target_pairs={{0,1},{1,0},{2,3},{3,2},{4,5},{5,4},{6,7},{7,6},{8,9},{9,8},{10,11... | collective-permute-start | bytes 1572872 | tf_op jit(solution)/shard_map/ppermute | solution.py:76
  0.5 9.4 %collective-permute-start.2 = (bf16[32,2048]{1,0:T(8,128)(2,1)}, bf16[32,2048]{1,0:T(8,128)(2,1)S(1)}, u32[]{:S(2)}, u32[]{:S(2)}) collective-permute-start(bf16[32,2048]{1,0:T(8,128)(2,1)} %refs_4_.4), channel_id=1, source_target_pairs={{0,6},{1,7},{2,4},{3,5},{4,2},{5,3},{6,0},{7,1},{8,14},{9,15},{10,... | collective-permute-start | bytes 393224 | tf_op jit(solution)/shard_map/ppermute | solution.py:76
  4.4 6.7 %collective-permute-start.1 = (bf16[32,2048]{1,0:T(8,128)(2,1)}, bf16[32,2048]{1,0:T(8,128)(2,1)S(1)}, u32[]{:S(2)}, u32[]{:S(2)}) collective-permute-start(bf16[32,2048]{1,0:T(8,128)(2,1)} %refs_4_.4), channel_id=1, source_target_pairs={{0,5},{1,4},{2,7},{3,6},{4,1},{5,0},{6,3},{7,2},{8,13},{9,12},{10,... | collective-permute-start | bytes 393224 | tf_op jit(solution)/shard_map/ppermute | solution.py:76
  4.4 6.7 %collective-permute-start = (bf16[32,2048]{1,0:T(8,128)(2,1)}, bf16[32,2048]{1,0:T(8,128)(2,1)S(1)}, u32[]{:S(2)}, u32[]{:S(2)}) collective-permute-start(bf16[32,2048]{1,0:T(8,128)(2,1)} %refs_4_.4), channel_id=1, source_target_pairs={{0,3},{1,2},{2,1},{3,0},{4,7},{5,6},{6,5},{7,4},{8,11},{9,10},{10,... | collective-permute-start | bytes 393224 | tf_op jit(solution)/shard_map/ppermute | solution.py:76
  6.6 4.5 %copy-start = (bf16[32,2048]{1,0:T(8,128)(2,1)S(1)}, bf16[32,2048]{1,0:T(8,128)(2,1)}, u32[]{:S(2)}) copy-start(bf16[32,2048]{1,0:T(8,128)(2,1)} %refs_4_.4) | copy-start | bytes 393220
  12.3 5.9 %collective-permute-start.5 = (bf16[32,1280]{1,0:T(8,128)(2,1)S(1)}, bf16[32,1280]{1,0:T(8,128)(2,1)S(1)}, u32[]{:S(2)}, u32[]{:S(2)}) collective-permute-start(bf16[32,1280]{1,0:T(8,128)(2,1)S(1)} %get-tuple-element.56), channel_id=1, source_target_pairs={{0,3},{1,2},{2,1},{3,0},{4,7},{5,6},{6,5},{7,4},{8,11},{9,10},{10,... | collective-permute-start | bytes 245768 | tf_op jit(solution)/shard_map/ppermute | solution.py:76
  13.7 4.4 %collective-permute-start.6 = (bf16[32,1280]{1,0:T(8,128)(2,1)S(1)}, bf16[32,1280]{1,0:T(8,128)(2,1)S(1)}, u32[]{:S(2)}, u32[]{:S(2)}) collective-permute-start(bf16[32,1280]{1,0:T(8,128)(2,1)S(1)} %get-tuple-element.57), channel_id=1, source_target_pairs={{0,5},{1,4},{2,7},{3,6},{4,1},{5,0},{6,3},{7,2},{8,13},{9,12},{10,... | collective-permute-start | bytes 245768 | tf_op jit(solution)/shard_map/ppermute | solution.py:76
  14.4 5.7 %collective-permute-start.7 = (bf16[32,1280]{1,0:T(8,128)(2,1)S(1)}, bf16[32,1280]{1,0:T(8,128)(2,1)S(1)}, u32[]{:S(2)}, u32[]{:S(2)}) collective-permute-start(bf16[32,1280]{1,0:T(8,128)(2,1)S(1)} %get-tuple-element.58), channel_id=1, source_target_pairs={{0,6},{1,7},{2,4},{3,5},{4,2},{5,3},{6,0},{7,1},{8,14},{9,15},{10,... | collective-permute-start | bytes 245768 | tf_op jit(solution)/shard_map/ppermute | solution.py:76
  21.8 8.9 %collective-permute-start.11 = (bf16[512,2048]{1,0:T(8,128)(2,1)S(1)}, bf16[512,2048]{1,0:T(8,128)(2,1)S(1)}, u32[]{:S(2)}, u32[]{:S(2)}) collective-permute-start(bf16[512,2048]{1,0:T(8,128)(2,1)S(1)} %get-tuple-element.74.refs_4_), channel_id=1, source_target_pairs={{0,1},{1,0},{2,3},{3,2},{4,5},{5,4},{6,7},{7,6},{8,9},{9,8},{10,11... | collective-permute-start | bytes 6291464 | tf_op jit(solution)/shard_map/ppermute | solution.py:76
  23.8 6.1 %collective-permute-start.8 = (bf16[32,1024]{1,0:T(8,128)(2,1)S(1)}, bf16[32,1024]{1,0:T(8,128)(2,1)S(1)}, u32[]{:S(2)}, u32[]{:S(2)}) collective-permute-start(bf16[32,1024]{1,0:T(8,128)(2,1)S(1)} %get-tuple-element.71), channel_id=1, source_target_pairs={{0,3},{1,2},{2,1},{3,0},{4,7},{5,6},{6,5},{7,4},{8,11},{9,10},{10,... | collective-permute-start | bytes 196616 | tf_op jit(solution)/shard_map/ppermute | solution.py:76
  23.8 6.1 %collective-permute-start.9 = (bf16[32,1024]{1,0:T(8,128)(2,1)S(1)}, bf16[32,1024]{1,0:T(8,128)(2,1)S(1)}, u32[]{:S(2)}, u32[]{:S(2)}) collective-permute-start(bf16[32,1024]{1,0:T(8,128)(2,1)S(1)} %get-tuple-element.72), channel_id=1, source_target_pairs={{0,5},{1,4},{2,7},{3,6},{4,1},{5,0},{6,3},{7,2},{8,13},{9,12},{10,... | collective-permute-start | bytes 196616 | tf_op jit(solution)/shard_map/ppermute | solution.py:76
  25.6 5.2 %collective-permute-start.10 = (bf16[32,1024]{1,0:T(8,128)(2,1)S(1)}, bf16[32,1024]{1,0:T(8,128)(2,1)S(1)}, u32[]{:S(2)}, u32[]{:S(2)}) collective-permute-start(bf16[32,1024]{1,0:T(8,128)(2,1)S(1)} %get-tuple-element.73), channel_id=1, source_target_pairs={{0,6},{1,7},{2,4},{3,5},{4,2},{5,3},{6,0},{7,1},{8,14},{9,15},{10,... | collective-permute-start | bytes 196616 | tf_op jit(solution)/shard_map/ppermute | solution.py:76
  31.7 5.8 %collective-permute-start.15 = (bf16[16,2048]{1,0:T(8,128)(2,1)S(1)}, bf16[16,2048]{1,0:T(8,128)(2,1)S(1)}, u32[]{:S(2)}, u32[]{:S(2)}) collective-permute-start(bf16[16,2048]{1,0:T(8,128)(2,1)S(1)} %get-tuple-element.83), channel_id=1, source_target_pairs={{0,3},{1,2},{2,1},{3,0},{4,7},{5,6},{6,5},{7,4},{8,11},{9,10},{10,... | collective-permute-start | bytes 196616 | tf_op jit(solution)/shard_map/ppermute | solution.py:76
  31.9 7.2 %collective-permute-start.16 = (bf16[16,2048]{1,0:T(8,128)(2,1)S(1)}, bf16[16,2048]{1,0:T(8,128)(2,1)S(1)}, u32[]{:S(2)}, u32[]{:S(2)}) collective-permute-start(bf16[16,2048]{1,0:T(8,128)(2,1)S(1)} %get-tuple-element.84), channel_id=1, source_target_pairs={{0,5},{1,4},{2,7},{3,6},{4,1},{5,0},{6,3},{7,2},{8,13},{9,12},{10,... | collective-permute-start | bytes 196616 | tf_op jit(solution)/shard_map/ppermute | solution.py:76
  33.6 5.4 %collective-permute-start.17 = (bf16[16,2048]{1,0:T(8,128)(2,1)S(1)}, bf16[16,2048]{1,0:T(8,128)(2,1)S(1)}, u32[]{:S(2)}, u32[]{:S(2)}) collective-permute-start(bf16[16,2048]{1,0:T(8,128)(2,1)S(1)} %get-tuple-element.85), channel_id=1, source_target_pairs={{0,6},{1,7},{2,4},{3,5},{4,2},{5,3},{6,0},{7,1},{8,14},{9,15},{10,... | collective-permute-start | bytes 196616 | tf_op jit(solution)/shard_map/ppermute | solution.py:76
  35.7 10.1 %collective-permute-start.12 = (bf16[32,2048]{1,0:T(8,128)(2,1)S(1)}, bf16[32,2048]{1,0:T(8,128)(2,1)S(1)}, u32[]{:S(2)}, u32[]{:S(2)}) collective-permute-start(bf16[32,2048]{1,0:T(8,128)(2,1)S(1)} %get-tuple-element.79), channel_id=1, source_target_pairs={{0,3},{1,2},{2,1},{3,0},{4,7},{5,6},{6,5},{7,4},{8,11},{9,10},{10,... | collective-permute-start | bytes 393224 | tf_op jit(solution)/shard_map/ppermute | solution.py:76
  35.8 11.4 %collective-permute-start.13 = (bf16[32,2048]{1,0:T(8,128)(2,1)S(1)}, bf16[32,2048]{1,0:T(8,128)(2,1)S(1)}, u32[]{:S(2)}, u32[]{:S(2)}) collective-permute-start(bf16[32,2048]{1,0:T(8,128)(2,1)S(1)} %get-tuple-element.80), channel_id=1, source_target_pairs={{0,5},{1,4},{2,7},{3,6},{4,1},{5,0},{6,3},{7,2},{8,13},{9,12},{10,... | collective-permute-start | bytes 393224 | tf_op jit(solution)/shard_map/ppermute | solution.py:76
  37.6 9.6 %collective-permute-start.14 = (bf16[32,2048]{1,0:T(8,128)(2,1)S(1)}, bf16[32,2048]{1,0:T(8,128)(2,1)S(1)}, u32[]{:S(2)}, u32[]{:S(2)}) collective-permute-start(bf16[32,2048]{1,0:T(8,128)(2,1)S(1)} %get-tuple-element.81), channel_id=1, source_target_pairs={{0,6},{1,7},{2,4},{3,5},{4,2},{5,3},{6,0},{7,1},{8,14},{9,15},{10,... | collective-permute-start | bytes 393224 | tf_op jit(solution)/shard_map/ppermute | solution.py:76
  39.2 1.3 %collective-permute-start.18 = (bf16[8,2048]{1,0:T(8,128)(2,1)S(1)}, bf16[8,2048]{1,0:T(8,128)(2,1)S(1)}, u32[]{:S(2)}, u32[]{:S(2)}) collective-permute-start(bf16[8,2048]{1,0:T(8,128)(2,1)S(1)} %get-tuple-element.89), channel_id=1, source_target_pairs={{0,1},{1,0},{2,3},{3,2},{4,5},{5,4},{6,7},{7,6},{8,9},{9,8},{10,11... | collective-permute-start | bytes 98312 | tf_op jit(solution)/shard_map/ppermute | solution.py:76
  42.6 1.2 %collective-permute-start.19 = (bf16[8,2048]{1,0:T(8,128)(2,1)S(1)}, bf16[8,2048]{1,0:T(8,128)(2,1)S(1)}, u32[]{:S(2)}, u32[]{:S(2)}) collective-permute-start(bf16[8,2048]{1,0:T(8,128)(2,1)S(1)} %get-tuple-element.93), channel_id=1, source_target_pairs={{0,1},{1,0},{2,3},{3,2},{4,5},{5,4},{6,7},{7,6},{8,9},{9,8},{10,11... | collective-permute-start | bytes 98312 | tf_op jit(solution)/shard_map/ppermute | solution.py:76
  43.9 3.4 %collective-permute-start.20 = (bf16[4,2048]{1,0:T(4,128)(2,1)S(1)}, bf16[4,2048]{1,0:T(4,128)(2,1)S(1)}, u32[]{:S(2)}, u32[]{:S(2)}) collective-permute-start(bf16[4,2048]{1,0:T(4,128)(2,1)S(1)} %get-tuple-element.96), channel_id=1, source_target_pairs={{0,3},{1,2},{2,1},{3,0},{4,7},{5,6},{6,5},{7,4},{8,11},{9,10},{10,... | collective-permute-start | bytes 49160 | tf_op jit(solution)/shard_map/ppermute | solution.py:76
  44.2 3.2 %collective-permute-start.21 = (bf16[4,2048]{1,0:T(4,128)(2,1)S(1)}, bf16[4,2048]{1,0:T(4,128)(2,1)S(1)}, u32[]{:S(2)}, u32[]{:S(2)}) collective-permute-start(bf16[4,2048]{1,0:T(4,128)(2,1)S(1)} %get-tuple-element.97), channel_id=1, source_target_pairs={{0,5},{1,4},{2,7},{3,6},{4,1},{5,0},{6,3},{7,2},{8,13},{9,12},{10,... | collective-permute-start | bytes 49160 | tf_op jit(solution)/shard_map/ppermute | solution.py:76
  45.8 4.6 %collective-permute-start.22 = (bf16[4,2048]{1,0:T(4,128)(2,1)S(1)}, bf16[4,2048]{1,0:T(4,128)(2,1)S(1)}, u32[]{:S(2)}, u32[]{:S(2)}) collective-permute-start(bf16[4,2048]{1,0:T(4,128)(2,1)S(1)} %get-tuple-element.98), channel_id=1, source_target_pairs={{0,6},{1,7},{2,4},{3,5},{4,2},{5,3},{6,0},{7,1},{8,14},{9,15},{10,... | collective-permute-start | bytes 49160 | tf_op jit(solution)/shard_map/ppermute | solution.py:76

commit v5 on v3

--- a/solution.py
+++ b/solution.py
@@ -84,76 +84,74 @@
     return -(-(WIN + 2 * (path_len - 1) + 16) // 16) * 16
 
 
-def prep_kernel(path_len, n_weights, *refs):
+def prep_kernel(path_len, per_chip, n_weights, *refs):
     key_cache, value_cache, prefix_ref, accepted_ref, kind_ref = refs[:5]
-    small_in = refs[5:10]
-    sources = refs[10 : 10 + n_weights]
-    refs = refs[10 + n_weights :]
-    keys_ref, values_ref, mask_ref, rot_ref = refs[:4]
-    targets = refs[4 : 4 + n_weights]
-    refs = refs[4 + n_weights :]
-    path_ref, parents_ref, freq_ref, q_gain_ref, k_gain_ref = refs[:5]
-    small_sems, cache_sems, weight_sems = refs[5:]
-
-    new = mask_ref.shape[0]
-    kv_heads, span, head = keys_ref.shape
-    cache_len = key_cache.shape[1]
+    small_in = refs[5:7]
+    sources = refs[7 : 7 + n_weights]
+    refs = refs[7 + n_weights :]
+    chips = len(refs) - 5 - n_weights
+    outs = refs[:chips]
+    targets = refs[chips : chips + n_weights]
+    path_ref, parents_ref, small_sems, cache_sems, weight_sems = refs[chips + n_weights :]
+
+    new = parents_ref.shape[1]
+    cache_len, kv_width = key_cache.shape[1:]
+    head = outs[0].shape[1]
+    group = chips * per_chip // (kv_width // head)
     wide = window_rows(path_len)
-    sink_at, win_at = new, new + 16
-    end = win_at + wide
+    kept = wide + 16
+    chip = lax.axis_index("tensor") // 2
 
     small = [
         pltpu.make_async_copy(source, target, small_sems.at[which])
-        for which, (source, target) in enumerate(zip(small_in, refs[:5]))
+        for which, (source, target) in enumerate(zip(small_in, (path_ref, parents_ref)))
     ]
     for copy in small:
         copy.start()
-    copies = [
-        pltpu.make_async_copy(source, target, weight_sems.at[which])
-        for which, (source, target) in enumerate(zip(sources, targets))
-    ]
     prefix = prefix_ref[0]
     accepted = accepted_ref[0]
     total = prefix + accepted
     low = jnp.maximum(total - WIN, 0)
     start = pl.multiple_of(jnp.minimum((low // 16) * 16, cache_len - wide), 16)
-    for which, (cache, buf) in enumerate(((key_cache, keys_ref), (value_cache, values_ref))):
-        for kv in range(kv_heads):
-            cols = pl.ds(kv * head, head)
+    copies = []
+    for j in range(chips):
+        at = pl.multiple_of((chip ^ j) * per_chip // group * head, head)
+        for which, cache in enumerate((key_cache, value_cache)):
+            base = which * kept
             copies.append(
                 pltpu.make_async_copy(
-                    cache.at[0, pl.ds(start, wide), cols],
-                    buf.at[kv, pl.ds(win_at, wide)],
-                    cache_sems.at[which, kv, 0],
+                    cache.at[0, pl.ds(start, wide), pl.ds(at, head)],
+                    outs[j].at[pl.ds(base, wide)],
+                    cache_sems.at[which, j, 0],
                 )
             )
             copies.append(
                 pltpu.make_async_copy(
-                    cache.at[0, pl.ds(0, 16), cols],
-                    buf.at[kv, pl.ds(sink_at, 16)],
-                    cache_sems.at[which, kv, 1],
+                    cache.at[0, pl.ds(0, 16), pl.ds(at, head)],
+                    outs[j].at[pl.ds(base + wide, 16)],
+                    cache_sems.at[which, j, 1],
                 )
             )
+    for which, (source, target) in enumerate(zip(sources, targets)):
+        copies.append(pltpu.make_async_copy(source, target, weight_sems.at[which]))
     for copy in copies:
         copy.start()
 
-    for buf in (keys_ref, values_ref):
-        buf[:, 0:new, :] = jnp.zeros((kv_heads, new, head), BF16)
-        buf[:, end:span, :] = jnp.zeros((kv_heads, span - end, head), BF16)
-
     for copy in small:
         copy.wait()
+    span = -(-(new + kept) // head) * head
     column = iota((1, span), 1)
-    row = jnp.where(column < win_at, column - sink_at, start + column - win_at)
+    sink_at = new + wide
+    row = jnp.where(column < sink_at, start + column - new, column - sink_at)
     taken = jnp.zeros((1, span), jnp.bool_)
-    for step in range(path_len):
-        at = prefix + path_ref[0, step]
-        taken = taken | ((row == at) & (step < accepted))
+    for place in range(path_len):
+        at = prefix + path_ref[0, place]
+        taken = taken | ((row == at) & (place < accepted))
     old = (row < prefix) & ((row < SINK) | (row >= total - WIN))
-    in_window = (column >= win_at) & (column < end) & (old | taken)
-    in_sink = (column >= sink_at) & (column < win_at) & (row < SINK) & (row < prefix) & (start > 0)
-    seen = jnp.where(in_window | in_sink, 0.0, NEG_FILL)
-    mask_ref[...] = jnp.broadcast_to(seen, mask_ref.shape)
+    in_window = (column >= new) & (column < sink_at) & (old | taken)
+    in_sink = (column >= sink_at) & (column < sink_at + 16)
+    in_sink = in_sink & (row < SINK) & (row < prefix) & (start > 0)
+    seen = jnp.where(in_window | in_sink, 1.0, 0.0)
 
     down, across = iota((new, new), 0), iota((new, new), 1)
     eye = (down == across).astype(F32)
@@ -165,17 +163,20 @@
     tree = (kind_ref[0] == 1).astype(F32)
     causal = (across <= down).astype(F32)
     allowed = tree * reach + (1.0 - tree) * causal
-    mask_ref[:, 0:new] = jnp.where(allowed > 0.5, 0.0, NEG_FILL)
     depth = tree * (jnp.sum(reach, axis=1, keepdims=True) - 1.0)
     depth = depth + (1.0 - tree) * iota((new, 1), 0).astype(F32)
-    angle = (total.astype(F32) + depth) * freq_ref[...]
-    lane = iota(angle.shape, 1)
-    cosine, sine = jnp.cos(angle), jnp.sin(angle)
-    sine = jnp.where(lane < head // 2, -sine, sine)
-    for which, gain_ref in enumerate((q_gain_ref, k_gain_ref)):
-        gain = jnp.broadcast_to(gain_ref[...], angle.shape)
-        rot_ref[2 * which] = cosine * gain
-        rot_ref[2 * which + 1] = sine * pltpu.roll(gain, head // 2, 1)
+    position = total.astype(F32) + depth
+    high = jnp.floor(position * (1.0 / 128.0))
+    lane = iota((new, head), 1)
+    spread = (iota((new, head), 0) == lane).astype(F32)
+    facts = dot(allowed.astype(BF16), spread.astype(BF16))
+    facts = facts + jnp.where(lane == new, high, 0.0)
+    facts = facts + jnp.where(lane == new + 1, position - 128.0 * high, 0.0)
+    lines = [facts] + [seen[:, at : at + head] for at in range(0, span, head)]
+    lines.append(jnp.zeros((16 - span // head, head), F32))
+    facts = jnp.concatenate(lines, axis=0).astype(BF16)
+    for j in range(chips):
+        outs[j][2 * kept : 2 * kept + new + 16, :] = facts
     for copy in copies:
         copy.wait()
 
@@ -254,63 +255,92 @@
         copy.wait()
 
 
-def project_kernel(count, *refs):
-    blocks = refs[:count]
-    gain_ref, wq_ref, wkv_ref, wq_sib, wkv_sib = refs[count : count + 5]
-    outs = refs[count + 5 :]
+def project_kernel(chips, pairs, *refs):
+    blocks = refs[:chips]
+    gain_ref, wq_ref, wkv_ref, wq_sib, wkv_sib = refs[chips : chips + 5]
+    outs = refs[chips + 5 : 2 * chips + 5]
+    sent = refs[2 * chips + 5 :]
+    me = lax.axis_index("tensor")
+    chip = me // 2
     rows = blocks[0].shape[0]
     gain = gain_ref[...]
     values = [(norm_rows(block[...].astype(F32)) * gain).astype(BF16) for block in blocks]
     values = jnp.concatenate(values, axis=0)
-
-    def put(result, at):
-        result = result.astype(BF16)
-        for j in range(count):
-            outs[j][:, at : at + result.shape[1]] = result[j * rows : (j + 1) * rows]
-
-    wide, narrow = wq_ref.shape[1], wkv_ref.shape[0]
-    put(dot(values, wq_ref[...]), 0)
-    put(dot(values, wq_sib[...]), wide)
-    put(dot_last(values, wkv_ref[...]), 2 * wide)
-    put(dot_last(values, wkv_sib[...]), 2 * wide + narrow)
-
-
-def attend_kernel(chips, q_width, kv_ready, *refs):
-    got = refs[:chips]
-    at = chips + 1 if kv_ready else chips
-    keys_ref, values_ref, mask_ref, rot_ref = refs[at : at + 4]
-    outs = refs[at + 5 : at + 5 + chips]
-    fresh_ref = refs[chips] if kv_ready else refs[-1]
-    me = lax.axis_index("tensor")
-    chip = me // 2
-    new = got[0].shape[0]
-    kv_heads, span, head = keys_ref.shape
-    per_chip = 2 * q_width // head
-    group = chips * per_chip // kv_heads
-
-    if not kv_ready:
-        for rel in range(2 * chips):
-            left = 2 * q_width + (rel % 2) * head
-            fresh_ref[step(rel // 2) ^ (rel % 2)] = got[rel // 2][:, left : left + head]
-
-    def rope(values, which):
-        values = norm_rows(values.astype(F32))
-        turned = pltpu.roll(values, head // 2, 1)
-        return (values * rot_ref[2 * which] + turned * rot_ref[2 * which + 1]).astype(BF16)
-
+    wide = wq_ref.shape[1]
+    for which, w_ref in enumerate((wq_ref, wq_sib)):
+        result = dot(values, w_ref[...]).astype(BF16)
+        for j in range(chips):
+            outs[j][:, which * wide : (which + 1) * wide] = result[j * rows : (j + 1) * rows]
+    first, second = dot_last(values, wkv_ref[...]), dot_last(values, wkv_sib[...])
+    turn = me % 2 == 1
+    if pairs:
+        turn = turn ^ ((chip == 0) | (chip == chips - 1))
+    lower, upper = jnp.where(turn, second, first), jnp.where(turn, first, second)
+    narrow = lower.shape[1]
+    for which, part in enumerate((lower.astype(BF16), upper.astype(BF16))):
+        for j in range(chips):
+            block = part[j * rows : (j + 1) * rows]
+            if pairs:
+                sent[which][chip ^ j] = block
+            else:
+                sent[0][chip ^ j, :, which * narrow : (which + 1) * narrow] = block
+
+
+def hold_kernel(*_):
+    pass
+
+
+def fresh_kernel(one_ref, two_ref, key_ref, value_ref):
+    chip = lax.axis_index("tensor") // 2
+    turn = (chip == 0) | (chip == one_ref.shape[0] - 1)
+    one, two = one_ref[...].astype(F32), two_ref[...].astype(F32)
+    key_ref[...] = jnp.where(turn, two, one).astype(BF16)
+    value_ref[...] = jnp.where(turn, one, two).astype(BF16)
+
+
+def attend_kernel(chips, *refs):
+    queries = refs[:chips]
+    caches = refs[chips : 2 * chips]
+    key_ref, value_ref, freq_ref, q_gain_ref, k_gain_ref = refs[2 * chips : 2 * chips + 5]
+    outs = refs[-chips:]
+    chip = lax.axis_index("tensor") // 2
+    new, wide = queries[0].shape
+    head = key_ref.shape[2]
+    per_chip = wide // head
+    kept = (caches[0].shape[0] - new - 16) // 2
+    span = -(-(new + kept) // head) * head
+    empty = jnp.zeros((span - new - kept, head), BF16)
+    lane = iota((new, head), 1)
     scale = head ** (-0.5) * LOG2E
     for j in range(chips):
-        kv = (chip ^ j) * per_chip // group
-        key_at, value_at = kv, kv + kv_heads
-        if not kv_ready:
-            key_at, value_at = me ^ key_at, me ^ value_at
-        keys = jnp.concatenate([rope(fresh_ref[key_at], 1), keys_ref[kv, new:span]], axis=0)
-        values = jnp.concatenate([fresh_ref[value_at], values_ref[kv, new:span]], axis=0)
+        facts = caches[j][2 * kept : 2 * kept + new + 16, :].astype(F32)
+        own = facts[:new]
+        high = jnp.sum(jnp.where(lane == new, own, 0.0), axis=1, keepdims=True)
+        rest = jnp.sum(jnp.where(lane == new + 1, own, 0.0), axis=1, keepdims=True)
+        angle = (128.0 * high + rest) * freq_ref[...]
+        cosine, sine = jnp.cos(angle), jnp.sin(angle)
+        sine = jnp.where(lane < head // 2, -sine, sine)
+
+        def rope(values, gain_ref):
+            values = norm_rows(values.astype(F32)) * gain_ref[...]
+            return (values * cosine + pltpu.roll(values, head // 2, 1) * sine).astype(BF16)
+
+        masks = []
+        for at in range(span // head):
+            seen = jnp.broadcast_to(facts[new + at : new + at + 1], (new, head))
+            if at == 0:
+                seen = jnp.where(lane < new, own, seen)
+            masks.append(jnp.where(seen > 0.5, 0.0, NEG_FILL))
+        mask = jnp.concatenate(masks, axis=1)
+        key = rope(key_ref[chip ^ j], k_gain_ref)
+        keys = jnp.concatenate([key, caches[j][0:kept, :], empty], axis=0)
+        values = jnp.concatenate([value_ref[chip ^ j], caches[j][kept : 2 * kept, :], empty], axis=0)
         query = jnp.concatenate(
-            [rope(got[j][:, h * head : (h + 1) * head], 0) for h in range(per_chip)], axis=0
+            [rope(queries[j][:, h * head : (h + 1) * head], q_gain_ref) for h in range(per_chip)],
+            axis=0,
         )
         score = dot_last(query, keys) * scale
-        score = score.reshape(per_chip, new, span) + mask_ref[...][None]
+        score = score.reshape(per_chip, new, span) + mask[None]
         expo = jnp.exp2(score - jnp.max(score, axis=-1, keepdims=True))
         denom = jnp.sum(expo, axis=-1, keepdims=True).reshape(per_chip * new, 1)
         expo = expo.astype(BF16).reshape(per_chip * new, span)
@@ -451,18 +481,12 @@
 
     freq = ROPE_BASE ** (-2.0 * np.arange(head // 2) / head)
     freq = jnp.asarray(np.concatenate([freq, freq])[None, :], F32)
-    span = -(-(new + 16 + window_rows(path_len)) // 128) * 128
-    weights = [attn_gain[None, :], w_query, w_keyval]
-    keys, values, mask, rot, gain, wq, wkv = call(
-        functools.partial(prep_kernel, path_len, len(weights)),
+    length = 2 * (window_rows(path_len) + 16) + new + 16
+    weights = [attn_gain[None, :], query_gain[None, :], key_gain[None, :], freq, w_query, w_keyval]
+    prepared = call(
+        functools.partial(prep_kernel, path_len, 2 * q_width // head, len(weights)),
         "prep",
-        [
-            in_vmem((kv_heads, span, head), BF16),
-            in_vmem((kv_heads, span, head), BF16),
-            in_vmem((new, span), F32),
-            in_vmem((4, new, head), F32),
-        ]
-        + [in_vmem(w.shape, w.dtype) for w in weights],
+        [in_vmem((length, head), BF16)] * chips + [in_vmem(w.shape, w.dtype) for w in weights],
         [
             (key_cache, hbm),
             (value_cache, hbm),
@@ -471,36 +495,36 @@
             (slot_kinds, smem),
             (accept_path, hbm),
             (parents, hbm),
-            (freq, hbm),
-            (query_gain[None, :], hbm),
-            (key_gain[None, :], hbm),
         ]
         + [(w, hbm) for w in weights],
         [
             pltpu.SMEM((1, path_len), jnp.int32),
             pltpu.VMEM((1, new), jnp.int32),
-            pltpu.VMEM((1, head), F32),
-            pltpu.VMEM((1, head), F32),
-            pltpu.VMEM((1, head), F32),
-            pltpu.SemaphoreType.DMA((5,)),
-            pltpu.SemaphoreType.DMA((2, kv_heads, 2)),
+            pltpu.SemaphoreType.DMA((2,)),
+            pltpu.SemaphoreType.DMA((2, chips, 2)),
             pltpu.SemaphoreType.DMA((len(weights),)),
         ],
         limit=16,
-        moved=4 * span * kv_heads * head * 2,
-    )
-
+        moved=4 * chips * length * head,
+    )
+    gain, q_gain, k_gain, freq, wq, wkv = prepared[chips:]
+    caches = exchange(prepared[:chips])
+
+    pairs = new_width == head and chips == 4
+    if pairs:
+        sent = [in_vmem((chips, new, head), BF16)] * 2
+    else:
+        sent = [in_vmem((chips, new, 2 * new_width), BF16)]
     projected = call(
-        functools.partial(project_kernel, chips),
+        functools.partial(project_kernel, chips, pairs),
         "project",
-        [in_vmem((new, 2 * (q_width + new_width)), BF16)] * chips,
+        [in_vmem((new, 2 * q_width), BF16)] * chips + sent,
         [(block, vmem) for block in blocks]
         + [(w, vmem) for w in (gain, wq, wkv, wq_sib, wkv_sib)],
         limit=16,
-        flops=4 * tokens * width * (q_width + new_width),
-        moved=4 * width * (q_width + new_width),
-    )
-    got = exchange(projected)
+    )
+    queries, sent = projected[:chips], projected[chips:]
+    wo_sib = hop(w_out, 1)
 
     weights = [ffn_gain[None, :], w_out, w_down]
     pick, combine, weight, ffn, wo, wd = call(
@@ -512,7 +536,7 @@
             in_vmem((rows, 128), F32),
         ]
         + [in_vmem(w.shape, w.dtype) for w in weights],
-        [(projected[0], anywhere), (expert_ids.T, hbm), (gate_probs.T, hbm)]
+        [(queries[0], anywhere), (expert_ids.T, hbm), (gate_probs.T, hbm)]
         + [(w, hbm) for w in weights],
         [
             pltpu.VMEM((top, all_tokens), jnp.int32),
@@ -523,43 +547,55 @@
             pltpu.SemaphoreType.DMA((2 + len(weights),)),
         ],
         limit=16,
-        moved=4 * width * (q_width + w_down.shape[1]),
-    )
-    kv_ready = []
-    if new_width != head:
-        pieces = [None] * devices
-        for rel in range(devices):
-            left = 2 * q_width + (rel % 2) * new_width
-            pieces[step(rel // 2) ^ (rel % 2)] = got[rel // 2][:, left : left + new_width]
-        pieces = jnp.stack(pieces)[lax.axis_index("tensor") ^ jnp.arange(devices)]
-        pieces = pieces.transpose(1, 0, 2).reshape(new, 2 * kv_heads, head)
-        kv_ready = [(pieces.transpose(1, 0, 2), vmem)]
-    *attended, wo = call(
-        functools.partial(attend_kernel, chips, q_width, bool(kv_ready)),
-        "attend",
-        [in_vmem((new, 2 * q_width), BF16)] * chips + [in_vmem(wo.shape, wo.dtype)],
-        [(block, vmem) for block in got]
-        + kv_ready
-        + [(keys, vmem), (values, vmem), (mask, vmem), (rot, vmem)]
-        + [(wo, vmem)],
-        [] if kv_ready else [pltpu.VMEM((devices, new, head), BF16)],
-        limit=16,
-        same={chips + len(kv_ready) + 4: chips},
-        flops=8 * new * chips * q_width * span,
-        moved=4 * span * kv_heads * head,
-    )
-    wo_sib = hop(wo, 1)
-    heads = exchange(attended)
+    )
+    if pairs:
+        routes = ([(0, 1), (1, 2), (2, 0), (3, 3)], [(0, 0), (1, 3), (2, 1), (3, 2)])
+        came = []
+        second = call(
+            hold_kernel,
+            "hold",
+            [in_vmem((chips, new, head), BF16)],
+            [(sent[1], vmem), (wo_sib, anywhere)],
+            limit=8,
+            same={0: 0},
+        )[0]
+        for part, route in zip((sent[0], second), routes):
+            links = [(step(p) ^ core, step(q) ^ core) for p, q in route for core in range(2)]
+            came.append(lax.ppermute(part, "tensor", links))
+        key_new, value_new = call(
+            fresh_kernel,
+            "fresh",
+            [in_vmem((chips, new, head), BF16)] * 2,
+            [(came[0], vmem), (came[1], vmem)],
+            limit=8,
+        )
+    else:
+        groups = [[step(p) ^ core for p in range(chips)] for core in range(2)]
+        every = lax.all_gather(sent[0], "tensor", axis_index_groups=groups)
+        every = every.transpose(1, 2, 0, 3).reshape(chips, new, 2 * kv_heads * head)
+        at = lax.axis_index("tensor") // 2 * kv_heads // chips * head
+        key_new = lax.dynamic_slice_in_dim(every, at, head, 2)
+        value_new = lax.dynamic_slice_in_dim(every, at + kv_heads * head, head, 2)
     picked, wg, wu = call(
         functools.partial(select_kernel, chips),
         "select",
         [in_vmem((rows, width), F32)] + [in_vmem(w.shape, w.dtype) for w in (w_gate, w_up)],
         [(block, vmem) for block in blocks]
-        + [(pick, vmem), (attended[0], anywhere), (w_gate, hbm), (w_up, hbm)],
+        + [(pick, vmem), (queries[0], anywhere), (w_gate, hbm), (w_up, hbm)],
         [pltpu.SemaphoreType.DMA((2,))],
         limit=8,
-        flops=2 * rows * width * tokens,
-        moved=8 * width * w_gate.shape[1],
+    )
+    heads = call(
+        functools.partial(attend_kernel, chips),
+        "attend",
+        [in_vmem((new, 2 * q_width), BF16)] * chips,
+        [(block, vmem) for block in queries]
+        + [(block, vmem) for block in caches]
+        + [(x, vmem) for x in (key_new, value_new, freq, q_gain, k_gain)]
+        + [(wg, anywhere)],
+        limit=16,
+        flops=8 * new * chips * q_width * length // 2,
+        moved=2 * chips * length * head,
     )
 
     def spread(name, each, more):

time: 50.1 us -> 55.1 us (1.100)
  starting transfers between devices: 21.4 us -> 25.1 us
  waiting for transfers between devices: 9.43 us -> 10.6 us
    ppermute x0 -> x2, starting transfers between devices: none -> 4.73 us  [body(): came.append(lax.ppermute(part, 'tensor', links))]
    ppermute x0 -> x2, waiting for transfers between devices: none -> 2.18 us  [body(): came.append(lax.ppermute(part, 'tensor', links))]
    ppermute x23 -> x20, waiting for transfers between devices: 9.43 us -> 8.43 us  [hop(): lax.ppermute(value, 'tensor', [(i, i ^ step) for i in range(devices)])]
    ppermute x23 -> x20, starting transfers between devices: 21.4 us -> 20.4 us  [hop(): lax.ppermute(value, 'tensor', [(i, i ^ step) for i in range(devices)])]
    pallas_call x12 -> x14, Pallas kernels: 17 us -> 17 us  [call(): pl.pallas_call(kernel, out_shape=outs, in_specs=specs, out_specs=[pl.Bloc...]
  transfers between devices with their start and end apart: 23 -> 22, of which waited for: 7 -> 6; matrix products, arithmetic and copies ran while one was open for 0% -> 0% of each run, Pallas kernels for 24% -> 24%
where the time goes in v5:
time: 55.1 us; the launch traced here: 54.9 us
  starting transfers between devices  25.1 us (46%)
  Pallas kernels  17 us (31%)
  waiting for transfers between devices  10.6 us (19%)
  between operations  2.12 us (4%)
    ppermute x20, starting transfers between devices, hop(): lax.ppermute(value, 'tensor', [(i, i ^ step) for i in range(devices)])  20.4 us
    pallas_call x14, Pallas kernels, call(): pl.pallas_call(kernel, out_shape=outs, in_specs=specs, out_specs=[pl.Bloc...  17 us
    ppermute x20, waiting for transfers between devices, hop(): lax.ppermute(value, 'tensor', [(i, i ^ step) for i in range(devices)])  8.43 us
    ppermute x2, starting transfers between devices, body(): came.append(lax.ppermute(part, 'tensor', links))  4.73 us
    ppermute x2, waiting for transfers between devices, body(): came.append(lax.ppermute(part, 'tensor', links))  2.18 us
  transfers between devices with their start and end apart: 22, of which 6 were waited for; matrix products, arithmetic and copies ran while one was open for 0% of the time, Pallas kernels for 24%

profile of v5, /device:TPU:0, one launch (start us, length us, event | category | flops | bytes accessed | tf_op | source)
XLA Modules:
  0.0 54.9 jit_solution(809749524430548835)
XLA Ops:
  0.0 0.5 collective-permute-start.3
  1.0 2.6 %collective-permute-start = (bf16[32,2048]{1,0:T(8,128)(2,1)}, bf16[32,2048]{1,0:T(8,128)(2,1)S(1)}, u32[]{:S(2)}, u32[]{:S(2)}) collective-permute-start(bf16[32,2048]{1,0:T(8,128)(2,1)} %refs_4_.4), channel_id=1, source_target_pairs={{0,3},{1,2},{2,1},{3,0},{4,7},{5,6},{6,5},{7,4},{8,11},{9,10},{10,... | collective-permute-start | bytes 393224 | tf_op jit(solution)/shard_map/ppermute | solution.py:76
  3.6 1.2 %collective-permute-start.1 = (bf16[32,2048]{1,0:T(8,128)(2,1)}, bf16[32,2048]{1,0:T(8,128)(2,1)S(1)}, u32[]{:S(2)}, u32[]{:S(2)}) collective-permute-start(bf16[32,2048]{1,0:T(8,128)(2,1)} %refs_4_.4), channel_id=1, source_target_pairs={{0,5},{1,4},{2,7},{3,6},{4,1},{5,0},{6,3},{7,2},{8,13},{9,12},{10,... | collective-permute-start | bytes 393224 | tf_op jit(solution)/shard_map/ppermute | solution.py:76
  4.8 2.8 %collective-permute-done.refs_1_ = bf16[32,2048]{1,0:T(8,128)(2,1)S(1)} collective-permute-done((bf16[32,2048]{1,0:T(8,128)(2,1)}, bf16[32,2048]{1,0:T(8,128)(2,1)S(1)}, u32[]{:S(2)}, u32[]{:S(2)}) %collective-permute-start) | collective-permute-done | bytes 131104 | tf_op jit(solution)/shard_map/ppermute | solution.py:76
  7.6 2.3 %collective-permute-start.2 = (bf16[32,2048]{1,0:T(8,128)(2,1)}, bf16[32,2048]{1,0:T(8,128)(2,1)S(1)}, u32[]{:S(2)}, u32[]{:S(2)}) collective-permute-start(bf16[32,2048]{1,0:T(8,128)(2,1)} %refs_4_.4), channel_id=1, source_target_pairs={{0,6},{1,7},{2,4},{3,5},{4,2},{5,3},{6,0},{7,1},{8,14},{9,15},{10,... | collective-permute-start | bytes 393224 | tf_op jit(solution)/shard_map/ppermute | solution.py:76
  11.8 3.1 %prep.1 = (bf16[1168,128]{1,0:T(8,128)(2,1)S(1)}, bf16[1168,128]{1,0:T(8,128)(2,1)S(1)}, bf16[1168,128]{1,0:T(8,128)(2,1)S(1)}, bf16[1168,128]{1,0:T(8,128)(2,1)...) custom-call(bf16[1,1024,512]{2,1,0:T(8,128)(2,1)} %refs_0_.3, ...), custom_call_target="tpu_custom_call" | custom-call | bytes 2392064 | tf_op jit(solution)/shard_map/prep/pallas_call | solution.py:61
  14.9 0.6 %collective-permute-start.5 = (bf16[1168,128]{1,0:T(8,128)(2,1)S(1)}, bf16[1168,128]{1,0:T(8,128)(2,1)S(1)}, u32[]{:S(2)}, u32[]{:S(2)}) collective-permute-start(bf16[1168,128]{1,0:T(8,128)(2,1)S(1)} %get-tuple-element.60), channel_id=1, source_target_pairs={{0,3},{1,2},{2,1},{3,0},{4,7},{5,6},{6,5},{7,4},{8,11},{9,10},{10,... | collective-permute-start | bytes 897032 | tf_op jit(solution)/shard_map/ppermute | solution.py:76
  15.9 2.3 %collective-permute-start.7 = (bf16[1168,128]{1,0:T(8,128)(2,1)S(1)}, bf16[1168,128]{1,0:T(8,128)(2,1)S(1)}, u32[]{:S(2)}, u32[]{:S(2)}) collective-permute-start(bf16[1168,128]{1,0:T(8,128)(2,1)S(1)} %get-tuple-element.62), channel_id=1, source_target_pairs={{0,6},{1,7},{2,4},{3,5},{4,2},{5,3},{6,0},{7,1},{8,14},{9,15},{10,... | collective-permute-start | bytes 897032 | tf_op jit(solution)/shard_map/ppermute | solution.py:76
  18.2 1.1 %project.1 = (bf16[32,1024]{1,0:T(8,128)(2,1)S(1)}, bf16[32,1024]{1,0:T(8,128)(2,1)S(1)}, bf16[32,1024]{1,0:T(8,128)(2,1)S(1)}, bf16[32,1024]{1,0:T(8,128)(2,1)S...) custom-call(bf16[32,2048]{1,0:T(8,128)(2,1)S(1)} %copy-done, ...), custom_call_target="tpu_custom_call" | custom-call | tf_op jit(solution)/shard_map/project/pallas_call | solution.py:61
  19.4 0.7 %collective-permute-start.10 = (bf16[4,32,128]{2,1,0:T(8,128)(2,1)S(1)}, bf16[4,32,128]{2,1,0:T(8,128)(2,1)S(1)}, u32[]{:S(2)}, u32[]{:S(2)}) collective-permute-start(bf16[4,32,128]{2,1,0:T(8,128)(2,1)S(1)} %hold.1), channel_id=1, source_target_pairs={{0,0},{1,1},{3,6},{2,7},{5,3},{4,2},{6,5},{7,4},{8,8},{9,9},{11,14... | collective-permute-start | bytes 98312 | tf_op jit(solution)/shard_map/ppermute | solution.py:564
  20.0 4.1 %collective-permute-start.8 = (bf16[4,32,128]{2,1,0:T(8,128)(2,1)S(1)}, bf16[4,32,128]{2,1,0:T(8,128)(2,1)S(1)}, u32[]{:S(2)}, u32[]{:S(2)}) collective-permute-start(bf16[4,32,128]{2,1,0:T(8,128)(2,1)S(1)} %get-tuple-element.63), channel_id=1, source_target_pairs={{0,3},{1,2},{3,5},{2,4},{5,0},{4,1},{6,6},{7,7},{8,11},{9,10},{11,... | collective-permute-start | bytes 98312 | tf_op jit(solution)/shard_map/ppermute | solution.py:564
  24.1 2.6 %route.1 = (f32[64,128]{1,0:T(8,128)S(1)}, f32[32,16]{1,0:T(8,128)S(1)}, f32[16,128]{1,0:T(8,128)S(1)}, f32[1,2048]{1,0:T(1,128)S(1)}, bf16[512,2048]{1,0:T(8,128)(2,1)S(1)}, /*index=5*/bf16[1,768,2048]{2,1,0:T(8,128)(2,1)S(1)}) custom-call(bf16[32,1024]{1,0:T(8,128)(2,1)S(1)} %get-tuple-element.55.refs_0_.refs_5_, s32[8,256]{1,0:T(8,128)} %bitcast.7, ...), custom_call_target="tpu_custom_call" | custom-call | tf_op jit(solution)/shard_map/route/pallas_call | solution.py:61
  26.7 2.9 %select.1 = (f32[16,2048]{1,0:T(8,128)S(1)}, bf16[1,768,2048]{2,1,0:T(8,128)(2,1)S(1)}, bf16[1,768,2048]{2,1,0:T(8,128)(2,1)S(1)}) custom-call(bf16[32,2048]{1,0:T(8,128)(2,1)S(1)} %copy-done, bf16[32,2048]{1,0:T(8,128)(2,1)S(1)} %collective-permute-done.refs_1_, bf16[32,2048]{1,0:T(8,128)(2,1)S(1)} %collective-permute-done.1.refs_2_, ...), custom_call_target="tpu_custom_call" | custom-call | tf_op jit(solution)/shard_map/select/pallas_call | solution.py:61
  29.6 2.2 %collective-permute-done.8.one_ref = bf16[4,32,128]{2,1,0:T(8,128)(2,1)S(1)} collective-permute-done((bf16[4,32,128]{2,1,0:T(8,128)(2,1)S(1)}, bf16[4,32,128]{2,1,0:T(8,128)(2,1)S(1)}, u32[]{:S(2)}, u32[]{:S(2)}) %collective-permute-start.8) | collective-permute-done | bytes 32800 | tf_op jit(solution)/shard_map/ppermute | solution.py:564
  31.8 2.3 %attend.1 = (bf16[32,1024]{1,0:T(8,128)(2,1)S(1)}, bf16[32,1024]{1,0:T(8,128)(2,1)S(1)}, bf16[32,1024]{1,0:T(8,128)(2,1)S(1)}, bf16[32,1024]{1,0:T(8,128)(2,1)S(1)}) custom-call(bf16[32,1024]{1,0:T(8,128)(2,1)S(1)} %get-tuple-element.55.refs_0_.refs_5_, bf16[32,1024]{1,0:T(8,128)(2,1)S(1)} %get-tuple-element.56.refs_1_, ...), custom_call_target="tpu_custom_call" | custom-call | flops 306184192 | bytes 1196032 | tf_op jit(solution)/shard_map/attend/pallas_call | solution.py:61
  34.1 1.0 %experts.1 = (bf16[16,2048]{1,0:T(8,128)(2,1)S(1)}, bf16[16,2048]{1,0:T(8,128)(2,1)S(1)}, bf16[16,2048]{1,0:T(8,128)(2,1)S(1)}, bf16[16,2048]{1,0:T(8,128)(2,1)S(1)}) custom-call(bf16[32,1024]{1,0:T(8,128)(2,1)S(1)} %get-tuple-element.72.refs_0_, bf16[32,1024]{1,0:T(8,128)(2,1)S(1)} %get-tuple-element.73.refs_1_, ...), custom_call_target="tpu_custom_call" | custom-call | flops 268435456 | bytes 4194304 | tf_op jit(solution)/shard_map/experts/pallas_call | solution.py:61
  35.1 1.2 %collective-permute-start.14 = (bf16[16,2048]{1,0:T(8,128)(2,1)S(1)}, bf16[16,2048]{1,0:T(8,128)(2,1)S(1)}, u32[]{:S(2)}, u32[]{:S(2)}) collective-permute-start(bf16[16,2048]{1,0:T(8,128)(2,1)S(1)} %get-tuple-element.83), channel_id=1, source_target_pairs={{0,3},{1,2},{2,1},{3,0},{4,7},{5,6},{6,5},{7,4},{8,11},{9,10},{10,... | collective-permute-start | bytes 196616 | tf_op jit(solution)/shard_map/ppermute | solution.py:76
  36.4 0.8 %collective-permute-start.15 = (bf16[16,2048]{1,0:T(8,128)(2,1)S(1)}, bf16[16,2048]{1,0:T(8,128)(2,1)S(1)}, u32[]{:S(2)}, u32[]{:S(2)}) collective-permute-start(bf16[16,2048]{1,0:T(8,128)(2,1)S(1)} %get-tuple-element.84), channel_id=1, source_target_pairs={{0,5},{1,4},{2,7},{3,6},{4,1},{5,0},{6,3},{7,2},{8,13},{9,12},{10,... | collective-permute-start | bytes 196616 | tf_op jit(solution)/shard_map/ppermute | solution.py:76
  37.2 1.2 %collective-permute-start.16 = (bf16[16,2048]{1,0:T(8,128)(2,1)S(1)}, bf16[16,2048]{1,0:T(8,128)(2,1)S(1)}, u32[]{:S(2)}, u32[]{:S(2)}) collective-permute-start(bf16[16,2048]{1,0:T(8,128)(2,1)S(1)} %get-tuple-element.85), channel_id=1, source_target_pairs={{0,6},{1,7},{2,4},{3,5},{4,2},{5,3},{6,0},{7,1},{8,14},{9,15},{10,... | collective-permute-start | bytes 196616 | tf_op jit(solution)/shard_map/ppermute | solution.py:76
  38.4 0.7 %slots.1 = (bf16[32,2048]{1,0:T(8,128)(2,1)S(1)}, bf16[32,2048]{1,0:T(8,128)(2,1)S(1)}, bf16[32,2048]{1,0:T(8,128)(2,1)S(1)}, bf16[32,2048]{1,0:T(8,128)(2,1)S(1)}) custom-call(bf16[32,1024]{1,0:T(8,128)(2,1)S(1)} %get-tuple-element.72.refs_0_, bf16[32,1024]{1,0:T(8,128)(2,1)S(1)} %get-tuple-element.73.refs_1_, ...), custom_call_target="tpu_custom_call" | custom-call | flops 536870912 | bytes 4194304 | tf_op jit(solution)/shard_map/slots/pallas_call | solution.py:61
  39.1 0.9 %collective-permute-start.11 = (bf16[32,2048]{1,0:T(8,128)(2,1)S(1)}, bf16[32,2048]{1,0:T(8,128)(2,1)S(1)}, u32[]{:S(2)}, u32[]{:S(2)}) collective-permute-start(bf16[32,2048]{1,0:T(8,128)(2,1)S(1)} %get-tuple-element.79), channel_id=1, source_target_pairs={{0,3},{1,2},{2,1},{3,0},{4,7},{5,6},{6,5},{7,4},{8,11},{9,10},{10,... | collective-permute-start | bytes 393224 | tf_op jit(solution)/shard_map/ppermute | solution.py:76
  40.1 1.1 %collective-permute-start.12 = (bf16[32,2048]{1,0:T(8,128)(2,1)S(1)}, bf16[32,2048]{1,0:T(8,128)(2,1)S(1)}, u32[]{:S(2)}, u32[]{:S(2)}) collective-permute-start(bf16[32,2048]{1,0:T(8,128)(2,1)S(1)} %get-tuple-element.80), channel_id=1, source_target_pairs={{0,5},{1,4},{2,7},{3,6},{4,1},{5,0},{6,3},{7,2},{8,13},{9,12},{10,... | collective-permute-start | bytes 393224 | tf_op jit(solution)/shard_map/ppermute | solution.py:76
  41.2 1.2 %collective-permute-start.13 = (bf16[32,2048]{1,0:T(8,128)(2,1)S(1)}, bf16[32,2048]{1,0:T(8,128)(2,1)S(1)}, u32[]{:S(2)}, u32[]{:S(2)}) collective-permute-start(bf16[32,2048]{1,0:T(8,128)(2,1)S(1)} %get-tuple-element.81), channel_id=1, source_target_pairs={{0,6},{1,7},{2,4},{3,5},{4,2},{5,3},{6,0},{7,1},{8,14},{9,15},{10,... | collective-permute-start | bytes 393224 | tf_op jit(solution)/shard_map/ppermute | solution.py:76
  42.6 1.2 %collective-permute-done.17.other_ref = bf16[8,2048]{1,0:T(8,128)(2,1)S(1)} collective-permute-done((bf16[8,2048]{1,0:T(8,128)(2,1)S(1)}, bf16[8,2048]{1,0:T(8,128)(2,1)S(1)}, u32[]{:S(2)}, u32[]{:S(2)}) %collective-permute-start.17) | collective-permute-done | bytes 32800 | tf_op jit(solution)/shard_map/ppermute | solution.py:76
  43.8 2.2 %expert.1 = (f32[8,2048]{1,0:T(8,128)S(1)}, bf16[8,2048]{1,0:T(8,128)(2,1)S(1)}) custom-call(bf16[8,2048]{1,0:T(8,128)(2,1)S(1)} %get-tuple-element.88.own_ref, bf16[8,2048]{1,0:T(8,128)(2,1)S(1)} %collective-permute-done.17.other_ref, bf16[1,768,2048]{2,1,0:T(8,128)(2,1)S(1)} %get-tuple-element.71.refs_13_.refs_7_.gate_ref, ...), custom_call_target="tpu_custom_call" | custom-call | flops 150994944 | bytes 9437184 | tf_op jit(solution)/shard_map/expert/pallas_call | solution.py:61
  46.2 1.0 %collective-permute-done.18.other_ref = bf16[8,2048]{1,0:T(8,128)(2,1)S(1)} collective-permute-done((bf16[8,2048]{1,0:T(8,128)(2,1)S(1)}, bf16[8,2048]{1,0:T(8,128)(2,1)S(1)}, u32[]{:S(2)}, u32[]{:S(2)}) %collective-permute-start.18) | collective-permute-done | bytes 32800 | tf_op jit(solution)/shard_map/ppermute | solution.py:76
  47.4 1.3 %collective-permute-start.19 = (bf16[4,2048]{1,0:T(4,128)(2,1)S(1)}, bf16[4,2048]{1,0:T(4,128)(2,1)S(1)}, u32[]{:S(2)}, u32[]{:S(2)}) collective-permute-start(bf16[4,2048]{1,0:T(4,128)(2,1)S(1)} %get-tuple-element.96), channel_id=1, source_target_pairs={{0,3},{1,2},{2,1},{3,0},{4,7},{5,6},{6,5},{7,4},{8,11},{9,10},{10,... | collective-permute-start | bytes 49160 | tf_op jit(solution)/shard_map/ppermute | solution.py:76
  48.7 0.8 %collective-permute-start.20 = (bf16[4,2048]{1,0:T(4,128)(2,1)S(1)}, bf16[4,2048]{1,0:T(4,128)(2,1)S(1)}, u32[]{:S(2)}, u32[]{:S(2)}) collective-permute-start(bf16[4,2048]{1,0:T(4,128)(2,1)S(1)} %get-tuple-element.97), channel_id=1, source_target_pairs={{0,5},{1,4},{2,7},{3,6},{4,1},{5,0},{6,3},{7,2},{8,13},{9,12},{10,... | collective-permute-start | bytes 49160 | tf_op jit(solution)/shard_map/ppermute | solution.py:76
  49.4 1.2 %collective-permute-start.21 = (bf16[4,2048]{1,0:T(4,128)(2,1)S(1)}, bf16[4,2048]{1,0:T(4,128)(2,1)S(1)}, u32[]{:S(2)}, u32[]{:S(2)}) collective-permute-start(bf16[4,2048]{1,0:T(4,128)(2,1)S(1)} %get-tuple-element.98), channel_id=1, source_target_pairs={{0,6},{1,7},{2,4},{3,5},{4,2},{5,3},{6,0},{7,1},{8,14},{9,15},{10,... | collective-permute-start | bytes 49160 | tf_op jit(solution)/shard_map/ppermute | solution.py:76
  50.7 1.1 %collective-permute-done.20.refs_4_ = bf16[4,2048]{1,0:T(4,128)(2,1)S(1)} collective-permute-done((bf16[4,2048]{1,0:T(4,128)(2,1)S(1)}, bf16[4,2048]{1,0:T(4,128)(2,1)S(1)}, u32[]{:S(2)}, u32[]{:S(2)}) %collective-permute-start.20) | collective-permute-done | bytes 16416 | tf_op jit(solution)/shard_map/ppermute | solution.py:76
  51.8 2.2 %collective-permute-done.21.refs_5_ = bf16[4,2048]{1,0:T(4,128)(2,1)S(1)} collective-permute-done((bf16[4,2048]{1,0:T(4,128)(2,1)S(1)}, bf16[4,2048]{1,0:T(4,128)(2,1)S(1)}, u32[]{:S(2)}, u32[]{:S(2)}) %collective-permute-start.21) | collective-permute-done | bytes 16416 | tf_op jit(solution)/shard_map/ppermute | solution.py:76
  54.1 0.8 %combine.1 = bf16[32,2048]{1,0:T(8,128)(2,1)} custom-call(f32[32,2048]{1,0:T(8,128)S(1)} %hidden.1.refs_0_, f32[32,16]{1,0:T(8,128)S(1)} %get-tuple-element.82.refs_1_, bf16[4,2048]{1,0:T(4,128)(2,1)S(1)} %get-tuple-element.95.refs_2_, bf16[4,2048]{1,0:T(4,128)(2,1)S(1)} %collective-permute-done.19.refs_3_, ...), custom_call_target="tpu_custom_call" | custom-call | bytes 393216 | tf_op jit(solution)/shard_map/combine/pallas_call | solution.py:61
  (28 shorter events, 1.5 us)
Async XLA Ops:
  0.0 18.2 %copy-start = (bf16[32,2048]{1,0:T(8,128)(2,1)S(1)}, bf16[32,2048]{1,0:T(8,128)(2,1)}, u32[]{:S(2)}) copy-start(bf16[32,2048]{1,0:T(8,128)(2,1)} %refs_4_.4) | copy-start | bytes 393220
  0.0 18.2 %collective-permute-start.3 = (bf16[2048,512]{1,0:T(8,128)(2,1)}, bf16[2048,512]{1,0:T(8,128)(2,1)S(1)}, u32[]{:S(2)}, u32[]{:S(2)}) collective-permute-start(bf16[2048,512]{1,0:T(8,128)(2,1)} %refs_11_.1), channel_id=1, source_target_pairs={{0,1},{1,0},{2,3},{3,2},{4,5},{5,4},{6,7},{7,6},{8,9},{9,8},{10,11... | collective-permute-start | bytes 6291464 | tf_op jit(solution)/shard_map/ppermute | solution.py:76
  0.5 18.9 %collective-permute-start.9 = (bf16[512,2048]{1,0:T(8,128)(2,1)}, bf16[512,2048]{1,0:T(8,128)(2,1)S(1)}, u32[]{:S(2)}, u32[]{:S(2)}) collective-permute-start(bf16[512,2048]{1,0:T(8,128)(2,1)} %refs_4_.3), channel_id=1, source_target_pairs={{0,1},{1,0},{2,3},{3,2},{4,5},{5,4},{6,7},{7,6},{8,9},{9,8},{10,11... | collective-permute-start | bytes 6291464 | tf_op jit(solution)/shard_map/ppermute | solution.py:76
  0.5 15.4 %collective-permute-start.4 = (bf16[128,2048]{1,0:T(8,128)(2,1)}, bf16[128,2048]{1,0:T(8,128)(2,1)S(1)}, u32[]{:S(2)}, u32[]{:S(2)}) collective-permute-start(bf16[128,2048]{1,0:T(8,128)(2,1)} %refs_12_.1), channel_id=1, source_target_pairs={{0,1},{1,0},{2,3},{3,2},{4,5},{5,4},{6,7},{7,6},{8,9},{9,8},{10,11... | collective-permute-start | bytes 1572872 | tf_op jit(solution)/shard_map/ppermute | solution.py:76
  1.0 6.6 %collective-permute-start = (bf16[32,2048]{1,0:T(8,128)(2,1)}, bf16[32,2048]{1,0:T(8,128)(2,1)S(1)}, u32[]{:S(2)}, u32[]{:S(2)}) collective-permute-start(bf16[32,2048]{1,0:T(8,128)(2,1)} %refs_4_.4), channel_id=1, source_target_pairs={{0,3},{1,2},{2,1},{3,0},{4,7},{5,6},{6,5},{7,4},{8,11},{9,10},{10,... | collective-permute-start | bytes 393224 | tf_op jit(solution)/shard_map/ppermute | solution.py:76
  3.6 11.3 %collective-permute-start.1 = (bf16[32,2048]{1,0:T(8,128)(2,1)}, bf16[32,2048]{1,0:T(8,128)(2,1)S(1)}, u32[]{:S(2)}, u32[]{:S(2)}) collective-permute-start(bf16[32,2048]{1,0:T(8,128)(2,1)} %refs_4_.4), channel_id=1, source_target_pairs={{0,5},{1,4},{2,7},{3,6},{4,1},{5,0},{6,3},{7,2},{8,13},{9,12},{10,... | collective-permute-start | bytes 393224 | tf_op jit(solution)/shard_map/ppermute | solution.py:76
  7.6 8.0 %collective-permute-start.2 = (bf16[32,2048]{1,0:T(8,128)(2,1)}, bf16[32,2048]{1,0:T(8,128)(2,1)S(1)}, u32[]{:S(2)}, u32[]{:S(2)}) collective-permute-start(bf16[32,2048]{1,0:T(8,128)(2,1)} %refs_4_.4), channel_id=1, source_target_pairs={{0,6},{1,7},{2,4},{3,5},{4,2},{5,3},{6,0},{7,1},{8,14},{9,15},{10,... | collective-permute-start | bytes 393224 | tf_op jit(solution)/shard_map/ppermute | solution.py:76
  14.9 16.9 %collective-permute-start.5 = (bf16[1168,128]{1,0:T(8,128)(2,1)S(1)}, bf16[1168,128]{1,0:T(8,128)(2,1)S(1)}, u32[]{:S(2)}, u32[]{:S(2)}) collective-permute-start(bf16[1168,128]{1,0:T(8,128)(2,1)S(1)} %get-tuple-element.60), channel_id=1, source_target_pairs={{0,3},{1,2},{2,1},{3,0},{4,7},{5,6},{6,5},{7,4},{8,11},{9,10},{10,... | collective-permute-start | bytes 897032 | tf_op jit(solution)/shard_map/ppermute | solution.py:76
  15.6 16.3 %collective-permute-start.6 = (bf16[1168,128]{1,0:T(8,128)(2,1)S(1)}, bf16[1168,128]{1,0:T(8,128)(2,1)S(1)}, u32[]{:S(2)}, u32[]{:S(2)}) collective-permute-start(bf16[1168,128]{1,0:T(8,128)(2,1)S(1)} %get-tuple-element.61), channel_id=1, source_target_pairs={{0,5},{1,4},{2,7},{3,6},{4,1},{5,0},{6,3},{7,2},{8,13},{9,12},{10,... | collective-permute-start | bytes 897032 | tf_op jit(solution)/shard_map/ppermute | solution.py:76
  15.9 15.9 %collective-permute-start.7 = (bf16[1168,128]{1,0:T(8,128)(2,1)S(1)}, bf16[1168,128]{1,0:T(8,128)(2,1)S(1)}, u32[]{:S(2)}, u32[]{:S(2)}) collective-permute-start(bf16[1168,128]{1,0:T(8,128)(2,1)S(1)} %get-tuple-element.62), channel_id=1, source_target_pairs={{0,6},{1,7},{2,4},{3,5},{4,2},{5,3},{6,0},{7,1},{8,14},{9,15},{10,... | collective-permute-start | bytes 897032 | tf_op jit(solution)/shard_map/ppermute | solution.py:76
  19.4 10.3 %collective-permute-start.10 = (bf16[4,32,128]{2,1,0:T(8,128)(2,1)S(1)}, bf16[4,32,128]{2,1,0:T(8,128)(2,1)S(1)}, u32[]{:S(2)}, u32[]{:S(2)}) collective-permute-start(bf16[4,32,128]{2,1,0:T(8,128)(2,1)S(1)} %hold.1), channel_id=1, source_target_pairs={{0,0},{1,1},{3,6},{2,7},{5,3},{4,2},{6,5},{7,4},{8,8},{9,9},{11,14... | collective-permute-start | bytes 98312 | tf_op jit(solution)/shard_map/ppermute | solution.py:564
  20.0 11.8 %collective-permute-start.8 = (bf16[4,32,128]{2,1,0:T(8,128)(2,1)S(1)}, bf16[4,32,128]{2,1,0:T(8,128)(2,1)S(1)}, u32[]{:S(2)}, u32[]{:S(2)}) collective-permute-start(bf16[4,32,128]{2,1,0:T(8,128)(2,1)S(1)} %get-tuple-element.63), channel_id=1, source_target_pairs={{0,3},{1,2},{3,5},{2,4},{5,0},{4,1},{6,6},{7,7},{8,11},{9,10},{11,... | collective-permute-start | bytes 98312 | tf_op jit(solution)/shard_map/ppermute | solution.py:564
  35.1 6.1 %collective-permute-start.14 = (bf16[16,2048]{1,0:T(8,128)(2,1)S(1)}, bf16[16,2048]{1,0:T(8,128)(2,1)S(1)}, u32[]{:S(2)}, u32[]{:S(2)}) collective-permute-start(bf16[16,2048]{1,0:T(8,128)(2,1)S(1)} %get-tuple-element.83), channel_id=1, source_target_pairs={{0,3},{1,2},{2,1},{3,0},{4,7},{5,6},{6,5},{7,4},{8,11},{9,10},{10,... | collective-permute-start | bytes 196616 | tf_op jit(solution)/shard_map/ppermute | solution.py:76
  36.4 6.1 %collective-permute-start.15 = (bf16[16,2048]{1,0:T(8,128)(2,1)S(1)}, bf16[16,2048]{1,0:T(8,128)(2,1)S(1)}, u32[]{:S(2)}, u32[]{:S(2)}) collective-permute-start(bf16[16,2048]{1,0:T(8,128)(2,1)S(1)} %get-tuple-element.84), channel_id=1, source_target_pairs={{0,5},{1,4},{2,7},{3,6},{4,1},{5,0},{6,3},{7,2},{8,13},{9,12},{10,... | collective-permute-start | bytes 196616 | tf_op jit(solution)/shard_map/ppermute | solution.py:76
  37.2 5.2 %collective-permute-start.16 = (bf16[16,2048]{1,0:T(8,128)(2,1)S(1)}, bf16[16,2048]{1,0:T(8,128)(2,1)S(1)}, u32[]{:S(2)}, u32[]{:S(2)}) collective-permute-start(bf16[16,2048]{1,0:T(8,128)(2,1)S(1)} %get-tuple-element.85), channel_id=1, source_target_pairs={{0,6},{1,7},{2,4},{3,5},{4,2},{5,3},{6,0},{7,1},{8,14},{9,15},{10,... | collective-permute-start | bytes 196616 | tf_op jit(solution)/shard_map/ppermute | solution.py:76
  39.1 10.3 %collective-permute-start.11 = (bf16[32,2048]{1,0:T(8,128)(2,1)S(1)}, bf16[32,2048]{1,0:T(8,128)(2,1)S(1)}, u32[]{:S(2)}, u32[]{:S(2)}) collective-permute-start(bf16[32,2048]{1,0:T(8,128)(2,1)S(1)} %get-tuple-element.79), channel_id=1, source_target_pairs={{0,3},{1,2},{2,1},{3,0},{4,7},{5,6},{6,5},{7,4},{8,11},{9,10},{10,... | collective-permute-start | bytes 393224 | tf_op jit(solution)/shard_map/ppermute | solution.py:76
  40.1 10.6 %collective-permute-start.12 = (bf16[32,2048]{1,0:T(8,128)(2,1)S(1)}, bf16[32,2048]{1,0:T(8,128)(2,1)S(1)}, u32[]{:S(2)}, u32[]{:S(2)}) collective-permute-start(bf16[32,2048]{1,0:T(8,128)(2,1)S(1)} %get-tuple-element.80), channel_id=1, source_target_pairs={{0,5},{1,4},{2,7},{3,6},{4,1},{5,0},{6,3},{7,2},{8,13},{9,12},{10,... | collective-permute-start | bytes 393224 | tf_op jit(solution)/shard_map/ppermute | solution.py:76
  41.2 9.4 %collective-permute-start.13 = (bf16[32,2048]{1,0:T(8,128)(2,1)S(1)}, bf16[32,2048]{1,0:T(8,128)(2,1)S(1)}, u32[]{:S(2)}, u32[]{:S(2)}) collective-permute-start(bf16[32,2048]{1,0:T(8,128)(2,1)S(1)} %get-tuple-element.81), channel_id=1, source_target_pairs={{0,6},{1,7},{2,4},{3,5},{4,2},{5,3},{6,0},{7,1},{8,14},{9,15},{10,... | collective-permute-start | bytes 393224 | tf_op jit(solution)/shard_map/ppermute | solution.py:76
  42.6 1.3 %collective-permute-start.17 = (bf16[8,2048]{1,0:T(8,128)(2,1)S(1)}, bf16[8,2048]{1,0:T(8,128)(2,1)S(1)}, u32[]{:S(2)}, u32[]{:S(2)}) collective-permute-start(bf16[8,2048]{1,0:T(8,128)(2,1)S(1)} %get-tuple-element.89), channel_id=1, source_target_pairs={{0,1},{1,0},{2,3},{3,2},{4,5},{5,4},{6,7},{7,6},{8,9},{9,8},{10,11... | collective-permute-start | bytes 98312 | tf_op jit(solution)/shard_map/ppermute | solution.py:76
  46.0 1.2 %collective-permute-start.18 = (bf16[8,2048]{1,0:T(8,128)(2,1)S(1)}, bf16[8,2048]{1,0:T(8,128)(2,1)S(1)}, u32[]{:S(2)}, u32[]{:S(2)}) collective-permute-start(bf16[8,2048]{1,0:T(8,128)(2,1)S(1)} %get-tuple-element.93), channel_id=1, source_target_pairs={{0,1},{1,0},{2,3},{3,2},{4,5},{5,4},{6,7},{7,6},{8,9},{9,8},{10,11... | collective-permute-start | bytes 98312 | tf_op jit(solution)/shard_map/ppermute | solution.py:76
  47.4 3.4 %collective-permute-start.19 = (bf16[4,2048]{1,0:T(4,128)(2,1)S(1)}, bf16[4,2048]{1,0:T(4,128)(2,1)S(1)}, u32[]{:S(2)}, u32[]{:S(2)}) collective-permute-start(bf16[4,2048]{1,0:T(4,128)(2,1)S(1)} %get-tuple-element.96), channel_id=1, source_target_pairs={{0,3},{1,2},{2,1},{3,0},{4,7},{5,6},{6,5},{7,4},{8,11},{9,10},{10,... | collective-permute-start | bytes 49160 | tf_op jit(solution)/shard_map/ppermute | solution.py:76
  48.7 3.2 %collective-permute-start.20 = (bf16[4,2048]{1,0:T(4,128)(2,1)S(1)}, bf16[4,2048]{1,0:T(4,128)(2,1)S(1)}, u32[]{:S(2)}, u32[]{:S(2)}) collective-permute-start(bf16[4,2048]{1,0:T(4,128)(2,1)S(1)} %get-tuple-element.97), channel_id=1, source_target_pairs={{0,5},{1,4},{2,7},{3,6},{4,1},{5,0},{6,3},{7,2},{8,13},{9,12},{10,... | collective-permute-start | bytes 49160 | tf_op jit(solution)/shard_map/ppermute | solution.py:76
  49.4 4.6 %collective-permute-start.21 = (bf16[4,2048]{1,0:T(4,128)(2,1)S(1)}, bf16[4,2048]{1,0:T(4,128)(2,1)S(1)}, u32[]{:S(2)}, u32[]{:S(2)}) collective-permute-start(bf16[4,2048]{1,0:T(4,128)(2,1)S(1)} %get-tuple-element.98), channel_id=1, source_target_pairs={{0,6},{1,7},{2,4},{3,5},{4,2},{5,3},{6,0},{7,1},{8,14},{9,15},{10,... | collective-permute-start | bytes 49160 | tf_op jit(solution)/shard_map/ppermute | solution.py:76

commit v6 on v3

--- a/solution.py
+++ b/solution.py
@@ -23,7 +23,7 @@
 
 
 def step(j):
-    return 2 * j + bin(j).count("1") % 2
+    return 2 * j + (j >> 1) % 2
 
 
 def iota(shape, dim):
@@ -203,10 +203,7 @@
     chips = devices // 2
     tokens = chips * new
     slot = iota((all_tokens, tokens), 1) // new
-    odd = slot
-    for shift in (4, 2, 1):
-        odd = odd ^ (odd >> shift)
-    source = (me ^ (2 * slot + (odd & 1))) * new + iota((all_tokens, tokens), 1) % new
+    source = (me ^ (2 * slot + ((slot >> 1) & 1))) * new + iota((all_tokens, tokens), 1) % new
     order = (iota((all_tokens, tokens), 0) == source).astype(F32)
     ids = dot(ids_ref[...].astype(F32).astype(BF16), order.astype(BF16))
     gates = lax.dot_general(

time: 50.1 us -> 49.9 us (level)
  transfers between devices with their start and end apart: 23 -> 23, of which waited for: 7 -> 9; matrix products, arithmetic and copies ran while one was open for 0% -> 0% of each run, Pallas kernels for 24% -> 24%
where the time goes in v6:
time: 49.9 us; the launch traced here: 49.5 us
  starting transfers between devices  21.4 us (43%)
  Pallas kernels  17 us (34%)
  waiting for transfers between devices  9.06 us (18%)
  between operations  2.09 us (4%)
    ppermute x23, starting transfers between devices, hop(): lax.ppermute(value, 'tensor', [(i, i ^ step) for i in range(devices)])  21.4 us
    pallas_call x12, Pallas kernels, call(): pl.pallas_call(kernel, out_shape=outs, in_specs=specs, out_specs=[pl.Bloc...  17 us
    ppermute x23, waiting for transfers between devices, hop(): lax.ppermute(value, 'tensor', [(i, i ^ step) for i in range(devices)])  9.06 us
  transfers between devices with their start and end apart: 23, of which 9 were waited for; matrix products, arithmetic and copies ran while one was open for 0% of the time, Pallas kernels for 24%

profile of v6, /device:TPU:0, one launch (start us, length us, event | category | flops | bytes accessed | tf_op | source)
XLA Modules:
  0.0 49.5 jit_solution(3178514904310068153)
XLA Ops:
  0.0 0.5 collective-permute-start.3
  0.5 3.5 %collective-permute-start.2 = (bf16[32,2048]{1,0:T(8,128)(2,1)}, bf16[32,2048]{1,0:T(8,128)(2,1)S(1)}, u32[]{:S(2)}, u32[]{:S(2)}) collective-permute-start(bf16[32,2048]{1,0:T(8,128)(2,1)} %refs_4_.4), channel_id=1, source_target_pairs={{0,7},{1,6},{2,5},{3,4},{4,3},{5,2},{6,1},{7,0},{8,15},{9,14},{10,... | collective-permute-start | bytes 393224 | tf_op jit(solution)/shard_map/ppermute | solution.py:76
  4.0 0.6 %collective-permute-start.1 = (bf16[32,2048]{1,0:T(8,128)(2,1)}, bf16[32,2048]{1,0:T(8,128)(2,1)S(1)}, u32[]{:S(2)}, u32[]{:S(2)}) collective-permute-start(bf16[32,2048]{1,0:T(8,128)(2,1)} %refs_4_.4), channel_id=1, source_target_pairs={{0,5},{1,4},{2,7},{3,6},{4,1},{5,0},{6,3},{7,2},{8,13},{9,12},{10,... | collective-permute-start | bytes 393224 | tf_op jit(solution)/shard_map/ppermute | solution.py:76
  6.6 3.2 %prep.1 = (bf16[4,640,128]{2,1,0:T(8,128)(2,1)S(1)}, bf16[4,640,128]{2,1,0:T(8,128)(2,1)S(1)}, f32[32,640]{1,0:T(8,128)S(1)}, f32[4,32,128]{2,1,0:T(8,128)S(1)},...) custom-call(bf16[1,1024,512]{2,1,0:T(8,128)(2,1)} %refs_0_.3, ...), custom_call_target="tpu_custom_call" | custom-call | bytes 2621440 | tf_op jit(solution)/shard_map/prep/pallas_call | solution.py:61
  9.8 1.2 %collective-permute-done.1.refs_2_ = bf16[32,2048]{1,0:T(8,128)(2,1)S(1)} collective-permute-done((bf16[32,2048]{1,0:T(8,128)(2,1)}, bf16[32,2048]{1,0:T(8,128)(2,1)S(1)}, u32[]{:S(2)}, u32[]{:S(2)}) %collective-permute-start.1) | collective-permute-done | bytes 131104 | tf_op jit(solution)/shard_map/ppermute | solution.py:76
  11.0 0.8 %collective-permute-done.refs_1_ = bf16[32,2048]{1,0:T(8,128)(2,1)S(1)} collective-permute-done((bf16[32,2048]{1,0:T(8,128)(2,1)}, bf16[32,2048]{1,0:T(8,128)(2,1)S(1)}, u32[]{:S(2)}, u32[]{:S(2)}) %collective-permute-start) | collective-permute-done | bytes 131104 | tf_op jit(solution)/shard_map/ppermute | solution.py:76
  11.8 1.1 %project.1 = (bf16[32,1280]{1,0:T(8,128)(2,1)S(1)}, bf16[32,1280]{1,0:T(8,128)(2,1)S(1)}, bf16[32,1280]{1,0:T(8,128)(2,1)S(1)}, bf16[32,1280]{1,0:T(8,128)(2,1)S(1)}) custom-call(bf16[32,2048]{1,0:T(8,128)(2,1)S(1)} %copy-done, bf16[32,2048]{1,0:T(8,128)(2,1)S(1)} %collective-permute-done.refs_1_, bf16[32,2048]{1,0:T(8,128)(2,1)S(1)} %collective-permute-done.1.refs_2_, ...), custom_call_target="tpu_custom_call" | custom-call | flops 671088640 | bytes 5242880 | tf_op jit(solution)/shard_map/project/pallas_call | solution.py:61
  12.9 1.6 %collective-permute-start.5 = (bf16[32,1280]{1,0:T(8,128)(2,1)S(1)}, bf16[32,1280]{1,0:T(8,128)(2,1)S(1)}, u32[]{:S(2)}, u32[]{:S(2)}) collective-permute-start(bf16[32,1280]{1,0:T(8,128)(2,1)S(1)} %get-tuple-element.50), channel_id=1, source_target_pairs={{0,2},{1,3},{2,0},{3,1},{4,6},{5,7},{6,4},{7,5},{8,10},{9,11},{10,... | collective-permute-start | bytes 245768 | tf_op jit(solution)/shard_map/ppermute | solution.py:76
  14.5 1.7 %collective-permute-start.7 = (bf16[32,1280]{1,0:T(8,128)(2,1)S(1)}, bf16[32,1280]{1,0:T(8,128)(2,1)S(1)}, u32[]{:S(2)}, u32[]{:S(2)}) collective-permute-start(bf16[32,1280]{1,0:T(8,128)(2,1)S(1)} %get-tuple-element.52), channel_id=1, source_target_pairs={{0,7},{1,6},{2,5},{3,4},{4,3},{5,2},{6,1},{7,0},{8,15},{9,14},{10,... | collective-permute-start | bytes 245768 | tf_op jit(solution)/shard_map/ppermute | solution.py:76
  16.2 2.6 %route.1 = (f32[64,128]{1,0:T(8,128)S(1)}, f32[32,16]{1,0:T(8,128)S(1)}, f32[16,128]{1,0:T(8,128)S(1)}, f32[1,2048]{1,0:T(1,128)S(1)}, bf16[512,2048]{1,0:T(8,128)(2,1)S(1)}, /*index=5*/bf16[1,768,2048]{2,1,0:T(8,128)(2,1)S(1)}) custom-call(bf16[32,1280]{1,0:T(8,128)(2,1)S(1)} %get-tuple-element.49.refs_0_, s32[8,256]{1,0:T(8,128)} %bitcast.7, ...), custom_call_target="tpu_custom_call" | custom-call | bytes 10485760 | tf_op jit(solution)/shard_map/route/pallas_call | solution.py:61
  18.8 2.1 %collective-permute-done.6.refs_2_ = bf16[32,1280]{1,0:T(8,128)(2,1)S(1)} collective-permute-done((bf16[32,1280]{1,0:T(8,128)(2,1)S(1)}, bf16[32,1280]{1,0:T(8,128)(2,1)S(1)}, u32[]{:S(2)}, u32[]{:S(2)}) %collective-permute-start.6) | collective-permute-done | bytes 81952 | tf_op jit(solution)/shard_map/ppermute | solution.py:76
  20.9 2.1 %attend.1 = (bf16[32,1024]{1,0:T(8,128)(2,1)S(1)}, bf16[32,1024]{1,0:T(8,128)(2,1)S(1)}, bf16[32,1024]{1,0:T(8,128)(2,1)S(1)}, bf16[32,1024]{1,0:T(8,128)(2,1)S(1)}, bf16[512,2048]{1,0:T(8,128)(2,1)S(1)}) custom-call(bf16[32,1280]{1,0:T(8,128)(2,1)S(1)} %get-tuple-element.49.refs_0_, ...), custom_call_target="tpu_custom_call", output_to_operand_aliasing={{4}: (8, {})} | custom-call | flops 335544320 | bytes 1310720 | tf_op jit(solution)/shard_map/attend/pallas_call | solution.py:61
  23.5 1.4 %collective-permute-start.9 = (bf16[32,1024]{1,0:T(8,128)(2,1)S(1)}, bf16[32,1024]{1,0:T(8,128)(2,1)S(1)}, u32[]{:S(2)}, u32[]{:S(2)}) collective-permute-start(bf16[32,1024]{1,0:T(8,128)(2,1)S(1)} %get-tuple-element.60), channel_id=1, source_target_pairs={{0,5},{1,4},{2,7},{3,6},{4,1},{5,0},{6,3},{7,2},{8,13},{9,12},{10,... | collective-permute-start | bytes 196616 | tf_op jit(solution)/shard_map/ppermute | solution.py:76
  24.9 1.5 %collective-permute-start.10 = (bf16[32,1024]{1,0:T(8,128)(2,1)S(1)}, bf16[32,1024]{1,0:T(8,128)(2,1)S(1)}, u32[]{:S(2)}, u32[]{:S(2)}) collective-permute-start(bf16[32,1024]{1,0:T(8,128)(2,1)S(1)} %get-tuple-element.61), channel_id=1, source_target_pairs={{0,7},{1,6},{2,5},{3,4},{4,3},{5,2},{6,1},{7,0},{8,15},{9,14},{10,... | collective-permute-start | bytes 196616 | tf_op jit(solution)/shard_map/ppermute | solution.py:76
  26.4 2.9 %select.1 = (f32[16,2048]{1,0:T(8,128)S(1)}, bf16[1,768,2048]{2,1,0:T(8,128)(2,1)S(1)}, bf16[1,768,2048]{2,1,0:T(8,128)(2,1)S(1)}) custom-call(bf16[32,2048]{1,0:T(8,128)(2,1)S(1)} %copy-done, bf16[32,2048]{1,0:T(8,128)(2,1)S(1)} %collective-permute-done.refs_1_, bf16[32,2048]{1,0:T(8,128)(2,1)S(1)} %collective-permute-done.1.refs_2_, ...), custom_call_target="tpu_custom_call" | custom-call | flops 8388608 | bytes 12582912 | tf_op jit(solution)/shard_map/select/pallas_call | solution.py:61
  29.6 1.0 %experts.1 = (bf16[16,2048]{1,0:T(8,128)(2,1)S(1)}, bf16[16,2048]{1,0:T(8,128)(2,1)S(1)}, bf16[16,2048]{1,0:T(8,128)(2,1)S(1)}, bf16[16,2048]{1,0:T(8,128)(2,1)S(1)}) custom-call(bf16[32,1024]{1,0:T(8,128)(2,1)S(1)} %get-tuple-element.58.refs_5_.refs_0_, bf16[32,1024]{1,0:T(8,128)(2,1)S(1)} %collective-permute-done.8.refs_1_, ...), custom_call_target="tpu_custom_call" | custom-call | flops 268435456 | bytes 4194304 | tf_op jit(solution)/shard_map/experts/pallas_call | solution.py:61
  30.6 1.1 %collective-permute-start.15 = (bf16[16,2048]{1,0:T(8,128)(2,1)S(1)}, bf16[16,2048]{1,0:T(8,128)(2,1)S(1)}, u32[]{:S(2)}, u32[]{:S(2)}) collective-permute-start(bf16[16,2048]{1,0:T(8,128)(2,1)S(1)} %get-tuple-element.71), channel_id=1, source_target_pairs={{0,2},{1,3},{2,0},{3,1},{4,6},{5,7},{6,4},{7,5},{8,10},{9,11},{10,... | collective-permute-start | bytes 196616 | tf_op jit(solution)/shard_map/ppermute | solution.py:76
  31.7 0.8 %collective-permute-start.16 = (bf16[16,2048]{1,0:T(8,128)(2,1)S(1)}, bf16[16,2048]{1,0:T(8,128)(2,1)S(1)}, u32[]{:S(2)}, u32[]{:S(2)}) collective-permute-start(bf16[16,2048]{1,0:T(8,128)(2,1)S(1)} %get-tuple-element.72), channel_id=1, source_target_pairs={{0,5},{1,4},{2,7},{3,6},{4,1},{5,0},{6,3},{7,2},{8,13},{9,12},{10,... | collective-permute-start | bytes 196616 | tf_op jit(solution)/shard_map/ppermute | solution.py:76
  32.5 1.4 %collective-permute-start.17 = (bf16[16,2048]{1,0:T(8,128)(2,1)S(1)}, bf16[16,2048]{1,0:T(8,128)(2,1)S(1)}, u32[]{:S(2)}, u32[]{:S(2)}) collective-permute-start(bf16[16,2048]{1,0:T(8,128)(2,1)S(1)} %get-tuple-element.73), channel_id=1, source_target_pairs={{0,7},{1,6},{2,5},{3,4},{4,3},{5,2},{6,1},{7,0},{8,15},{9,14},{10,... | collective-permute-start | bytes 196616 | tf_op jit(solution)/shard_map/ppermute | solution.py:76
  33.9 0.7 %slots.1 = (bf16[32,2048]{1,0:T(8,128)(2,1)S(1)}, bf16[32,2048]{1,0:T(8,128)(2,1)S(1)}, bf16[32,2048]{1,0:T(8,128)(2,1)S(1)}, bf16[32,2048]{1,0:T(8,128)(2,1)S(1)}) custom-call(bf16[32,1024]{1,0:T(8,128)(2,1)S(1)} %get-tuple-element.58.refs_5_.refs_0_, bf16[32,1024]{1,0:T(8,128)(2,1)S(1)} %collective-permute-done.8.refs_1_, ...), custom_call_target="tpu_custom_call" | custom-call | flops 536870912 | bytes 4194304 | tf_op jit(solution)/shard_map/slots/pallas_call | solution.py:61
  34.6 1.1 %collective-permute-start.12 = (bf16[32,2048]{1,0:T(8,128)(2,1)S(1)}, bf16[32,2048]{1,0:T(8,128)(2,1)S(1)}, u32[]{:S(2)}, u32[]{:S(2)}) collective-permute-start(bf16[32,2048]{1,0:T(8,128)(2,1)S(1)} %get-tuple-element.67), channel_id=1, source_target_pairs={{0,2},{1,3},{2,0},{3,1},{4,6},{5,7},{6,4},{7,5},{8,10},{9,11},{10,... | collective-permute-start | bytes 393224 | tf_op jit(solution)/shard_map/ppermute | solution.py:76
  35.7 0.5 collective-permute-start.13
  36.2 1.7 %collective-permute-start.14 = (bf16[32,2048]{1,0:T(8,128)(2,1)S(1)}, bf16[32,2048]{1,0:T(8,128)(2,1)S(1)}, u32[]{:S(2)}, u32[]{:S(2)}) collective-permute-start(bf16[32,2048]{1,0:T(8,128)(2,1)S(1)} %get-tuple-element.69), channel_id=1, source_target_pairs={{0,7},{1,6},{2,5},{3,4},{4,3},{5,2},{6,1},{7,0},{8,15},{9,14},{10,... | collective-permute-start | bytes 393224 | tf_op jit(solution)/shard_map/ppermute | solution.py:76
  38.2 1.2 %collective-permute-done.18.other_ref = bf16[8,2048]{1,0:T(8,128)(2,1)S(1)} collective-permute-done((bf16[8,2048]{1,0:T(8,128)(2,1)S(1)}, bf16[8,2048]{1,0:T(8,128)(2,1)S(1)}, u32[]{:S(2)}, u32[]{:S(2)}) %collective-permute-start.18) | collective-permute-done | bytes 32800 | tf_op jit(solution)/shard_map/ppermute | solution.py:76
  39.3 2.2 %expert.1 = (f32[8,2048]{1,0:T(8,128)S(1)}, bf16[8,2048]{1,0:T(8,128)(2,1)S(1)}) custom-call(bf16[8,2048]{1,0:T(8,128)(2,1)S(1)} %get-tuple-element.76.own_ref, bf16[8,2048]{1,0:T(8,128)(2,1)S(1)} %collective-permute-done.18.other_ref, bf16[1,768,2048]{2,1,0:T(8,128)(2,1)S(1)} %get-tuple-element.64.refs_7_.gate_ref, ...), custom_call_target="tpu_custom_call" | custom-call | flops 150994944 | bytes 9437184 | tf_op jit(solution)/shard_map/expert/pallas_call | solution.py:61
  41.7 1.0 %collective-permute-done.19.other_ref = bf16[8,2048]{1,0:T(8,128)(2,1)S(1)} collective-permute-done((bf16[8,2048]{1,0:T(8,128)(2,1)S(1)}, bf16[8,2048]{1,0:T(8,128)(2,1)S(1)}, u32[]{:S(2)}, u32[]{:S(2)}) %collective-permute-start.19) | collective-permute-done | bytes 32800 | tf_op jit(solution)/shard_map/ppermute | solution.py:76
  42.9 1.1 %collective-permute-start.20 = (bf16[4,2048]{1,0:T(4,128)(2,1)S(1)}, bf16[4,2048]{1,0:T(4,128)(2,1)S(1)}, u32[]{:S(2)}, u32[]{:S(2)}) collective-permute-start(bf16[4,2048]{1,0:T(4,128)(2,1)S(1)} %get-tuple-element.84), channel_id=1, source_target_pairs={{0,2},{1,3},{2,0},{3,1},{4,6},{5,7},{6,4},{7,5},{8,10},{9,11},{10,... | collective-permute-start | bytes 49160 | tf_op jit(solution)/shard_map/ppermute | solution.py:76
  43.9 0.7 %collective-permute-start.21 = (bf16[4,2048]{1,0:T(4,128)(2,1)S(1)}, bf16[4,2048]{1,0:T(4,128)(2,1)S(1)}, u32[]{:S(2)}, u32[]{:S(2)}) collective-permute-start(bf16[4,2048]{1,0:T(4,128)(2,1)S(1)} %get-tuple-element.85), channel_id=1, source_target_pairs={{0,5},{1,4},{2,7},{3,6},{4,1},{5,0},{6,3},{7,2},{8,13},{9,12},{10,... | collective-permute-start | bytes 49160 | tf_op jit(solution)/shard_map/ppermute | solution.py:76
  44.6 1.5 %collective-permute-start.22 = (bf16[4,2048]{1,0:T(4,128)(2,1)S(1)}, bf16[4,2048]{1,0:T(4,128)(2,1)S(1)}, u32[]{:S(2)}, u32[]{:S(2)}) collective-permute-start(bf16[4,2048]{1,0:T(4,128)(2,1)S(1)} %get-tuple-element.86), channel_id=1, source_target_pairs={{0,7},{1,6},{2,5},{3,4},{4,3},{5,2},{6,1},{7,0},{8,15},{9,14},{10,... | collective-permute-start | bytes 49160 | tf_op jit(solution)/shard_map/ppermute | solution.py:76
  46.7 0.5 %collective-permute-done.21.refs_4_ = bf16[4,2048]{1,0:T(4,128)(2,1)S(1)} collective-permute-done((bf16[4,2048]{1,0:T(4,128)(2,1)S(1)}, bf16[4,2048]{1,0:T(4,128)(2,1)S(1)}, u32[]{:S(2)}, u32[]{:S(2)}) %collective-permute-start.21) | collective-permute-done | bytes 16416 | tf_op jit(solution)/shard_map/ppermute | solution.py:76
  47.2 1.5 %collective-permute-done.22.refs_5_ = bf16[4,2048]{1,0:T(4,128)(2,1)S(1)} collective-permute-done((bf16[4,2048]{1,0:T(4,128)(2,1)S(1)}, bf16[4,2048]{1,0:T(4,128)(2,1)S(1)}, u32[]{:S(2)}, u32[]{:S(2)}) %collective-permute-start.22) | collective-permute-done | bytes 16416 | tf_op jit(solution)/shard_map/ppermute | solution.py:76
  48.7 0.8 %combine.1 = bf16[32,2048]{1,0:T(8,128)(2,1)} custom-call(f32[32,2048]{1,0:T(8,128)S(1)} %hidden.1.refs_0_, f32[32,16]{1,0:T(8,128)S(1)} %get-tuple-element.70.refs_1_, bf16[4,2048]{1,0:T(4,128)(2,1)S(1)} %get-tuple-element.83.refs_2_, bf16[4,2048]{1,0:T(4,128)(2,1)S(1)} %collective-permute-done.20.refs_3_, ...), custom_call_target="tpu_custom_call" | custom-call | bytes 393216 | tf_op jit(solution)/shard_map/combine/pallas_call | solution.py:61
  (28 shorter events, 1.9 us)
Async XLA Ops:
  0.0 11.8 %collective-permute-start.3 = (bf16[2048,512]{1,0:T(8,128)(2,1)}, bf16[2048,512]{1,0:T(8,128)(2,1)S(1)}, u32[]{:S(2)}, u32[]{:S(2)}) collective-permute-start(bf16[2048,512]{1,0:T(8,128)(2,1)} %refs_11_.1), channel_id=1, source_target_pairs={{0,1},{1,0},{2,3},{3,2},{4,5},{5,4},{6,7},{7,6},{8,9},{9,8},{10,11... | collective-permute-start | bytes 6291464 | tf_op jit(solution)/shard_map/ppermute | solution.py:76
  0.5 11.3 %collective-permute-start.4 = (bf16[128,2048]{1,0:T(8,128)(2,1)}, bf16[128,2048]{1,0:T(8,128)(2,1)S(1)}, u32[]{:S(2)}, u32[]{:S(2)}) collective-permute-start(bf16[128,2048]{1,0:T(8,128)(2,1)} %refs_12_.1), channel_id=1, source_target_pairs={{0,1},{1,0},{2,3},{3,2},{4,5},{5,4},{6,7},{7,6},{8,9},{9,8},{10,11... | collective-permute-start | bytes 1572872 | tf_op jit(solution)/shard_map/ppermute | solution.py:76
  0.5 9.3 %collective-permute-start.2 = (bf16[32,2048]{1,0:T(8,128)(2,1)}, bf16[32,2048]{1,0:T(8,128)(2,1)S(1)}, u32[]{:S(2)}, u32[]{:S(2)}) collective-permute-start(bf16[32,2048]{1,0:T(8,128)(2,1)} %refs_4_.4), channel_id=1, source_target_pairs={{0,7},{1,6},{2,5},{3,4},{4,3},{5,2},{6,1},{7,0},{8,15},{9,14},{10,... | collective-permute-start | bytes 393224 | tf_op jit(solution)/shard_map/ppermute | solution.py:76
  4.0 7.0 %collective-permute-start.1 = (bf16[32,2048]{1,0:T(8,128)(2,1)}, bf16[32,2048]{1,0:T(8,128)(2,1)S(1)}, u32[]{:S(2)}, u32[]{:S(2)}) collective-permute-start(bf16[32,2048]{1,0:T(8,128)(2,1)} %refs_4_.4), channel_id=1, source_target_pairs={{0,5},{1,4},{2,7},{3,6},{4,1},{5,0},{6,3},{7,2},{8,13},{9,12},{10,... | collective-permute-start | bytes 393224 | tf_op jit(solution)/shard_map/ppermute | solution.py:76
  4.6 7.1 %collective-permute-start = (bf16[32,2048]{1,0:T(8,128)(2,1)}, bf16[32,2048]{1,0:T(8,128)(2,1)S(1)}, u32[]{:S(2)}, u32[]{:S(2)}) collective-permute-start(bf16[32,2048]{1,0:T(8,128)(2,1)} %refs_4_.4), channel_id=1, source_target_pairs={{0,2},{1,3},{2,0},{3,1},{4,6},{5,7},{6,4},{7,5},{8,10},{9,11},{10,... | collective-permute-start | bytes 393224 | tf_op jit(solution)/shard_map/ppermute | solution.py:76
  6.6 5.2 %copy-start = (bf16[32,2048]{1,0:T(8,128)(2,1)S(1)}, bf16[32,2048]{1,0:T(8,128)(2,1)}, u32[]{:S(2)}) copy-start(bf16[32,2048]{1,0:T(8,128)(2,1)} %refs_4_.4) | copy-start | bytes 393220
  12.9 5.9 %collective-permute-start.5 = (bf16[32,1280]{1,0:T(8,128)(2,1)S(1)}, bf16[32,1280]{1,0:T(8,128)(2,1)S(1)}, u32[]{:S(2)}, u32[]{:S(2)}) collective-permute-start(bf16[32,1280]{1,0:T(8,128)(2,1)S(1)} %get-tuple-element.50), channel_id=1, source_target_pairs={{0,2},{1,3},{2,0},{3,1},{4,6},{5,7},{6,4},{7,5},{8,10},{9,11},{10,... | collective-permute-start | bytes 245768 | tf_op jit(solution)/shard_map/ppermute | solution.py:76
  14.5 6.4 %collective-permute-start.6 = (bf16[32,1280]{1,0:T(8,128)(2,1)S(1)}, bf16[32,1280]{1,0:T(8,128)(2,1)S(1)}, u32[]{:S(2)}, u32[]{:S(2)}) collective-permute-start(bf16[32,1280]{1,0:T(8,128)(2,1)S(1)} %get-tuple-element.51), channel_id=1, source_target_pairs={{0,5},{1,4},{2,7},{3,6},{4,1},{5,0},{6,3},{7,2},{8,13},{9,12},{10,... | collective-permute-start | bytes 245768 | tf_op jit(solution)/shard_map/ppermute | solution.py:76
  14.5 6.4 %collective-permute-start.7 = (bf16[32,1280]{1,0:T(8,128)(2,1)S(1)}, bf16[32,1280]{1,0:T(8,128)(2,1)S(1)}, u32[]{:S(2)}, u32[]{:S(2)}) collective-permute-start(bf16[32,1280]{1,0:T(8,128)(2,1)S(1)} %get-tuple-element.52), channel_id=1, source_target_pairs={{0,7},{1,6},{2,5},{3,4},{4,3},{5,2},{6,1},{7,0},{8,15},{9,14},{10,... | collective-permute-start | bytes 245768 | tf_op jit(solution)/shard_map/ppermute | solution.py:76
  23.0 6.6 %collective-permute-start.11 = (bf16[512,2048]{1,0:T(8,128)(2,1)S(1)}, bf16[512,2048]{1,0:T(8,128)(2,1)S(1)}, u32[]{:S(2)}, u32[]{:S(2)}) collective-permute-start(bf16[512,2048]{1,0:T(8,128)(2,1)S(1)} %get-tuple-element.62.refs_4_), channel_id=1, source_target_pairs={{0,1},{1,0},{2,3},{3,2},{4,5},{5,4},{6,7},{7,6},{8,9},{9,8},{10,11... | collective-permute-start | bytes 6291464 | tf_op jit(solution)/shard_map/ppermute | solution.py:76
  23.1 6.1 %collective-permute-start.8 = (bf16[32,1024]{1,0:T(8,128)(2,1)S(1)}, bf16[32,1024]{1,0:T(8,128)(2,1)S(1)}, u32[]{:S(2)}, u32[]{:S(2)}) collective-permute-start(bf16[32,1024]{1,0:T(8,128)(2,1)S(1)} %get-tuple-element.59), channel_id=1, source_target_pairs={{0,2},{1,3},{2,0},{3,1},{4,6},{5,7},{6,4},{7,5},{8,10},{9,11},{10,... | collective-permute-start | bytes 196616 | tf_op jit(solution)/shard_map/ppermute | solution.py:76
  23.5 5.8 %collective-permute-start.9 = (bf16[32,1024]{1,0:T(8,128)(2,1)S(1)}, bf16[32,1024]{1,0:T(8,128)(2,1)S(1)}, u32[]{:S(2)}, u32[]{:S(2)}) collective-permute-start(bf16[32,1024]{1,0:T(8,128)(2,1)S(1)} %get-tuple-element.60), channel_id=1, source_target_pairs={{0,5},{1,4},{2,7},{3,6},{4,1},{5,0},{6,3},{7,2},{8,13},{9,12},{10,... | collective-permute-start | bytes 196616 | tf_op jit(solution)/shard_map/ppermute | solution.py:76
  24.9 4.7 %collective-permute-start.10 = (bf16[32,1024]{1,0:T(8,128)(2,1)S(1)}, bf16[32,1024]{1,0:T(8,128)(2,1)S(1)}, u32[]{:S(2)}, u32[]{:S(2)}) collective-permute-start(bf16[32,1024]{1,0:T(8,128)(2,1)S(1)} %get-tuple-element.61), channel_id=1, source_target_pairs={{0,7},{1,6},{2,5},{3,4},{4,3},{5,2},{6,1},{7,0},{8,15},{9,14},{10,... | collective-permute-start | bytes 196616 | tf_op jit(solution)/shard_map/ppermute | solution.py:76
  30.6 5.6 %collective-permute-start.15 = (bf16[16,2048]{1,0:T(8,128)(2,1)S(1)}, bf16[16,2048]{1,0:T(8,128)(2,1)S(1)}, u32[]{:S(2)}, u32[]{:S(2)}) collective-permute-start(bf16[16,2048]{1,0:T(8,128)(2,1)S(1)} %get-tuple-element.71), channel_id=1, source_target_pairs={{0,2},{1,3},{2,0},{3,1},{4,6},{5,7},{6,4},{7,5},{8,10},{9,11},{10,... | collective-permute-start | bytes 196616 | tf_op jit(solution)/shard_map/ppermute | solution.py:76
  31.7 6.2 %collective-permute-start.16 = (bf16[16,2048]{1,0:T(8,128)(2,1)S(1)}, bf16[16,2048]{1,0:T(8,128)(2,1)S(1)}, u32[]{:S(2)}, u32[]{:S(2)}) collective-permute-start(bf16[16,2048]{1,0:T(8,128)(2,1)S(1)} %get-tuple-element.72), channel_id=1, source_target_pairs={{0,5},{1,4},{2,7},{3,6},{4,1},{5,0},{6,3},{7,2},{8,13},{9,12},{10,... | collective-permute-start | bytes 196616 | tf_op jit(solution)/shard_map/ppermute | solution.py:76
  32.5 5.5 %collective-permute-start.17 = (bf16[16,2048]{1,0:T(8,128)(2,1)S(1)}, bf16[16,2048]{1,0:T(8,128)(2,1)S(1)}, u32[]{:S(2)}, u32[]{:S(2)}) collective-permute-start(bf16[16,2048]{1,0:T(8,128)(2,1)S(1)} %get-tuple-element.73), channel_id=1, source_target_pairs={{0,7},{1,6},{2,5},{3,4},{4,3},{5,2},{6,1},{7,0},{8,15},{9,14},{10,... | collective-permute-start | bytes 196616 | tf_op jit(solution)/shard_map/ppermute | solution.py:76
  34.6 9.9 %collective-permute-start.12 = (bf16[32,2048]{1,0:T(8,128)(2,1)S(1)}, bf16[32,2048]{1,0:T(8,128)(2,1)S(1)}, u32[]{:S(2)}, u32[]{:S(2)}) collective-permute-start(bf16[32,2048]{1,0:T(8,128)(2,1)S(1)} %get-tuple-element.67), channel_id=1, source_target_pairs={{0,2},{1,3},{2,0},{3,1},{4,6},{5,7},{6,4},{7,5},{8,10},{9,11},{10,... | collective-permute-start | bytes 393224 | tf_op jit(solution)/shard_map/ppermute | solution.py:76
  35.7 10.4 %collective-permute-start.13 = (bf16[32,2048]{1,0:T(8,128)(2,1)S(1)}, bf16[32,2048]{1,0:T(8,128)(2,1)S(1)}, u32[]{:S(2)}, u32[]{:S(2)}) collective-permute-start(bf16[32,2048]{1,0:T(8,128)(2,1)S(1)} %get-tuple-element.68), channel_id=1, source_target_pairs={{0,5},{1,4},{2,7},{3,6},{4,1},{5,0},{6,3},{7,2},{8,13},{9,12},{10,... | collective-permute-start | bytes 393224 | tf_op jit(solution)/shard_map/ppermute | solution.py:76
  36.2 9.9 %collective-permute-start.14 = (bf16[32,2048]{1,0:T(8,128)(2,1)S(1)}, bf16[32,2048]{1,0:T(8,128)(2,1)S(1)}, u32[]{:S(2)}, u32[]{:S(2)}) collective-permute-start(bf16[32,2048]{1,0:T(8,128)(2,1)S(1)} %get-tuple-element.69), channel_id=1, source_target_pairs={{0,7},{1,6},{2,5},{3,4},{4,3},{5,2},{6,1},{7,0},{8,15},{9,14},{10,... | collective-permute-start | bytes 393224 | tf_op jit(solution)/shard_map/ppermute | solution.py:76
  38.1 1.3 %collective-permute-start.18 = (bf16[8,2048]{1,0:T(8,128)(2,1)S(1)}, bf16[8,2048]{1,0:T(8,128)(2,1)S(1)}, u32[]{:S(2)}, u32[]{:S(2)}) collective-permute-start(bf16[8,2048]{1,0:T(8,128)(2,1)S(1)} %get-tuple-element.77), channel_id=1, source_target_pairs={{0,1},{1,0},{2,3},{3,2},{4,5},{5,4},{6,7},{7,6},{8,9},{9,8},{10,11... | collective-permute-start | bytes 98312 | tf_op jit(solution)/shard_map/ppermute | solution.py:76
  41.5 1.2 %collective-permute-start.19 = (bf16[8,2048]{1,0:T(8,128)(2,1)S(1)}, bf16[8,2048]{1,0:T(8,128)(2,1)S(1)}, u32[]{:S(2)}, u32[]{:S(2)}) collective-permute-start(bf16[8,2048]{1,0:T(8,128)(2,1)S(1)} %get-tuple-element.81), channel_id=1, source_target_pairs={{0,1},{1,0},{2,3},{3,2},{4,5},{5,4},{6,7},{7,6},{8,9},{9,8},{10,11... | collective-permute-start | bytes 98312 | tf_op jit(solution)/shard_map/ppermute | solution.py:76
  42.9 3.8 %collective-permute-start.20 = (bf16[4,2048]{1,0:T(4,128)(2,1)S(1)}, bf16[4,2048]{1,0:T(4,128)(2,1)S(1)}, u32[]{:S(2)}, u32[]{:S(2)}) collective-permute-start(bf16[4,2048]{1,0:T(4,128)(2,1)S(1)} %get-tuple-element.84), channel_id=1, source_target_pairs={{0,2},{1,3},{2,0},{3,1},{4,6},{5,7},{6,4},{7,5},{8,10},{9,11},{10,... | collective-permute-start | bytes 49160 | tf_op jit(solution)/shard_map/ppermute | solution.py:76
  43.9 3.3 %collective-permute-start.21 = (bf16[4,2048]{1,0:T(4,128)(2,1)S(1)}, bf16[4,2048]{1,0:T(4,128)(2,1)S(1)}, u32[]{:S(2)}, u32[]{:S(2)}) collective-permute-start(bf16[4,2048]{1,0:T(4,128)(2,1)S(1)} %get-tuple-element.85), channel_id=1, source_target_pairs={{0,5},{1,4},{2,7},{3,6},{4,1},{5,0},{6,3},{7,2},{8,13},{9,12},{10,... | collective-permute-start | bytes 49160 | tf_op jit(solution)/shard_map/ppermute | solution.py:76
  44.6 4.1 %collective-permute-start.22 = (bf16[4,2048]{1,0:T(4,128)(2,1)S(1)}, bf16[4,2048]{1,0:T(4,128)(2,1)S(1)}, u32[]{:S(2)}, u32[]{:S(2)}) collective-permute-start(bf16[4,2048]{1,0:T(4,128)(2,1)S(1)} %get-tuple-element.86), channel_id=1, source_target_pairs={{0,7},{1,6},{2,5},{3,4},{4,3},{5,2},{6,1},{7,0},{8,15},{9,14},{10,... | collective-permute-start | bytes 49160 | tf_op jit(solution)/shard_map/ppermute | solution.py:76

commit v7 on v6

--- a/solution.py
+++ b/solution.py
@@ -174,6 +174,8 @@
     sine = jnp.where(lane < head // 2, -sine, sine)
     for which, gain_ref in enumerate((q_gain_ref, k_gain_ref)):
         gain = jnp.broadcast_to(gain_ref[...], angle.shape)
+        if which == 0:
+            gain = gain * (head ** (-0.5) * LOG2E)
         rot_ref[2 * which] = cosine * gain
         rot_ref[2 * which + 1] = sine * pltpu.roll(gain, head // 2, 1)
     for copy in copies:
@@ -295,7 +297,7 @@
         turned = pltpu.roll(values, head // 2, 1)
         return (values * rot_ref[2 * which] + turned * rot_ref[2 * which + 1]).astype(BF16)
 
-    scale = head ** (-0.5) * LOG2E
+    ones = jnp.ones((span, head), BF16)
     for j in range(chips):
         kv = (chip ^ j) * per_chip // group
         key_at, value_at = kv, kv + kv_heads
@@ -306,12 +308,10 @@
         query = jnp.concatenate(
             [rope(got[j][:, h * head : (h + 1) * head], 0) for h in range(per_chip)], axis=0
         )
-        score = dot_last(query, keys) * scale
-        score = score.reshape(per_chip, new, span) + mask_ref[...][None]
+        score = dot_last(query, keys).reshape(per_chip, new, span) + mask_ref[...][None]
         expo = jnp.exp2(score - jnp.max(score, axis=-1, keepdims=True))
-        denom = jnp.sum(expo, axis=-1, keepdims=True).reshape(per_chip * new, 1)
         expo = expo.astype(BF16).reshape(per_chip * new, span)
-        result = (dot(expo, values) / denom).astype(BF16)
+        result = (dot(expo, values) / dot(expo, ones)).astype(BF16)
         for h in range(per_chip):
             outs[j][:, h * head : (h + 1) * head] = result[h * new : (h + 1) * new]
 

time: 49.9 us -> 50.2 us (level)
  no operation moved by 1% of the time
where the time goes in v7:
time: 50.2 us; the launch traced here: 49.8 us
  starting transfers between devices  21.4 us (43%)
  Pallas kernels  17.2 us (34%)
  waiting for transfers between devices  9.06 us (18%)
  between operations  2.09 us (4%)
    ppermute x23, starting transfers between devices, hop(): lax.ppermute(value, 'tensor', [(i, i ^ step) for i in range(devices)])  21.4 us
    pallas_call x12, Pallas kernels, call(): pl.pallas_call(kernel, out_shape=outs, in_specs=specs, out_specs=[pl.Bloc...  17.2 us
    ppermute x23, waiting for transfers between devices, hop(): lax.ppermute(value, 'tensor', [(i, i ^ step) for i in range(devices)])  9.06 us
  transfers between devices with their start and end apart: 23, of which 9 were waited for; matrix products, arithmetic and copies ran while one was open for 0% of the time, Pallas kernels for 24%

profile of v7, /device:TPU:0, one launch (start us, length us, event | category | flops | bytes accessed | tf_op | source)
XLA Modules:
  0.0 49.8 jit_solution(5172092691041221809)
XLA Ops:
  0.0 0.5 collective-permute-start.3
  0.5 3.5 %collective-permute-start.2 = (bf16[32,2048]{1,0:T(8,128)(2,1)}, bf16[32,2048]{1,0:T(8,128)(2,1)S(1)}, u32[]{:S(2)}, u32[]{:S(2)}) collective-permute-start(bf16[32,2048]{1,0:T(8,128)(2,1)} %refs_4_.4), channel_id=1, source_target_pairs={{0,7},{1,6},{2,5},{3,4},{4,3},{5,2},{6,1},{7,0},{8,15},{9,14},{10,... | collective-permute-start | bytes 393224 | tf_op jit(solution)/shard_map/ppermute | solution.py:76
  4.0 0.6 %collective-permute-start.1 = (bf16[32,2048]{1,0:T(8,128)(2,1)}, bf16[32,2048]{1,0:T(8,128)(2,1)S(1)}, u32[]{:S(2)}, u32[]{:S(2)}) collective-permute-start(bf16[32,2048]{1,0:T(8,128)(2,1)} %refs_4_.4), channel_id=1, source_target_pairs={{0,5},{1,4},{2,7},{3,6},{4,1},{5,0},{6,3},{7,2},{8,13},{9,12},{10,... | collective-permute-start | bytes 393224 | tf_op jit(solution)/shard_map/ppermute | solution.py:76
  6.6 3.2 %prep.1 = (bf16[4,640,128]{2,1,0:T(8,128)(2,1)S(1)}, bf16[4,640,128]{2,1,0:T(8,128)(2,1)S(1)}, f32[32,640]{1,0:T(8,128)S(1)}, f32[4,32,128]{2,1,0:T(8,128)S(1)},...) custom-call(bf16[1,1024,512]{2,1,0:T(8,128)(2,1)} %refs_0_.3, ...), custom_call_target="tpu_custom_call" | custom-call | bytes 2621440 | tf_op jit(solution)/shard_map/prep/pallas_call | solution.py:61
  9.8 1.2 %collective-permute-done.1.refs_2_ = bf16[32,2048]{1,0:T(8,128)(2,1)S(1)} collective-permute-done((bf16[32,2048]{1,0:T(8,128)(2,1)}, bf16[32,2048]{1,0:T(8,128)(2,1)S(1)}, u32[]{:S(2)}, u32[]{:S(2)}) %collective-permute-start.1) | collective-permute-done | bytes 131104 | tf_op jit(solution)/shard_map/ppermute | solution.py:76
  11.0 0.8 %collective-permute-done.refs_1_ = bf16[32,2048]{1,0:T(8,128)(2,1)S(1)} collective-permute-done((bf16[32,2048]{1,0:T(8,128)(2,1)}, bf16[32,2048]{1,0:T(8,128)(2,1)S(1)}, u32[]{:S(2)}, u32[]{:S(2)}) %collective-permute-start) | collective-permute-done | bytes 131104 | tf_op jit(solution)/shard_map/ppermute | solution.py:76
  11.8 1.1 %project.1 = (bf16[32,1280]{1,0:T(8,128)(2,1)S(1)}, bf16[32,1280]{1,0:T(8,128)(2,1)S(1)}, bf16[32,1280]{1,0:T(8,128)(2,1)S(1)}, bf16[32,1280]{1,0:T(8,128)(2,1)S(1)}) custom-call(bf16[32,2048]{1,0:T(8,128)(2,1)S(1)} %copy-done, bf16[32,2048]{1,0:T(8,128)(2,1)S(1)} %collective-permute-done.refs_1_, bf16[32,2048]{1,0:T(8,128)(2,1)S(1)} %collective-permute-done.1.refs_2_, ...), custom_call_target="tpu_custom_call" | custom-call | flops 671088640 | bytes 5242880 | tf_op jit(solution)/shard_map/project/pallas_call | solution.py:61
  12.9 1.6 %collective-permute-start.5 = (bf16[32,1280]{1,0:T(8,128)(2,1)S(1)}, bf16[32,1280]{1,0:T(8,128)(2,1)S(1)}, u32[]{:S(2)}, u32[]{:S(2)}) collective-permute-start(bf16[32,1280]{1,0:T(8,128)(2,1)S(1)} %get-tuple-element.50), channel_id=1, source_target_pairs={{0,2},{1,3},{2,0},{3,1},{4,6},{5,7},{6,4},{7,5},{8,10},{9,11},{10,... | collective-permute-start | bytes 245768 | tf_op jit(solution)/shard_map/ppermute | solution.py:76
  14.5 1.7 %collective-permute-start.7 = (bf16[32,1280]{1,0:T(8,128)(2,1)S(1)}, bf16[32,1280]{1,0:T(8,128)(2,1)S(1)}, u32[]{:S(2)}, u32[]{:S(2)}) collective-permute-start(bf16[32,1280]{1,0:T(8,128)(2,1)S(1)} %get-tuple-element.52), channel_id=1, source_target_pairs={{0,7},{1,6},{2,5},{3,4},{4,3},{5,2},{6,1},{7,0},{8,15},{9,14},{10,... | collective-permute-start | bytes 245768 | tf_op jit(solution)/shard_map/ppermute | solution.py:76
  16.2 2.6 %route.1 = (f32[64,128]{1,0:T(8,128)S(1)}, f32[32,16]{1,0:T(8,128)S(1)}, f32[16,128]{1,0:T(8,128)S(1)}, f32[1,2048]{1,0:T(1,128)S(1)}, bf16[512,2048]{1,0:T(8,128)(2,1)S(1)}, /*index=5*/bf16[1,768,2048]{2,1,0:T(8,128)(2,1)S(1)}) custom-call(bf16[32,1280]{1,0:T(8,128)(2,1)S(1)} %get-tuple-element.49.refs_0_, s32[8,256]{1,0:T(8,128)} %bitcast.7, ...), custom_call_target="tpu_custom_call" | custom-call | bytes 10485760 | tf_op jit(solution)/shard_map/route/pallas_call | solution.py:61
  18.8 2.1 %collective-permute-done.6.refs_2_ = bf16[32,1280]{1,0:T(8,128)(2,1)S(1)} collective-permute-done((bf16[32,1280]{1,0:T(8,128)(2,1)S(1)}, bf16[32,1280]{1,0:T(8,128)(2,1)S(1)}, u32[]{:S(2)}, u32[]{:S(2)}) %collective-permute-start.6) | collective-permute-done | bytes 81952 | tf_op jit(solution)/shard_map/ppermute | solution.py:76
  20.9 2.4 %attend.1 = (bf16[32,1024]{1,0:T(8,128)(2,1)S(1)}, bf16[32,1024]{1,0:T(8,128)(2,1)S(1)}, bf16[32,1024]{1,0:T(8,128)(2,1)S(1)}, bf16[32,1024]{1,0:T(8,128)(2,1)S(1)}, bf16[512,2048]{1,0:T(8,128)(2,1)S(1)}) custom-call(bf16[32,1280]{1,0:T(8,128)(2,1)S(1)} %get-tuple-element.49.refs_0_, ...), custom_call_target="tpu_custom_call", output_to_operand_aliasing={{4}: (8, {})} | custom-call | flops 335544320 | bytes 1310720 | tf_op jit(solution)/shard_map/attend/pallas_call | solution.py:61
  23.7 1.4 %collective-permute-start.9 = (bf16[32,1024]{1,0:T(8,128)(2,1)S(1)}, bf16[32,1024]{1,0:T(8,128)(2,1)S(1)}, u32[]{:S(2)}, u32[]{:S(2)}) collective-permute-start(bf16[32,1024]{1,0:T(8,128)(2,1)S(1)} %get-tuple-element.60), channel_id=1, source_target_pairs={{0,5},{1,4},{2,7},{3,6},{4,1},{5,0},{6,3},{7,2},{8,13},{9,12},{10,... | collective-permute-start | bytes 196616 | tf_op jit(solution)/shard_map/ppermute | solution.py:76
  25.1 1.5 %collective-permute-start.10 = (bf16[32,1024]{1,0:T(8,128)(2,1)S(1)}, bf16[32,1024]{1,0:T(8,128)(2,1)S(1)}, u32[]{:S(2)}, u32[]{:S(2)}) collective-permute-start(bf16[32,1024]{1,0:T(8,128)(2,1)S(1)} %get-tuple-element.61), channel_id=1, source_target_pairs={{0,7},{1,6},{2,5},{3,4},{4,3},{5,2},{6,1},{7,0},{8,15},{9,14},{10,... | collective-permute-start | bytes 196616 | tf_op jit(solution)/shard_map/ppermute | solution.py:76
  26.6 2.9 %select.1 = (f32[16,2048]{1,0:T(8,128)S(1)}, bf16[1,768,2048]{2,1,0:T(8,128)(2,1)S(1)}, bf16[1,768,2048]{2,1,0:T(8,128)(2,1)S(1)}) custom-call(bf16[32,2048]{1,0:T(8,128)(2,1)S(1)} %copy-done, bf16[32,2048]{1,0:T(8,128)(2,1)S(1)} %collective-permute-done.refs_1_, bf16[32,2048]{1,0:T(8,128)(2,1)S(1)} %collective-permute-done.1.refs_2_, ...), custom_call_target="tpu_custom_call" | custom-call | flops 8388608 | bytes 12582912 | tf_op jit(solution)/shard_map/select/pallas_call | solution.py:61
  29.9 1.0 %experts.1 = (bf16[16,2048]{1,0:T(8,128)(2,1)S(1)}, bf16[16,2048]{1,0:T(8,128)(2,1)S(1)}, bf16[16,2048]{1,0:T(8,128)(2,1)S(1)}, bf16[16,2048]{1,0:T(8,128)(2,1)S(1)}) custom-call(bf16[32,1024]{1,0:T(8,128)(2,1)S(1)} %get-tuple-element.58.refs_5_.refs_0_, bf16[32,1024]{1,0:T(8,128)(2,1)S(1)} %collective-permute-done.8.refs_1_, ...), custom_call_target="tpu_custom_call" | custom-call | flops 268435456 | bytes 4194304 | tf_op jit(solution)/shard_map/experts/pallas_call | solution.py:61
  30.9 1.1 %collective-permute-start.15 = (bf16[16,2048]{1,0:T(8,128)(2,1)S(1)}, bf16[16,2048]{1,0:T(8,128)(2,1)S(1)}, u32[]{:S(2)}, u32[]{:S(2)}) collective-permute-start(bf16[16,2048]{1,0:T(8,128)(2,1)S(1)} %get-tuple-element.71), channel_id=1, source_target_pairs={{0,2},{1,3},{2,0},{3,1},{4,6},{5,7},{6,4},{7,5},{8,10},{9,11},{10,... | collective-permute-start | bytes 196616 | tf_op jit(solution)/shard_map/ppermute | solution.py:76
  32.0 0.8 %collective-permute-start.16 = (bf16[16,2048]{1,0:T(8,128)(2,1)S(1)}, bf16[16,2048]{1,0:T(8,128)(2,1)S(1)}, u32[]{:S(2)}, u32[]{:S(2)}) collective-permute-start(bf16[16,2048]{1,0:T(8,128)(2,1)S(1)} %get-tuple-element.72), channel_id=1, source_target_pairs={{0,5},{1,4},{2,7},{3,6},{4,1},{5,0},{6,3},{7,2},{8,13},{9,12},{10,... | collective-permute-start | bytes 196616 | tf_op jit(solution)/shard_map/ppermute | solution.py:76
  32.8 1.4 %collective-permute-start.17 = (bf16[16,2048]{1,0:T(8,128)(2,1)S(1)}, bf16[16,2048]{1,0:T(8,128)(2,1)S(1)}, u32[]{:S(2)}, u32[]{:S(2)}) collective-permute-start(bf16[16,2048]{1,0:T(8,128)(2,1)S(1)} %get-tuple-element.73), channel_id=1, source_target_pairs={{0,7},{1,6},{2,5},{3,4},{4,3},{5,2},{6,1},{7,0},{8,15},{9,14},{10,... | collective-permute-start | bytes 196616 | tf_op jit(solution)/shard_map/ppermute | solution.py:76
  34.2 0.7 %slots.1 = (bf16[32,2048]{1,0:T(8,128)(2,1)S(1)}, bf16[32,2048]{1,0:T(8,128)(2,1)S(1)}, bf16[32,2048]{1,0:T(8,128)(2,1)S(1)}, bf16[32,2048]{1,0:T(8,128)(2,1)S(1)}) custom-call(bf16[32,1024]{1,0:T(8,128)(2,1)S(1)} %get-tuple-element.58.refs_5_.refs_0_, bf16[32,1024]{1,0:T(8,128)(2,1)S(1)} %collective-permute-done.8.refs_1_, ...), custom_call_target="tpu_custom_call" | custom-call | flops 536870912 | bytes 4194304 | tf_op jit(solution)/shard_map/slots/pallas_call | solution.py:61
  34.9 1.1 %collective-permute-start.12 = (bf16[32,2048]{1,0:T(8,128)(2,1)S(1)}, bf16[32,2048]{1,0:T(8,128)(2,1)S(1)}, u32[]{:S(2)}, u32[]{:S(2)}) collective-permute-start(bf16[32,2048]{1,0:T(8,128)(2,1)S(1)} %get-tuple-element.67), channel_id=1, source_target_pairs={{0,2},{1,3},{2,0},{3,1},{4,6},{5,7},{6,4},{7,5},{8,10},{9,11},{10,... | collective-permute-start | bytes 393224 | tf_op jit(solution)/shard_map/ppermute | solution.py:76
  36.0 0.5 %collective-permute-start.13 = (bf16[32,2048]{1,0:T(8,128)(2,1)S(1)}, bf16[32,2048]{1,0:T(8,128)(2,1)S(1)}, u32[]{:S(2)}, u32[]{:S(2)}) collective-permute-start(bf16[32,2048]{1,0:T(8,128)(2,1)S(1)} %get-tuple-element.68), channel_id=1, source_target_pairs={{0,5},{1,4},{2,7},{3,6},{4,1},{5,0},{6,3},{7,2},{8,13},{9,12},{10,... | collective-permute-start | bytes 393224 | tf_op jit(solution)/shard_map/ppermute | solution.py:76
  36.5 1.7 %collective-permute-start.14 = (bf16[32,2048]{1,0:T(8,128)(2,1)S(1)}, bf16[32,2048]{1,0:T(8,128)(2,1)S(1)}, u32[]{:S(2)}, u32[]{:S(2)}) collective-permute-start(bf16[32,2048]{1,0:T(8,128)(2,1)S(1)} %get-tuple-element.69), channel_id=1, source_target_pairs={{0,7},{1,6},{2,5},{3,4},{4,3},{5,2},{6,1},{7,0},{8,15},{9,14},{10,... | collective-permute-start | bytes 393224 | tf_op jit(solution)/shard_map/ppermute | solution.py:76
  38.4 1.2 %collective-permute-done.18.other_ref = bf16[8,2048]{1,0:T(8,128)(2,1)S(1)} collective-permute-done((bf16[8,2048]{1,0:T(8,128)(2,1)S(1)}, bf16[8,2048]{1,0:T(8,128)(2,1)S(1)}, u32[]{:S(2)}, u32[]{:S(2)}) %collective-permute-start.18) | collective-permute-done | bytes 32800 | tf_op jit(solution)/shard_map/ppermute | solution.py:76
  39.6 2.2 %expert.1 = (f32[8,2048]{1,0:T(8,128)S(1)}, bf16[8,2048]{1,0:T(8,128)(2,1)S(1)}) custom-call(bf16[8,2048]{1,0:T(8,128)(2,1)S(1)} %get-tuple-element.76.own_ref, bf16[8,2048]{1,0:T(8,128)(2,1)S(1)} %collective-permute-done.18.other_ref, bf16[1,768,2048]{2,1,0:T(8,128)(2,1)S(1)} %get-tuple-element.64.refs_7_.gate_ref, ...), custom_call_target="tpu_custom_call" | custom-call | flops 150994944 | bytes 9437184 | tf_op jit(solution)/shard_map/expert/pallas_call | solution.py:61
  42.0 1.0 %collective-permute-done.19.other_ref = bf16[8,2048]{1,0:T(8,128)(2,1)S(1)} collective-permute-done((bf16[8,2048]{1,0:T(8,128)(2,1)S(1)}, bf16[8,2048]{1,0:T(8,128)(2,1)S(1)}, u32[]{:S(2)}, u32[]{:S(2)}) %collective-permute-start.19) | collective-permute-done | bytes 32800 | tf_op jit(solution)/shard_map/ppermute | solution.py:76
  43.1 1.1 %collective-permute-start.20 = (bf16[4,2048]{1,0:T(4,128)(2,1)S(1)}, bf16[4,2048]{1,0:T(4,128)(2,1)S(1)}, u32[]{:S(2)}, u32[]{:S(2)}) collective-permute-start(bf16[4,2048]{1,0:T(4,128)(2,1)S(1)} %get-tuple-element.84), channel_id=1, source_target_pairs={{0,2},{1,3},{2,0},{3,1},{4,6},{5,7},{6,4},{7,5},{8,10},{9,11},{10,... | collective-permute-start | bytes 49160 | tf_op jit(solution)/shard_map/ppermute | solution.py:76
  44.2 0.7 %collective-permute-start.21 = (bf16[4,2048]{1,0:T(4,128)(2,1)S(1)}, bf16[4,2048]{1,0:T(4,128)(2,1)S(1)}, u32[]{:S(2)}, u32[]{:S(2)}) collective-permute-start(bf16[4,2048]{1,0:T(4,128)(2,1)S(1)} %get-tuple-element.85), channel_id=1, source_target_pairs={{0,5},{1,4},{2,7},{3,6},{4,1},{5,0},{6,3},{7,2},{8,13},{9,12},{10,... | collective-permute-start | bytes 49160 | tf_op jit(solution)/shard_map/ppermute | solution.py:76
  44.9 1.5 %collective-permute-start.22 = (bf16[4,2048]{1,0:T(4,128)(2,1)S(1)}, bf16[4,2048]{1,0:T(4,128)(2,1)S(1)}, u32[]{:S(2)}, u32[]{:S(2)}) collective-permute-start(bf16[4,2048]{1,0:T(4,128)(2,1)S(1)} %get-tuple-element.86), channel_id=1, source_target_pairs={{0,7},{1,6},{2,5},{3,4},{4,3},{5,2},{6,1},{7,0},{8,15},{9,14},{10,... | collective-permute-start | bytes 49160 | tf_op jit(solution)/shard_map/ppermute | solution.py:76
  46.9 0.5 %collective-permute-done.21.refs_4_ = bf16[4,2048]{1,0:T(4,128)(2,1)S(1)} collective-permute-done((bf16[4,2048]{1,0:T(4,128)(2,1)S(1)}, bf16[4,2048]{1,0:T(4,128)(2,1)S(1)}, u32[]{:S(2)}, u32[]{:S(2)}) %collective-permute-start.21) | collective-permute-done | bytes 16416 | tf_op jit(solution)/shard_map/ppermute | solution.py:76
  47.5 1.5 %collective-permute-done.22.refs_5_ = bf16[4,2048]{1,0:T(4,128)(2,1)S(1)} collective-permute-done((bf16[4,2048]{1,0:T(4,128)(2,1)S(1)}, bf16[4,2048]{1,0:T(4,128)(2,1)S(1)}, u32[]{:S(2)}, u32[]{:S(2)}) %collective-permute-start.22) | collective-permute-done | bytes 16416 | tf_op jit(solution)/shard_map/ppermute | solution.py:76
  48.9 0.8 %combine.1 = bf16[32,2048]{1,0:T(8,128)(2,1)} custom-call(f32[32,2048]{1,0:T(8,128)S(1)} %hidden.1.refs_0_, f32[32,16]{1,0:T(8,128)S(1)} %get-tuple-element.70.refs_1_, bf16[4,2048]{1,0:T(4,128)(2,1)S(1)} %get-tuple-element.83.refs_2_, bf16[4,2048]{1,0:T(4,128)(2,1)S(1)} %collective-permute-done.20.refs_3_, ...), custom_call_target="tpu_custom_call" | custom-call | bytes 393216 | tf_op jit(solution)/shard_map/combine/pallas_call | solution.py:61
  (28 shorter events, 1.9 us)
Async XLA Ops:
  0.0 11.8 %collective-permute-start.3 = (bf16[2048,512]{1,0:T(8,128)(2,1)}, bf16[2048,512]{1,0:T(8,128)(2,1)S(1)}, u32[]{:S(2)}, u32[]{:S(2)}) collective-permute-start(bf16[2048,512]{1,0:T(8,128)(2,1)} %refs_11_.1), channel_id=1, source_target_pairs={{0,1},{1,0},{2,3},{3,2},{4,5},{5,4},{6,7},{7,6},{8,9},{9,8},{10,11... | collective-permute-start | bytes 6291464 | tf_op jit(solution)/shard_map/ppermute | solution.py:76
  0.5 11.3 %collective-permute-start.4 = (bf16[128,2048]{1,0:T(8,128)(2,1)}, bf16[128,2048]{1,0:T(8,128)(2,1)S(1)}, u32[]{:S(2)}, u32[]{:S(2)}) collective-permute-start(bf16[128,2048]{1,0:T(8,128)(2,1)} %refs_12_.1), channel_id=1, source_target_pairs={{0,1},{1,0},{2,3},{3,2},{4,5},{5,4},{6,7},{7,6},{8,9},{9,8},{10,11... | collective-permute-start | bytes 1572872 | tf_op jit(solution)/shard_map/ppermute | solution.py:76
  0.5 9.3 %collective-permute-start.2 = (bf16[32,2048]{1,0:T(8,128)(2,1)}, bf16[32,2048]{1,0:T(8,128)(2,1)S(1)}, u32[]{:S(2)}, u32[]{:S(2)}) collective-permute-start(bf16[32,2048]{1,0:T(8,128)(2,1)} %refs_4_.4), channel_id=1, source_target_pairs={{0,7},{1,6},{2,5},{3,4},{4,3},{5,2},{6,1},{7,0},{8,15},{9,14},{10,... | collective-permute-start | bytes 393224 | tf_op jit(solution)/shard_map/ppermute | solution.py:76
  4.0 7.0 %collective-permute-start.1 = (bf16[32,2048]{1,0:T(8,128)(2,1)}, bf16[32,2048]{1,0:T(8,128)(2,1)S(1)}, u32[]{:S(2)}, u32[]{:S(2)}) collective-permute-start(bf16[32,2048]{1,0:T(8,128)(2,1)} %refs_4_.4), channel_id=1, source_target_pairs={{0,5},{1,4},{2,7},{3,6},{4,1},{5,0},{6,3},{7,2},{8,13},{9,12},{10,... | collective-permute-start | bytes 393224 | tf_op jit(solution)/shard_map/ppermute | solution.py:76
  4.6 7.1 %collective-permute-start = (bf16[32,2048]{1,0:T(8,128)(2,1)}, bf16[32,2048]{1,0:T(8,128)(2,1)S(1)}, u32[]{:S(2)}, u32[]{:S(2)}) collective-permute-start(bf16[32,2048]{1,0:T(8,128)(2,1)} %refs_4_.4), channel_id=1, source_target_pairs={{0,2},{1,3},{2,0},{3,1},{4,6},{5,7},{6,4},{7,5},{8,10},{9,11},{10,... | collective-permute-start | bytes 393224 | tf_op jit(solution)/shard_map/ppermute | solution.py:76
  6.6 5.2 %copy-start = (bf16[32,2048]{1,0:T(8,128)(2,1)S(1)}, bf16[32,2048]{1,0:T(8,128)(2,1)}, u32[]{:S(2)}) copy-start(bf16[32,2048]{1,0:T(8,128)(2,1)} %refs_4_.4) | copy-start | bytes 393220
  12.9 5.9 %collective-permute-start.5 = (bf16[32,1280]{1,0:T(8,128)(2,1)S(1)}, bf16[32,1280]{1,0:T(8,128)(2,1)S(1)}, u32[]{:S(2)}, u32[]{:S(2)}) collective-permute-start(bf16[32,1280]{1,0:T(8,128)(2,1)S(1)} %get-tuple-element.50), channel_id=1, source_target_pairs={{0,2},{1,3},{2,0},{3,1},{4,6},{5,7},{6,4},{7,5},{8,10},{9,11},{10,... | collective-permute-start | bytes 245768 | tf_op jit(solution)/shard_map/ppermute | solution.py:76
  14.5 6.4 %collective-permute-start.6 = (bf16[32,1280]{1,0:T(8,128)(2,1)S(1)}, bf16[32,1280]{1,0:T(8,128)(2,1)S(1)}, u32[]{:S(2)}, u32[]{:S(2)}) collective-permute-start(bf16[32,1280]{1,0:T(8,128)(2,1)S(1)} %get-tuple-element.51), channel_id=1, source_target_pairs={{0,5},{1,4},{2,7},{3,6},{4,1},{5,0},{6,3},{7,2},{8,13},{9,12},{10,... | collective-permute-start | bytes 245768 | tf_op jit(solution)/shard_map/ppermute | solution.py:76
  14.5 6.4 %collective-permute-start.7 = (bf16[32,1280]{1,0:T(8,128)(2,1)S(1)}, bf16[32,1280]{1,0:T(8,128)(2,1)S(1)}, u32[]{:S(2)}, u32[]{:S(2)}) collective-permute-start(bf16[32,1280]{1,0:T(8,128)(2,1)S(1)} %get-tuple-element.52), channel_id=1, source_target_pairs={{0,7},{1,6},{2,5},{3,4},{4,3},{5,2},{6,1},{7,0},{8,15},{9,14},{10,... | collective-permute-start | bytes 245768 | tf_op jit(solution)/shard_map/ppermute | solution.py:76
  23.3 6.6 %collective-permute-start.11 = (bf16[512,2048]{1,0:T(8,128)(2,1)S(1)}, bf16[512,2048]{1,0:T(8,128)(2,1)S(1)}, u32[]{:S(2)}, u32[]{:S(2)}) collective-permute-start(bf16[512,2048]{1,0:T(8,128)(2,1)S(1)} %get-tuple-element.62.refs_4_), channel_id=1, source_target_pairs={{0,1},{1,0},{2,3},{3,2},{4,5},{5,4},{6,7},{7,6},{8,9},{9,8},{10,11... | collective-permute-start | bytes 6291464 | tf_op jit(solution)/shard_map/ppermute | solution.py:76
  23.4 6.1 %collective-permute-start.8 = (bf16[32,1024]{1,0:T(8,128)(2,1)S(1)}, bf16[32,1024]{1,0:T(8,128)(2,1)S(1)}, u32[]{:S(2)}, u32[]{:S(2)}) collective-permute-start(bf16[32,1024]{1,0:T(8,128)(2,1)S(1)} %get-tuple-element.59), channel_id=1, source_target_pairs={{0,2},{1,3},{2,0},{3,1},{4,6},{5,7},{6,4},{7,5},{8,10},{9,11},{10,... | collective-permute-start | bytes 196616 | tf_op jit(solution)/shard_map/ppermute | solution.py:76
  23.7 5.8 %collective-permute-start.9 = (bf16[32,1024]{1,0:T(8,128)(2,1)S(1)}, bf16[32,1024]{1,0:T(8,128)(2,1)S(1)}, u32[]{:S(2)}, u32[]{:S(2)}) collective-permute-start(bf16[32,1024]{1,0:T(8,128)(2,1)S(1)} %get-tuple-element.60), channel_id=1, source_target_pairs={{0,5},{1,4},{2,7},{3,6},{4,1},{5,0},{6,3},{7,2},{8,13},{9,12},{10,... | collective-permute-start | bytes 196616 | tf_op jit(solution)/shard_map/ppermute | solution.py:76
  25.1 4.7 %collective-permute-start.10 = (bf16[32,1024]{1,0:T(8,128)(2,1)S(1)}, bf16[32,1024]{1,0:T(8,128)(2,1)S(1)}, u32[]{:S(2)}, u32[]{:S(2)}) collective-permute-start(bf16[32,1024]{1,0:T(8,128)(2,1)S(1)} %get-tuple-element.61), channel_id=1, source_target_pairs={{0,7},{1,6},{2,5},{3,4},{4,3},{5,2},{6,1},{7,0},{8,15},{9,14},{10,... | collective-permute-start | bytes 196616 | tf_op jit(solution)/shard_map/ppermute | solution.py:76
  30.9 5.6 %collective-permute-start.15 = (bf16[16,2048]{1,0:T(8,128)(2,1)S(1)}, bf16[16,2048]{1,0:T(8,128)(2,1)S(1)}, u32[]{:S(2)}, u32[]{:S(2)}) collective-permute-start(bf16[16,2048]{1,0:T(8,128)(2,1)S(1)} %get-tuple-element.71), channel_id=1, source_target_pairs={{0,2},{1,3},{2,0},{3,1},{4,6},{5,7},{6,4},{7,5},{8,10},{9,11},{10,... | collective-permute-start | bytes 196616 | tf_op jit(solution)/shard_map/ppermute | solution.py:76
  32.0 6.2 %collective-permute-start.16 = (bf16[16,2048]{1,0:T(8,128)(2,1)S(1)}, bf16[16,2048]{1,0:T(8,128)(2,1)S(1)}, u32[]{:S(2)}, u32[]{:S(2)}) collective-permute-start(bf16[16,2048]{1,0:T(8,128)(2,1)S(1)} %get-tuple-element.72), channel_id=1, source_target_pairs={{0,5},{1,4},{2,7},{3,6},{4,1},{5,0},{6,3},{7,2},{8,13},{9,12},{10,... | collective-permute-start | bytes 196616 | tf_op jit(solution)/shard_map/ppermute | solution.py:76
  32.8 5.5 %collective-permute-start.17 = (bf16[16,2048]{1,0:T(8,128)(2,1)S(1)}, bf16[16,2048]{1,0:T(8,128)(2,1)S(1)}, u32[]{:S(2)}, u32[]{:S(2)}) collective-permute-start(bf16[16,2048]{1,0:T(8,128)(2,1)S(1)} %get-tuple-element.73), channel_id=1, source_target_pairs={{0,7},{1,6},{2,5},{3,4},{4,3},{5,2},{6,1},{7,0},{8,15},{9,14},{10,... | collective-permute-start | bytes 196616 | tf_op jit(solution)/shard_map/ppermute | solution.py:76
  34.9 9.9 %collective-permute-start.12 = (bf16[32,2048]{1,0:T(8,128)(2,1)S(1)}, bf16[32,2048]{1,0:T(8,128)(2,1)S(1)}, u32[]{:S(2)}, u32[]{:S(2)}) collective-permute-start(bf16[32,2048]{1,0:T(8,128)(2,1)S(1)} %get-tuple-element.67), channel_id=1, source_target_pairs={{0,2},{1,3},{2,0},{3,1},{4,6},{5,7},{6,4},{7,5},{8,10},{9,11},{10,... | collective-permute-start | bytes 393224 | tf_op jit(solution)/shard_map/ppermute | solution.py:76
  36.0 10.4 %collective-permute-start.13 = (bf16[32,2048]{1,0:T(8,128)(2,1)S(1)}, bf16[32,2048]{1,0:T(8,128)(2,1)S(1)}, u32[]{:S(2)}, u32[]{:S(2)}) collective-permute-start(bf16[32,2048]{1,0:T(8,128)(2,1)S(1)} %get-tuple-element.68), channel_id=1, source_target_pairs={{0,5},{1,4},{2,7},{3,6},{4,1},{5,0},{6,3},{7,2},{8,13},{9,12},{10,... | collective-permute-start | bytes 393224 | tf_op jit(solution)/shard_map/ppermute | solution.py:76
  36.5 9.9 %collective-permute-start.14 = (bf16[32,2048]{1,0:T(8,128)(2,1)S(1)}, bf16[32,2048]{1,0:T(8,128)(2,1)S(1)}, u32[]{:S(2)}, u32[]{:S(2)}) collective-permute-start(bf16[32,2048]{1,0:T(8,128)(2,1)S(1)} %get-tuple-element.69), channel_id=1, source_target_pairs={{0,7},{1,6},{2,5},{3,4},{4,3},{5,2},{6,1},{7,0},{8,15},{9,14},{10,... | collective-permute-start | bytes 393224 | tf_op jit(solution)/shard_map/ppermute | solution.py:76
  38.4 1.3 %collective-permute-start.18 = (bf16[8,2048]{1,0:T(8,128)(2,1)S(1)}, bf16[8,2048]{1,0:T(8,128)(2,1)S(1)}, u32[]{:S(2)}, u32[]{:S(2)}) collective-permute-start(bf16[8,2048]{1,0:T(8,128)(2,1)S(1)} %get-tuple-element.77), channel_id=1, source_target_pairs={{0,1},{1,0},{2,3},{3,2},{4,5},{5,4},{6,7},{7,6},{8,9},{9,8},{10,11... | collective-permute-start | bytes 98312 | tf_op jit(solution)/shard_map/ppermute | solution.py:76
  41.8 1.2 %collective-permute-start.19 = (bf16[8,2048]{1,0:T(8,128)(2,1)S(1)}, bf16[8,2048]{1,0:T(8,128)(2,1)S(1)}, u32[]{:S(2)}, u32[]{:S(2)}) collective-permute-start(bf16[8,2048]{1,0:T(8,128)(2,1)S(1)} %get-tuple-element.81), channel_id=1, source_target_pairs={{0,1},{1,0},{2,3},{3,2},{4,5},{5,4},{6,7},{7,6},{8,9},{9,8},{10,11... | collective-permute-start | bytes 98312 | tf_op jit(solution)/shard_map/ppermute | solution.py:76
  43.1 3.8 %collective-permute-start.20 = (bf16[4,2048]{1,0:T(4,128)(2,1)S(1)}, bf16[4,2048]{1,0:T(4,128)(2,1)S(1)}, u32[]{:S(2)}, u32[]{:S(2)}) collective-permute-start(bf16[4,2048]{1,0:T(4,128)(2,1)S(1)} %get-tuple-element.84), channel_id=1, source_target_pairs={{0,2},{1,3},{2,0},{3,1},{4,6},{5,7},{6,4},{7,5},{8,10},{9,11},{10,... | collective-permute-start | bytes 49160 | tf_op jit(solution)/shard_map/ppermute | solution.py:76
  44.2 3.3 %collective-permute-start.21 = (bf16[4,2048]{1,0:T(4,128)(2,1)S(1)}, bf16[4,2048]{1,0:T(4,128)(2,1)S(1)}, u32[]{:S(2)}, u32[]{:S(2)}) collective-permute-start(bf16[4,2048]{1,0:T(4,128)(2,1)S(1)} %get-tuple-element.85), channel_id=1, source_target_pairs={{0,5},{1,4},{2,7},{3,6},{4,1},{5,0},{6,3},{7,2},{8,13},{9,12},{10,... | collective-permute-start | bytes 49160 | tf_op jit(solution)/shard_map/ppermute | solution.py:76
  44.9 4.1 %collective-permute-start.22 = (bf16[4,2048]{1,0:T(4,128)(2,1)S(1)}, bf16[4,2048]{1,0:T(4,128)(2,1)S(1)}, u32[]{:S(2)}, u32[]{:S(2)}) collective-permute-start(bf16[4,2048]{1,0:T(4,128)(2,1)S(1)} %get-tuple-element.86), channel_id=1, source_target_pairs={{0,7},{1,6},{2,5},{3,4},{4,3},{5,2},{6,1},{7,0},{8,15},{9,14},{10,... | collective-permute-start | bytes 49160 | tf_op jit(solution)/shard_map/ppermute | solution.py:76
